TPU v7x, 128 devices: a whole 4x4x4 slice. The times are simulated.
128 devices in a mesh: dp: 16 (over x, z), pipe: 4 (over y_lo, core), tensor: 2 (over y_hi).
Axes of the slice: x: 4, y: 4 (y_hi: 2, y_lo: 2; y = y_hi * 2 + y_lo), z: 4, core: 2. Of those that a mesh axis runs over, the one named last changes fastest.
Arguments:
- stream: bfloat16 [4, 4096, 8192], P('pipe', 'dp', 'tensor'), as said below
- backup_stream: bfloat16 [4, 4096, 8192], P('pipe', 'dp', 'tensor'), as said below
- norm_gain: float32 [8192], P('tensor'), may hold values from 0.5 to 2
- w_key: bfloat16 [4, 8192, 1024], P('pipe', None, 'tensor'), may hold values from -0.0625 to 0.0625
- w_value: bfloat16 [4, 8192, 1024], P('pipe', None, 'tensor'), may hold values from -0.0625 to 0.0625
- key_cot: bfloat16 [4, 4096, 1024], P('pipe', 'dp', 'tensor'), as said below
- value_cot: bfloat16 [4, 4096, 1024], P('pipe', 'dp', 'tensor'), as said below
- backup_key_cot: bfloat16 [4, 4096, 1024], P('pipe', 'dp', 'tensor'), as said below
- backup_value_cot: bfloat16 [4, 4096, 1024], P('pipe', 'dp', 'tensor'), as said below
- positions: int32 [4, 4096], P('pipe'), may hold values from 0 to 4095, as said below
- failed: int32 [4], replicated, may hold values from 0 to 15, as said below
- reroute_plan: int32 [4, 32], replicated, may hold values from 0 to 15, as said below
Outputs:
- grad_key: float32 [4, 8192, 1024], P('pipe', 'dp', 'tensor')
- grad_value: float32 [4, 8192, 1024], P('pipe', 'dp', 'tensor')
- stream_grad: bfloat16 [4, 4096, 8192], P('pipe', 'dp', 'tensor')
- spill_grad: bfloat16 [4, 768, 8192], P('pipe', 'dp', 'tensor')
Inputs may be any that keep to these rules, and one draw needn't show every extreme that they name: failed[s] is the replica of section s that has failed; some section has lost replica 0 and some other section replica 16 - 1. reroute_plan[s, b] never equals failed[s]; every other replica takes at least one block of each section, none more than 6, and some replica takes exactly 6. positions count from 0 at each document start; documents of a section's rows start at least every 4096 rows, and in some section exactly every 4096 rows. In stream[j] the rows of replica failed[(j + 1) mod 4] are zero. In backup_stream[s] only the rows of replica (failed[s] + 1) mod 16 are nonzero. In key_cot[s] the rows of replica failed[s] are zero. In value_cot[s] the rows of replica failed[s] are zero. In backup_key_cot[s] only the rows of replica (failed[s] + 1) mod 16 are nonzero. In backup_value_cot[s] only the rows of replica (failed[s] + 1) mod 16 are nonzero.
All inputs are finite; a program needn't handle non-finite values.
Results may differ from a plain program's by a relative error of at most 0.015.
Values may be sent and summed in bfloat16 or wider, within the bound.
No kernel may reach another device: no remote copies, remote signals or barrier semaphores. Data moves between devices by JAX's collectives and lax.ppermute only.
A program may use at most 128 MiB of HBM per device.

v0:
```python
import math

import jax
import jax.numpy as jnp
from jax import lax
from jax.sharding import PartitionSpec as P

D = 8192
HEAD = 128
BLOCK = 8


EPSILON = 1e-05
ROPE_BASE = 500000.0


def passed_along(block, axis, distance):
    devices = range(lax.axis_size(axis))
    route = [((i - distance) % len(devices), i) for i in devices]
    return lax.ppermute(block, axis, route)


def broadcast(shard, axis, root):
    mine = lax.axis_index(axis) == root
    return lax.psum(jnp.where(mine, shard, jnp.zeros_like(shard)), axis)


def frequencies():
    index_half = jnp.arange(HEAD // 2, dtype=jnp.float32)
    return jnp.exp(-(2.0 * index_half / HEAD) * math.log(ROPE_BASE))


def derotate(cotangent, position):
    row_count = cotangent.shape[0]
    pieces = cotangent.astype(jnp.float32).reshape(row_count, -1, 2, HEAD // 2)
    angles = position.astype(jnp.float32)[:, None] * frequencies()[None, :]
    cosine = jnp.cos(angles)[:, None, :]
    sine_values = jnp.sin(angles)[:, None, :]
    lower_half = pieces[:, :, 0, :]
    upper_half = pieces[:, :, 1, :]
    new_lower = lower_half * cosine + upper_half * sine_values
    new_upper = upper_half * cosine - lower_half * sine_values
    return jnp.stack([new_lower, new_upper], axis=2).reshape(row_count, -1).astype(jnp.bfloat16)


def slot_rows(plan_row, owners, capacity_blocks, block_size):
    block_count = plan_row.shape[0]
    block_ids = jnp.arange(block_count, dtype=jnp.int32)
    same_owner = plan_row[:, None] == plan_row[None, :]
    earlier = block_ids[None, :] < block_ids[:, None]
    block_rank = jnp.sum(jnp.where(same_owner & earlier, 1, 0), axis=1).astype(jnp.int32)
    slot_ids = jnp.arange(capacity_blocks, dtype=jnp.int32)
    matches = (plan_row[None, None, :] == owners[:, None, None]) & (
        block_rank[None, None, :] == slot_ids[None, :, None]
    )
    chosen = jnp.sum(jnp.where(matches, block_ids[None, None, :], 0), axis=2)
    filled = jnp.any(matches, axis=2)
    offsets = jnp.arange(block_size, dtype=jnp.int32)
    indices = (chosen[:, :, None] * block_size + offsets[None, None, :]).reshape(
        owners.shape[0], -1
    )
    occupied = jnp.repeat(filled, block_size, axis=1)
    return (indices, occupied)


def on_device(
    stream,
    backup_stream,
    norm_gain,
    w_key,
    w_value,
    key_cot,
    value_cot,
    backup_key_cot,
    backup_value_cot,
    positions,
    failed,
    reroute_plan,
):
    section_idx = lax.axis_index("pipe")
    member = lax.axis_index("dp")
    replicas = lax.axis_size("dp")
    fallen = failed[section_idx]
    keeper = (fallen + 1) % replicas
    plan_row = reroute_plan[section_idx]
    blocks = plan_row.shape[0]
    own_rows = stream.shape[1]
    capacity_blocks = 2 * ((blocks + replicas - 2) // (replicas - 1))
    incoming = passed_along(stream[0], "pipe", 1)
    own_positions = lax.dynamic_slice_in_dim(positions[0], member * own_rows, own_rows, 0)
    dead_positions = lax.dynamic_slice_in_dim(positions[0], fallen * own_rows, own_rows, 0)
    cot_key = derotate(key_cot[0], own_positions)
    cot_both = jnp.concatenate([cot_key, value_cot[0]], axis=1)
    saved_key = derotate(backup_key_cot[0], dead_positions)
    saved_both = jnp.concatenate([saved_key, backup_value_cot[0]], axis=1)
    dead_rows, dead_cots = (
        broadcast(backup_stream[0], "dp", keeper),
        broadcast(saved_both, "dp", keeper),
    )
    indices, occupied = slot_rows(plan_row, jnp.reshape(member, (1,)), capacity_blocks, BLOCK)
    index_list = indices[0]
    keep_slot = occupied[0][:, None]
    survives = member != fallen

    def combine(mine, far_rows):
        picked = jnp.where(
            keep_slot, jnp.take(far_rows, index_list, axis=0), jnp.zeros((), far_rows.dtype)
        )
        kept = jnp.where(survives, mine, jnp.zeros((), mine.dtype))
        return jnp.concatenate([kept, picked], axis=0)

    inputs = combine(incoming, dead_rows)
    cots = combine(cot_both, dead_cots)
    key_width = w_key.shape[2]
    values = inputs.astype(jnp.float32)
    squares = lax.psum(jnp.sum(values * values, axis=1), "tensor")
    scales = lax.rsqrt(squares / D + EPSILON)
    normed = (values * scales[:, None] * norm_gain).astype(jnp.bfloat16)
    partial_sum = lax.dot_general(
        lax.all_gather(normed, "tensor", axis=1, tiled=True),
        cots,
        (((0,), (0,)), ((), ())),
        preferred_element_type=jnp.float32,
    )
    weight_sum = lax.psum_scatter(
        partial_sum.astype(jnp.bfloat16), "dp", scatter_dimension=0, tiled=True
    ).astype(jnp.float32)
    contract = (((1,), (1,)), ((), ()))
    feature = lax.dot_general(
        cots[:, :key_width], w_key[0], contract, preferred_element_type=jnp.float32
    )
    feature = feature + lax.dot_general(
        cots[:, key_width:], w_value[0], contract, preferred_element_type=jnp.float32
    )
    feature_part = lax.psum_scatter(
        feature.astype(jnp.bfloat16), "tensor", scatter_dimension=1, tiled=True
    ).astype(jnp.float32)
    scaled = norm_gain * feature_part
    input_grad = (scales[:, None] * scaled).astype(jnp.bfloat16)
    returned = passed_along(input_grad, "pipe", -1)
    own_count = returned.shape[0] - index_list.shape[0]
    return (
        weight_sum[:, :key_width][None],
        weight_sum[:, key_width:][None],
        returned[:own_count][None],
        returned[own_count:][None],
    )


def solution(mesh):
    return jax.shard_map(
        on_device,
        mesh=mesh,
        in_specs=(
            P("pipe", "dp", "tensor"),
            P("pipe", "dp", "tensor"),
            P("tensor"),
            P("pipe", None, "tensor"),
            P("pipe", None, "tensor"),
            P("pipe", "dp", "tensor"),
            P("pipe", "dp", "tensor"),
            P("pipe", "dp", "tensor"),
            P("pipe", "dp", "tensor"),
            P("pipe", None),
            P(),
            P(),
        ),
        out_specs=(
            P("pipe", "dp", "tensor"),
            P("pipe", "dp", "tensor"),
            P("pipe", "dp", "tensor"),
            P("pipe", "dp", "tensor"),
        ),
        check_vma=False,
    )
```

profile of v0, /device:TPU:25, one launch (start us, length us, event | category | flops | bytes accessed | tf_op | source)
XLA Modules:
  0.0 428.0 jit_solution(5361297684138172872)
XLA Ops:
  7.2 1.4 dynamic_slice.12
  10.0 1.1 copy.21
  11.1 1.1 copy.23
  13.9 1.5 select_bitcast_fusion
  15.3 1.9 maximum_select_fusion.1
  20.1 91.9 %all-reduce.3.cloned.1.call-done = (bf16[256,4096]{1,0:T(8,128)(2,1)}, bf16[256,1024]{1,0:T(8,128)(2,1)}) async-done(((bf16[256,4096]{1,0:T(8,128)(2,1)}, bf16[256,1024]{1,0:T(8,128)(2,1)}), (bf16[256,4096]{1,0:T(8,128)(2,1)}, bf16[256,1024]{1,0:T(8,128)(2,1)})) %all-reduce.3.cloned.1.call-update) | async-done | bytes 2621456 | tf_op jit(solution)/shard_map/psum | solution.py:25
  112.1 1.8 gather_fusion.1
  114.0 11.4 %fusion.2 = f32[304,8192]{1,0:T(8,128)} fusion(bf16[1,8192,512]{2,1,0:T(8,128)(2,1)} %param.15, bf16[256,1024]{1,0:T(8,128)(2,1)S(1)} %maximum_select_fusion, bf16[48,1024]{1,0:T(8,128)(2,1)S(1)} %select_select_fusion.1), kind=kOutput, calls=%fused_computation.6 | convolution fusion | flops 2550759424 | bytes 18972672 | tf_op jit(solution)/shard_map/dot_general | solution.py:129
  125.4 12.1 %fusion = bf16[304,8192]{1,0:T(8,128)(2,1)} fusion(f32[304,8192]{1,0:T(8,128)} %fusion.2, bf16[1,8192,512]{2,1,0:T(8,128)(2,1)} %param.16, bf16[256,1024]{1,0:T(8,128)(2,1)S(1)} %maximum_select_fusion, bf16[48,1024]{1,0:T(8,128)(2,1)S(1)} %select_select_fusion.1), kind=kOutput, calls=%fused_computation.4 | convolution fusion | flops 2555740160 | bytes 23953408 | tf_op jit(solution)/shard_map/dot_general | solution.py:132
  137.6 1.5 copy-done.4
  139.1 1.5 collective-permute-start
  140.6 57.7 %collective-permute-done = bf16[256,4096]{1,0:T(8,128)(2,1)S(1)} collective-permute-done((bf16[256,4096]{1,0:T(8,128)(2,1)S(1)}, bf16[256,4096]{1,0:T(8,128)(2,1)S(1)}, u32[]{:S(2)}, u32[]{:S(2)}) %collective-permute-start) | collective-permute-done | bytes 2097184 | tf_op jit(solution)/shard_map/ppermute | solution.py:20
  198.5 3.1 gather_fusion
  202.3 5.7 %psum.22 = f32[304]{0:T(512)S(1)} all-reduce(f32[304]{0:T(512)S(1)} %fusion.4), channel_id=1, replica_groups=mesh['dp'=16,'pipe'=4,'tensor'=2] {'tensor'}, use_global_device_ids=true, to_apply=%region_5.6 | all-reduce | flops 304 | bytes 2432 | tf_op jit(solution)/shard_map/psum | solution.py:116
  208.1 12.0 %reduce-scatter.5.cloned.1.call-done = bf16[304,4096]{1,0:T(8,128)(2,1)} async-done(((bf16[304,8192]{1,0:T(8,128)(2,1)}), bf16[304,4096]{1,0:T(8,128)(2,1)}) %reduce-scatter.5.cloned.1.call-update) | async-done | bytes 2490384 | tf_op jit(solution)/shard_map/reduce_scatter | solution.py:135
  220.1 4.9 %multiply_convert_fusion = (bf16[304,4096]{1,0:T(8,128)(2,1)}, bf16[304,4096]{1,0:T(8,128)(2,1)}) fusion(bf16[304,4096]{1,0:T(8,128)(2,1)} %reduce-scatter.5.cloned.1.call-done, f32[4096]{0:T(1024)S(1)} %copy-done.3, f32[304]{0:T(512)S(1)} %add_rsqrt_fusion, bf16[48,4096]{1,0:T(8,128)(2,1)S(1)} %select_select_fusion, ...), kind=kLoop, calls=%fused_computation.13 | loop fusion | flops 13697024 | bytes 9979072 | tf_op jit(solution)/shard_map/convert_element_type | solution.py:139
  225.2 67.0 %all-gather.2.cloned.1.call-done = bf16[304,8192]{1,0:T(8,128)(2,1)} async-done(((bf16[304,4096]{1,0:T(8,128)(2,1)}), bf16[304,8192]{1,0:T(8,128)(2,1)}) %all-gather.2.cloned.1.call-update) | async-done | bytes 4980752 | tf_op jit(solution)/shard_map/all_gather | solution.py:120
  292.2 14.9 %convolution_convert_fusion = bf16[8192,1024]{1,0:T(8,128)(2,1)} fusion(bf16[304,8192]{1,0:T(8,128)(2,1)} %all-gather.2.cloned.1.call-done, bf16[48,1024]{1,0:T(8,128)(2,1)S(1)} %select_select_fusion.1, bf16[256,1024]{1,0:T(8,128)(2,1)S(1)} %maximum_select_fusion), kind=kOutput, calls=%fused_computation.2 | convolution fusion | flops 5109907456 | bytes 22380544 | tf_op jit(solution)/shard_map/dot_general | solution.py:119
  307.2 1.7 copy-done
  309.5 29.3 %collective-permute-done.1 = bf16[304,4096]{1,0:T(8,128)(2,1)S(1)} collective-permute-done((bf16[304,4096]{1,0:T(8,128)(2,1)S(1)}, bf16[304,4096]{1,0:T(8,128)(2,1)S(1)}, u32[]{:S(2)}, u32[]{:S(2)}) %collective-permute-start.1) | collective-permute-done | bytes 2490400 | tf_op jit(solution)/shard_map/ppermute | solution.py:20
  339.6 1.5 slice_bitcast_fusion
  341.0 77.5 %reduce-scatter.3.cloned.1.call-done = bf16[512,1024]{1,0:T(8,128)(2,1)} async-done(((bf16[8192,1024]{1,0:T(8,128)(2,1)}), bf16[512,1024]{1,0:T(8,128)(2,1)}) %reduce-scatter.3.cloned.1.call-update) | async-done | bytes 1048592 | tf_op jit(solution)/shard_map/reduce_scatter | solution.py:125
  418.5 1.5 convert_element_type.76
  420.0 1.5 slice_bitcast_fusion.1
  (51 shorter events, 6.7 us)
Async XLA Ops:
  7.2 6.7 %copy-start.1 = (bf16[1,256,4096]{2,1,0:T(8,128)(2,1)S(1)}, bf16[1,256,4096]{2,1,0:T(8,128)(2,1)}, u32[]{:S(2)}) copy-start(bf16[1,256,4096]{2,1,0:T(8,128)(2,1)} %param.13) | copy-start | bytes 6291460
  7.2 104.9 %all-reduce.3.cloned.1.call-start = ((), (), s32[]{:S(2)}) async-start(), calls=%async_computation.5 | async-start | bytes 5242880 | tf_op jit(solution)/shard_map/psum | solution.py:25
  13.7 6.3 %copy-start.2 = (bf16[1,256,512]{2,1,0:T(8,128)(2,1)S(1)}, bf16[1,256,512]{2,1,0:T(8,128)(2,1)}, u32[]{:S(2)}) copy-start(bf16[1,256,512]{2,1,0:T(8,128)(2,1)} %param.18) | copy-start | bytes 786436
  17.2 202.8 %reduce-scatter.5.cloned.1.call-start = ((), (), s32[]{:S(2)}) async-start(), calls=%async_computation.4 | async-start | bytes 7471104 | tf_op jit(solution)/shard_map/reduce_scatter | solution.py:135
  137.5 1.6 copy-start.4
  137.5 154.7 %all-gather.2.cloned.1.call-start = ((), (), s32[]{:S(2)}) async-start(), calls=%async_computation.2 | async-start | bytes 7471104 | tf_op jit(solution)/shard_map/all_gather | solution.py:120
  139.1 81.0 %copy-start.3 = (f32[4096]{0:T(1024)S(1)}, f32[4096]{0:T(1024)}, u32[]{:S(2)}) copy-start(f32[4096]{0:T(1024)} %param.14) | copy-start | bytes 49156
  139.1 59.2 %collective-permute-start = (bf16[256,4096]{1,0:T(8,128)(2,1)S(1)}, bf16[256,4096]{1,0:T(8,128)(2,1)S(1)}, u32[]{:S(2)}, u32[]{:S(2)}) collective-permute-start(bf16[256,4096]{1,0:T(8,128)(2,1)S(1)} %bitcast.46), channel_id=1, source_target_pairs={{6,0},{0,2},{2,4},{4,6},{7,1},{1,3},{3,5},{5,7},{14,8},{8,10},{10,... | collective-permute-start | bytes 6291464 | tf_op jit(solution)/shard_map/ppermute | solution.py:20
  225.0 193.6 %reduce-scatter.3.cloned.1.call-start = ((), (), s32[]{:S(2)}) async-start(), calls=%async_computation.3 | async-start | bytes 17825792 | tf_op jit(solution)/shard_map/reduce_scatter | solution.py:125
  307.2 1.7 copy-start
  308.9 29.9 %collective-permute-start.1 = (bf16[304,4096]{1,0:T(8,128)(2,1)S(1)}, bf16[304,4096]{1,0:T(8,128)(2,1)S(1)}, u32[]{:S(2)}, u32[]{:S(2)}) collective-permute-start(bf16[304,4096]{1,0:T(8,128)(2,1)S(1)} %copy-done), channel_id=1, source_target_pairs={{2,0},{4,2},{6,4},{0,6},{3,1},{5,3},{7,5},{1,7},{10,8},{12,10},{14... | collective-permute-start | bytes 7471112 | tf_op jit(solution)/shard_map/ppermute | solution.py:20
Sparse Core Ops, SparseCore 0:
  17.3 94.6 all-reduce.2
  137.7 82.3 reduce-scatter.4
  225.1 67.0 all-gather.1
  307.3 111.1 reduce-scatter.2
where the time goes:
time: 430 us; the launch traced here: 428 us
  waiting for transfers between devices  336 us (78%)
  matrix products  38.4 us (9%)
  local copies, waits for them, and re-layouts  16.3 us (4%)
  between operations  16 us (4%)
  other arithmetic  13.6 us (3%)
  blocking collectives  5.75 us (1%)
    psum x1, waiting for transfers between devices, broadcast(): return lax.psum(jnp.where(mine, shard, jnp.zeros_like(shard)), axis)  91.9 us
    ppermute x2, waiting for transfers between devices, passed_along(): return lax.ppermute(block, axis, route)  87 us
    reduce_scatter x1, waiting for transfers between devices, on_device(): lax.psum_scatter(partial_sum.astype(jnp.bfloat16), 'dp', scatter_dimensio...  77.5 us
    all_gather x1, waiting for transfers between devices, on_device(): lax.all_gather(normed, 'tensor', axis=1, tiled=True)  67 us
    dot_general x1, matrix products, on_device(): lax.dot_general(lax.all_gather(normed, 'tensor', axis=1, tiled=True), cot...  14.9 us
    dot_general x1, matrix products, on_device(): lax.dot_general(cots[:, key_width:], w_value[0], contract, preferred_elem...  12.1 us
    reduce_scatter x1, waiting for transfers between devices, on_device(): lax.psum_scatter(feature.astype(jnp.bfloat16), 'tensor', scatter_dimensio...  12 us
    dot_general x1, matrix products, on_device(): lax.dot_general(cots[:, :key_width], w_key[0], contract, preferred_elemen...  11.4 us
  transfers between devices with their start and end apart: 6, of which 6 were waited for; matrix products, arithmetic and copies ran while one was open for 2% of the time, Pallas kernels for 0%

commit v1 on v0

v1 whole, which is shorter than its diff:
```python
import itertools
import math

import jax
import jax.numpy as jnp
from jax import lax
from jax.experimental import pallas as pl
from jax.experimental.pallas import tpu as pltpu
from jax.sharding import PartitionSpec as P

D = 8192
HEAD = 128
BLOCK = 8
RING = 4
SECTIONS = 4

EPSILON = 1e-05
ROPE_BASE = 500000.0

AXES = ("dp", "pipe", "tensor")


def moved(block, rule):
    route = []
    for x, z, s, t in itertools.product(range(RING), range(RING), range(SECTIONS), range(2)):
        target = rule(x, z, s, t)
        if target is not None:
            a, b, c, d = target
            there = ((a % RING * RING + b % RING) * SECTIONS + c % SECTIONS) * 2 + d % 2
            route.append((((x * RING + z) * SECTIONS + s) * 2 + t, there))
    return lax.ppermute(block, AXES, route)


def frequencies():
    index_half = jnp.arange(HEAD // 2, dtype=jnp.float32)
    return jnp.exp(-(2.0 * index_half / HEAD) * math.log(ROPE_BASE))


def derotate(cotangent, position):
    row_count = cotangent.shape[0]
    pieces = cotangent.astype(jnp.float32).reshape(row_count, -1, 2, HEAD // 2)
    angles = position.astype(jnp.float32)[:, None] * frequencies()[None, :]
    cosine = jnp.cos(angles)[:, None, :]
    sine_values = jnp.sin(angles)[:, None, :]
    lower_half = pieces[:, :, 0, :]
    upper_half = pieces[:, :, 1, :]
    new_lower = lower_half * cosine + upper_half * sine_values
    new_upper = upper_half * cosine - lower_half * sine_values
    return jnp.stack([new_lower, new_upper], axis=2).reshape(row_count, -1).astype(jnp.bfloat16)


def slot_selection(plan_row, owner, capacity_blocks, rows):
    block_count = plan_row.shape[0]
    block_ids = jnp.arange(block_count, dtype=jnp.int32)
    same_owner = plan_row[:, None] == plan_row[None, :]
    earlier = block_ids[None, :] < block_ids[:, None]
    block_rank = jnp.sum(jnp.where(same_owner & earlier, 1, 0), axis=1).astype(jnp.int32)
    slot_of_block = jnp.where(plan_row == owner, block_rank, -1)
    slot_of_row = jnp.repeat(slot_of_block, BLOCK) * BLOCK + jnp.tile(
        jnp.arange(BLOCK, dtype=jnp.int32), block_count
    )
    slot_of_row = jnp.where(jnp.repeat(slot_of_block, BLOCK) < 0, -1, slot_of_row)
    slot_ids = jnp.arange(capacity_blocks * BLOCK, dtype=jnp.int32)
    return (slot_ids[:, None] == slot_of_row[None, :]).astype(jnp.bfloat16)


NT = (((1,), (1,)), ((), ()))
TN = (((0,), (0,)), ((), ()))
TILE = 1024


def feature_kernel(half, cots, scale, w_key, w_value, out):
    width = w_key.shape[1]
    total = lax.dot_general(cots[:, :width], w_key[...], NT, preferred_element_type=jnp.float32)
    total = total + lax.dot_general(
        cots[:, width:], w_value[...], NT, preferred_element_type=jnp.float32
    )
    out[...] = (total * scale[...]).astype(out.dtype)


def feature_half(cots, scale, w_key, w_value, half):
    rows = cots.shape[0]
    tiles = D // 2 // TILE
    width = w_key.shape[1]
    weights = pl.BlockSpec((TILE, width), lambda i, half: (half[0] * tiles + i, 0))
    return pl.pallas_call(
        feature_kernel,
        out_shape=jax.ShapeDtypeStruct((rows, D // 2), jnp.bfloat16),
        grid_spec=pltpu.PrefetchScalarGridSpec(
            num_scalar_prefetch=1,
            grid=(tiles,),
            in_specs=[
                pl.BlockSpec((rows, 2 * width), lambda i, half: (0, 0)),
                pl.BlockSpec((rows, 1), lambda i, half: (0, 0)),
                weights,
                weights,
            ],
            out_specs=pl.BlockSpec((rows, TILE), lambda i, half: (0, i)),
        ),
        compiler_params=pltpu.CompilerParams(vmem_limit_bytes=32 * 1024 * 1024),
    )(jnp.reshape(half, (1,)), cots, scale, w_key, w_value)


def on_device(
    stream,
    backup_stream,
    norm_gain,
    w_key,
    w_value,
    key_cot,
    value_cot,
    backup_key_cot,
    backup_value_cot,
    positions,
    failed,
    reroute_plan,
):
    section = lax.axis_index("pipe")
    member = lax.axis_index("dp")
    side = lax.axis_index("tensor")
    replicas = lax.axis_size("dp")
    at_x, at_z = member // RING, member % RING
    fallen = failed[section]
    keeper = (fallen + 1) % replicas
    plan_row = reroute_plan[section]
    rows = stream.shape[1]
    capacity_blocks = 2 * ((plan_row.shape[0] + replicas - 2) // (replicas - 1))
    width = w_key.shape[2]

    own_positions = lax.dynamic_slice_in_dim(positions[0], member * rows, rows, 0)
    dead_positions = lax.dynamic_slice_in_dim(positions[0], fallen * rows, rows, 0)
    cot_key = derotate(key_cot[0], own_positions)
    cot_value = value_cot[0]

    def to_stream(block):
        straight = moved(block, lambda x, z, s, t: (x, z, s - 1, t))
        across = moved(block, lambda x, z, s, t: (x, z, s - 1, 1 - t))
        return straight, across

    far_key = jnp.concatenate(to_stream(cot_key), axis=1)
    far_value = jnp.concatenate(to_stream(cot_value), axis=1)

    values = stream[0].astype(jnp.float32)
    saved = backup_stream[0].astype(jnp.float32)
    squares = jnp.concatenate([jnp.sum(values * values, axis=1), jnp.sum(saved * saved, axis=1)])
    scales = lax.rsqrt(lax.psum(squares, "tensor") / D + EPSILON)
    own_scale, saved_scale = scales[:rows, None], scales[rows:, None]
    normed = (values * own_scale * norm_gain).astype(jnp.bfloat16)
    saved_normed = (saved * saved_scale * norm_gain).astype(jnp.bfloat16)

    held_scale = jnp.where(member == keeper, saved_scale, 0.0)
    scale_high = held_scale.astype(jnp.bfloat16)
    scale_low = (held_scale - scale_high.astype(jnp.float32)).astype(jnp.bfloat16)
    saved_cots = jnp.concatenate(
        [
            derotate(backup_key_cot[0], dead_positions),
            backup_value_cot[0],
            jnp.broadcast_to(scale_high, (rows, HEAD)),
            jnp.broadcast_to(scale_low, (rows, HEAD)),
        ],
        axis=1,
    )
    dead_normed, dead_cots = lax.psum((saved_normed, saved_cots), "dp")

    cots = jnp.concatenate([cot_key, cot_value], axis=1)
    ones = jnp.ones((rows, 1), jnp.float32)
    across = feature_half(cots, ones, w_key[0], w_value[0], 1 - side)
    straight = feature_half(cots, ones, w_key[0], w_value[0], side)
    across = moved(across, lambda x, z, s, t: (x, z, s - 1, 1 - t))
    straight = moved(straight, lambda x, z, s, t: (x, z, s - 1, t))
    feature = straight.astype(jnp.float32) + across.astype(jnp.float32)
    stream_grad = (own_scale * (norm_gain * feature)).astype(jnp.bfloat16)

    fourth = normed.shape[1] // RING
    block = fourth // 2

    def along_x(tile, step):
        return moved(tile, lambda x, z, s, t: (x + step, z, s, t)) if step else tile

    def along_z(tile, step):
        return moved(tile, lambda x, z, s, t: (x, z + step, s, t)) if step else tile

    def reduced(piece_of, half_of, head_of, far_cots, at_gather, at_reduce, gather, reduce):
        lhs, rhs = [], []
        for step in range(RING):
            lhs.append(gather(piece_of((at_gather + step) % RING), step))
            rhs.append(gather(far_cots, step))
        lhs, rhs = jnp.concatenate(lhs, axis=0), jnp.concatenate(rhs, axis=0)
        total = None
        for step in (2, 1, 3, 0):
            there = (at_reduce + step) % RING
            part = lax.dot_general(
                lax.dynamic_slice_in_dim(lhs, half_of(there) * block, block, 1),
                lax.dynamic_slice_in_dim(rhs, head_of(there) * width, width, 1),
                TN,
                preferred_element_type=jnp.float32,
            )
            part = reduce(part.astype(jnp.bfloat16), step).astype(jnp.float32)
            total = part if total is None else total + part
        return total.astype(jnp.bfloat16)

    key_blocks = normed.reshape(rows, 2, RING, block)
    grad_key = reduced(
        lambda z: lax.dynamic_index_in_dim(key_blocks, z, 2, keepdims=False).reshape(rows, fourth),
        lambda x: x % 2,
        lambda x: (x // 2) ^ side,
        far_key,
        at_z,
        at_x,
        along_z,
        along_x,
    )
    grad_key = moved(grad_key, lambda x, z, s, t: (2 * t + x % 2, z, s + 1, x // 2))
    grad_value = reduced(
        lambda x: lax.dynamic_slice_in_dim(normed, (2 * (x % 2) + x // 2) * fourth, fourth, 1),
        lambda z: z % 2,
        lambda z: (z // 2) ^ (at_x // 2),
        far_value,
        at_x,
        at_z,
        along_x,
        along_z,
    )
    grad_value = moved(
        grad_value,
        lambda x, z, s, t: (2 * t + x % 2, 2 * (x // 2) + z % 2, s + 1, t ^ (z // 2) ^ (x // 2)),
    )

    home = member // (replicas // 2)
    dead_block = lax.dynamic_slice_in_dim(
        dead_normed, (member % (replicas // 2)) * block, block, 1
    )
    lent = moved(
        dead_block, lambda x, z, s, t: (x, z, s, 1 - t) if t == x // 2 else None
    )
    dead_block = jnp.where(home == side, dead_block, lent)
    dead_part = lax.dot_general(
        dead_block, dead_cots[:, : 2 * width], TN, preferred_element_type=jnp.float32
    )
    grad_key = grad_key.astype(jnp.float32) + dead_part[:, :width]
    grad_value = grad_value.astype(jnp.float32) + dead_part[:, width:]

    selection = slot_selection(plan_row, member, capacity_blocks, rows)
    slots = jnp.dot(selection, dead_cots, preferred_element_type=jnp.float32)
    slot_scale = slots[:, 2 * width : 2 * width + 1] + slots[:, 2 * width + HEAD : 2 * width + HEAD + 1]
    slot_cots = slots[:, : 2 * width].astype(jnp.bfloat16)
    across = feature_half(slot_cots, slot_scale, w_key[0], w_value[0], 1 - side)
    straight = feature_half(slot_cots, slot_scale, w_key[0], w_value[0], side)
    across = moved(across, lambda x, z, s, t: (x, z, s - 1, 1 - t))
    straight = moved(straight, lambda x, z, s, t: (x, z, s - 1, t))
    feature = straight.astype(jnp.float32) + across.astype(jnp.float32)
    spill_grad = (norm_gain * feature).astype(jnp.bfloat16)

    return grad_key[None], grad_value[None], stream_grad[None], spill_grad[None]


def solution(mesh):
    return jax.shard_map(
        on_device,
        mesh=mesh,
        in_specs=(
            P("pipe", "dp", "tensor"),
            P("pipe", "dp", "tensor"),
            P("tensor"),
            P("pipe", None, "tensor"),
            P("pipe", None, "tensor"),
            P("pipe", "dp", "tensor"),
            P("pipe", "dp", "tensor"),
            P("pipe", "dp", "tensor"),
            P("pipe", "dp", "tensor"),
            P("pipe", None),
            P(),
            P(),
        ),
        out_specs=(
            P("pipe", "dp", "tensor"),
            P("pipe", "dp", "tensor"),
            P("pipe", "dp", "tensor"),
            P("pipe", "dp", "tensor"),
        ),
        check_vma=False,
    )
```

time: 430 us -> 322 us (0.75)
  waiting for transfers between devices: 336 us -> 118 us
  starting transfers between devices: 2.49 us -> 49.5 us
  local copies, waits for them, and re-layouts: 16.3 us -> 50.8 us
  blocking collectives: 5.75 us -> 36 us
  matrix products: 38.4 us -> 16.5 us
  Pallas kernels: 0 us -> 12.9 us
  other arithmetic: 13.6 us -> 19.4 us
    reduce_scatter x2 -> x0, waiting for transfers between devices: 89.5 us -> none  [the longest x1 77.5 us: on_device(): lax.psum_scatter(partial_sum.astype(jnp.bfloat16), 'dp', scatter_dimensio...]
    all_gather x1 -> x0, waiting for transfers between devices: 67 us -> none  [on_device(): lax.all_gather(normed, 'tensor', axis=1, tiled=True)]
    psum x1, waiting for transfers between devices: 91.9 us -> 41.5 us  [on_device(): dead_normed, dead_cots = lax.psum((saved_normed, saved_cots), 'dp')]
    ppermute x2 -> x29, starting transfers between devices: 2.15 us -> 49.4 us  [moved(): return lax.ppermute(block, AXES, route)]
    psum x1, blocking collectives: 5.75 us -> 36 us  [on_device(): scales = lax.rsqrt(lax.psum(squares, 'tensor') / D + EPSILON)]
    unnamed x12 -> x53, local copies, waits for them, and re-layouts: 5.38 us -> 33.8 us
    dot_general x3 -> x10, matrix products: 38.4 us -> 16.5 us  [the longest x8 14.6 us: reduced(): lax.dot_general(lax.dynamic_slice_in_dim(lhs, half_of(there) * block, blo...]
    pallas_call x0 -> x4, Pallas kernels: none -> 12.9 us  [feature_half(): pl.pallas_call(feature_kernel, out_shape=jax.ShapeDtypeStruct((rows, D //...]
  transfers between devices with their start and end apart: 6 -> 30, of which waited for: 6 -> 11; matrix products, arithmetic and copies ran while one was open for 2% -> 16% of each run, Pallas kernels for 0% -> 4%
where the time goes in v1:
time: 322 us; the launch traced here: 319 us
  waiting for transfers between devices  118 us (37%)
  local copies, waits for them, and re-layouts  50.8 us (16%)
  starting transfers between devices  49.5 us (15%)
  blocking collectives  36 us (11%)
  other arithmetic  19.4 us (6%)
  matrix products  16.5 us (5%)
  between operations  16 us (5%)
  Pallas kernels  12.9 us (4%)
    ppermute x29, waiting for transfers between devices, moved(): return lax.ppermute(block, AXES, route)  76.1 us
    ppermute x29, starting transfers between devices, moved(): return lax.ppermute(block, AXES, route)  49.4 us
    psum x1, waiting for transfers between devices, on_device(): dead_normed, dead_cots = lax.psum((saved_normed, saved_cots), 'dp')  41.5 us
    psum x1, blocking collectives, on_device(): scales = lax.rsqrt(lax.psum(squares, 'tensor') / D + EPSILON)  36 us
    unnamed x53, local copies, waits for them, and re-layouts  33.8 us
    dot_general x8, matrix products, reduced(): lax.dot_general(lax.dynamic_slice_in_dim(lhs, half_of(there) * block, blo...  14.6 us
    pallas_call x4, Pallas kernels, feature_half(): pl.pallas_call(feature_kernel, out_shape=jax.ShapeDtypeStruct((rows, D //...  12.9 us
    convert_element_type x2, local copies, waits for them, and re-layouts, on_device(): values = stream[0].astype(jnp.float32)  11.4 us
  transfers between devices with their start and end apart: 30, of which 11 were waited for; matrix products, arithmetic and copies ran while one was open for 16% of the time, Pallas kernels for 4%

profile of v1, /device:TPU:25, one launch (start us, length us, event | category | flops | bytes accessed | tf_op | source)
XLA Modules:
  0.0 318.7 jit_solution(7654888015027437550)
XLA Ops:
  22.4 3.8 %shard_map.147 = bf16[256,4096]{1,0:T(8,128)(2,1)} custom-call(s32[1]{0:T(128)} %bitcast.21.half, bf16[256,1024]{1,0:T(8,128)(2,1)S(1)} %pad_maximum_fusion.5.cots, f32[256,1]{1,0:T(8,128)S(1)} %broadcast_in_dim.74.scale, bf16[8192,512]{1,0:T(8,128)(2,1)S(1)} %bitcast.48, bf16[8192,512]{1,0:T(8,128)(2,1)S(1)} %bitcast.52), custom_call_target="tpu_custom_call" | custom-call | tf_op jit(solution)/shard_map/pallas_call | solution.py:86
  26.3 3.4 %copy-done.1 = bf16[1,8192,512]{2,1,0:T(8,128)(2,1)S(1)} copy-done((bf16[1,8192,512]{2,1,0:T(8,128)(2,1)S(1)}, bf16[1,8192,512]{2,1,0:T(8,128)(2,1)}, u32[]{:S(2)}) %copy-start.1) | copy-done | bytes 8388632
  29.7 3.4 %copy-done.5 = bf16[1,8192,512]{2,1,0:T(8,128)(2,1)S(1)} copy-done((bf16[1,8192,512]{2,1,0:T(8,128)(2,1)S(1)}, bf16[1,8192,512]{2,1,0:T(8,128)(2,1)}, u32[]{:S(2)}) %copy-start.5) | copy-done | bytes 8388632
  36.2 4.1 %collective-permute-start.26 = (bf16[256,4096]{1,0:T(8,128)(2,1)S(1)}, bf16[256,4096]{1,0:T(8,128)(2,1)}, u32[]{:S(2)}, u32[]{:S(2)}) collective-permute-start(bf16[256,4096]{1,0:T(8,128)(2,1)S(1)} %shard_map.148), channel_id=1, source_target_pairs={{0,7},{1,6},{2,1},{3,0},{4,3},{5,2},{6,5},{7,4},{8,15},{9,14},{10,... | collective-permute-start | bytes 6291464 | tf_op jit(solution)/shard_map/ppermute | solution.py:31
  41.2 36.0 %psum.21 = f32[512]{0:T(512)S(1)} all-reduce(f32[512]{0:T(512)S(1)} %pad_maximum_fusion.8), channel_id=1, replica_groups=mesh['dp'=16,'pipe'=4,'tensor'=2] {'tensor'}, use_global_device_ids=true, to_apply=%region_2.3 | all-reduce | flops 512 | bytes 4096 | tf_op jit(solution)/shard_map/psum | solution.py:146
  78.0 6.1 %reshape.222 = f32[256,2,4,512]{3,2,1,0:T(4,128)} reshape(bf16[1,256,4096]{2,1,0:T(8,128)(2,1)} %param.12) | data formatting | bytes 6291456 | tf_op jit(solution)/shard_map/convert_element_type | solution.py:143
  84.3 5.3 %copy.27 = f32[256,2,4,512]{0,3,1,2:T(8,128)} copy(f32[256,2,4,512]{3,2,1,0:T(4,128)} %reshape.222) | data formatting | bytes 8388608 | tf_op jit(solution)/shard_map/convert_element_type | solution.py:143
  94.5 3.8 %collective-permute-start.2 = (bf16[256,1024]{0,1:T(8,128)(2,1)}, bf16[256,1024]{0,1:T(8,128)(2,1)}, u32[]{:S(2)}, u32[]{:S(2)}) collective-permute-start(bf16[256,1024]{0,1:T(8,128)(2,1)} %bitcast.5), channel_id=1, source_target_pairs={{0,24},{1,25},{2,26},{3,27},{4,28},{5,29},{6,30},{7,31},{8,0},{9,1... | collective-permute-start | bytes 1572872 | tf_op jit(solution)/shard_map/ppermute | solution.py:31
  106.2 11.7 %collective-permute-done.2 = bf16[256,1024]{0,1:T(8,128)(2,1)} collective-permute-done((bf16[256,1024]{0,1:T(8,128)(2,1)}, bf16[256,1024]{0,1:T(8,128)(2,1)}, u32[]{:S(2)}, u32[]{:S(2)}) %collective-permute-start.2) | collective-permute-done | bytes 524320 | tf_op jit(solution)/shard_map/ppermute | solution.py:31
  117.9 3.4 %collective-permute-start.7 = (bf16[256,1024]{0,1:T(8,128)(2,1)}, bf16[256,1024]{0,1:T(8,128)(2,1)}, u32[]{:S(2)}, u32[]{:S(2)}) collective-permute-start(bf16[256,1024]{0,1:T(8,128)(2,1)} %constant_dynamic-update-slice_fusion), channel_id=1, source_target_pairs={{0,24},{1,25},{2,26},{3,27},{4,28},{5,29},{6,30},{7,31},{8,0},{9,1... | collective-permute-start | bytes 1572872 | tf_op jit(solution)/shard_map/ppermute | solution.py:31
  121.9 5.9 %fusion.6 = (bf16[1,256,4096]{2,1,0:T(8,128)(2,1)}, bf16[256,4096]{1,0:T(8,128)(2,1)S(1)}, bf16[256,4096]{1,0:T(8,128)(2,1)}) fusion(bf16[256,4096]{1,0:T(8,128)(2,1)} %collective-permute-done.26, bf16[256,4096]{1,0:T(8,128)(2,1)} %collective-permute-done.25, f32[256]{0:T(256)S(1)} %get-tuple-element.25, f32[4096]{0:T(1024)S(1)} %copy-done.21, ...), kind=kLoop, calls=%fused_computation.12 | loop fusion | flops 14680064 | bytes 14698496 | tf_op jit(solution)/shard_map/broadcast_in_dim | solution.py:254
  133.8 8.3 %collective-permute-done.7 = bf16[256,1024]{0,1:T(8,128)(2,1)} collective-permute-done((bf16[256,1024]{0,1:T(8,128)(2,1)}, bf16[256,1024]{0,1:T(8,128)(2,1)}, u32[]{:S(2)}, u32[]{:S(2)}) %collective-permute-start.7) | collective-permute-done | bytes 524320 | tf_op jit(solution)/shard_map/ppermute | solution.py:31
  143.3 17.5 %collective-permute-done.5 = bf16[256,1024]{0,1:T(8,128)(2,1)} collective-permute-done((bf16[256,1024]{0,1:T(8,128)(2,1)}, bf16[256,1024]{0,1:T(8,128)(2,1)}, u32[]{:S(2)}, u32[]{:S(2)}) %collective-permute-start.5) | collective-permute-done | bytes 524320 | tf_op jit(solution)/shard_map/ppermute | solution.py:31
  173.6 7.9 %collective-permute-done.15 = bf16[256,1024]{1,0:T(8,128)(2,1)S(1)} collective-permute-done((bf16[256,1024]{1,0:T(8,128)(2,1)S(1)}, bf16[256,1024]{1,0:T(8,128)(2,1)S(1)}, u32[]{:S(2)}, u32[]{:S(2)}) %collective-permute-start.15) | collective-permute-done | bytes 524320 | tf_op jit(solution)/shard_map/ppermute | solution.py:31
  181.5 5.3 %collective-permute-start.10 = (bf16[512,512]{1,0:T(8,128)(2,1)}, bf16[512,512]{1,0:T(8,128)(2,1)}, u32[]{:S(2)}, u32[]{:S(2)}) collective-permute-start(bf16[512,512]{1,0:T(8,128)(2,1)} %convolution_convert_fusion.5), channel_id=1, source_target_pairs={{0,96},{1,97},{2,98},{3,99},{4,100},{5,101},{6,102},{7,103},{8,104... | collective-permute-start | bytes 1572872 | tf_op jit(solution)/shard_map/ppermute | solution.py:31
  186.8 8.2 %collective-permute-done.13 = bf16[256,1024]{1,0:T(8,128)(2,1)S(1)} collective-permute-done((bf16[256,1024]{1,0:T(8,128)(2,1)S(1)}, bf16[256,1024]{1,0:T(8,128)(2,1)S(1)}, u32[]{:S(2)}, u32[]{:S(2)}) %collective-permute-start.13) | collective-permute-done | bytes 524320 | tf_op jit(solution)/shard_map/ppermute | solution.py:31
  196.8 8.6 %collective-permute-start.21 = (bf16[512,512]{1,0:T(8,128)(2,1)}, bf16[512,512]{1,0:T(8,128)(2,1)S(1)}, u32[]{:S(2)}, u32[]{:S(2)}) collective-permute-start(bf16[512,512]{1,0:T(8,128)(2,1)} %convolution_convert_fusion.3), channel_id=1, source_target_pairs={{0,16},{1,17},{2,18},{3,19},{4,20},{5,21},{6,22},{7,23},{8,24},{9,... | collective-permute-start | bytes 1572872 | tf_op jit(solution)/shard_map/ppermute | solution.py:31
  212.3 5.4 %collective-permute-done.9 = bf16[512,512]{1,0:T(8,128)(2,1)} collective-permute-done((bf16[512,512]{1,0:T(8,128)(2,1)}, bf16[512,512]{1,0:T(8,128)(2,1)}, u32[]{:S(2)}, u32[]{:S(2)}) %collective-permute-start.9) | collective-permute-done | bytes 524320 | tf_op jit(solution)/shard_map/ppermute | solution.py:31
  222.4 6.3 %collective-permute-done.22 = bf16[512,512]{1,0:T(8,128)(2,1)} collective-permute-done((bf16[512,512]{1,0:T(8,128)(2,1)}, bf16[512,512]{1,0:T(8,128)(2,1)}, u32[]{:S(2)}, u32[]{:S(2)}) %collective-permute-start.22) | collective-permute-done | bytes 524320 | tf_op jit(solution)/shard_map/ppermute | solution.py:31
  231.5 41.5 %all-reduce.3.cloned.1.call-done = (bf16[256,1280]{0,1:T(8,128)(2,1)}, bf16[256,4096]{1,0:T(8,128)(2,1)}) async-done(((bf16[256,1280]{0,1:T(8,128)(2,1)}, bf16[256,4096]{1,0:T(8,128)(2,1)}), (bf16[256,1280]{0,1:T(8,128)(2,1)}, bf16[256,4096]{1,0:T(8,128)(2,1)})) %all-reduce.3.cloned.1.call-update) | async-done | bytes 2752528 | tf_op jit(solution)/shard_map/psum | solution.py:163
  280.0 3.4 %copy-done.6 = bf16[1,8192,512]{2,1,0:T(8,128)(2,1)S(1)} copy-done((bf16[1,8192,512]{2,1,0:T(8,128)(2,1)S(1)}, bf16[1,8192,512]{2,1,0:T(8,128)(2,1)}, u32[]{:S(2)}) %copy-start.6) | copy-done | bytes 8388632
  289.8 3.4 %copy-done.7 = bf16[1,8192,512]{2,1,0:T(8,128)(2,1)S(1)} copy-done((bf16[1,8192,512]{2,1,0:T(8,128)(2,1)S(1)}, bf16[1,8192,512]{2,1,0:T(8,128)(2,1)}, u32[]{:S(2)}) %copy-start.7) | copy-done | bytes 8388632
  296.1 4.9 %collective-permute-start.28 = (bf16[48,4096]{1,0:T(8,128)(2,1)S(1)}, bf16[48,4096]{1,0:T(8,128)(2,1)S(1)}, u32[]{:S(2)}, u32[]{:S(2)}) collective-permute-start(bf16[48,4096]{1,0:T(8,128)(2,1)S(1)} %shard_map.150), channel_id=1, source_target_pairs={{0,7},{1,6},{2,1},{3,0},{4,3},{5,2},{6,5},{7,4},{8,15},{9,14},{10,... | collective-permute-start | bytes 1179656 | tf_op jit(solution)/shard_map/ppermute | solution.py:31
  303.2 6.3 %collective-permute-done.28 = bf16[48,4096]{1,0:T(8,128)(2,1)S(1)} collective-permute-done((bf16[48,4096]{1,0:T(8,128)(2,1)S(1)}, bf16[48,4096]{1,0:T(8,128)(2,1)S(1)}, u32[]{:S(2)}, u32[]{:S(2)}) %collective-permute-start.28) | collective-permute-done | bytes 393248 | tf_op jit(solution)/shard_map/ppermute | solution.py:31
  (150 shorter events, 88.8 us)
Async XLA Ops:
  7.2 265.8 %all-reduce.3.cloned.1.call-start = ((), (), s32[]{:S(2)}) async-start(), calls=%async_computation | async-start | bytes 5505024 | tf_op jit(solution)/shard_map/psum | solution.py:163
  12.8 88.3 %collective-permute-start.4 = (bf16[256,512]{0,1:T(8,128)(2,1)S(1)}, bf16[256,512]{0,1:T(8,128)(2,1)}, u32[]{:S(2)}, u32[]{:S(2)}) collective-permute-start(bf16[256,512]{0,1:T(8,128)(2,1)S(1)} %bitcast.61), channel_id=1, source_target_pairs={{0,7},{1,6},{2,1},{3,0},{4,3},{5,2},{6,5},{7,4},{8,15},{9,14},{10,... | collective-permute-start | bytes 786440 | tf_op jit(solution)/shard_map/ppermute | solution.py:31
  14.4 80.1 %collective-permute-start.3 = (bf16[256,512]{0,1:T(8,128)(2,1)S(1)}, bf16[256,512]{0,1:T(8,128)(2,1)}, u32[]{:S(2)}, u32[]{:S(2)}) collective-permute-start(bf16[256,512]{0,1:T(8,128)(2,1)S(1)} %bitcast.62), channel_id=1, source_target_pairs={{0,6},{1,7},{2,0},{3,1},{4,2},{5,3},{6,4},{7,5},{8,14},{9,15},{10,... | collective-permute-start | bytes 786440 | tf_op jit(solution)/shard_map/ppermute | solution.py:31
  14.4 83.9 %collective-permute-start.16 = (bf16[256,512]{1,0:T(8,128)(2,1)}, bf16[256,512]{1,0:T(8,128)(2,1)}, u32[]{:S(2)}, u32[]{:S(2)}) collective-permute-start(bf16[256,512]{1,0:T(8,128)(2,1)} %bitcast.19), channel_id=1, source_target_pairs={{0,6},{1,7},{2,0},{3,1},{4,2},{5,3},{6,4},{7,5},{8,14},{9,15},{10,... | collective-permute-start | bytes 786440 | tf_op jit(solution)/shard_map/ppermute | solution.py:31
  26.2 95.1 %collective-permute-start.25 = (bf16[256,4096]{1,0:T(8,128)(2,1)}, bf16[256,4096]{1,0:T(8,128)(2,1)}, u32[]{:S(2)}, u32[]{:S(2)}) collective-permute-start(bf16[256,4096]{1,0:T(8,128)(2,1)} %shard_map.147), channel_id=1, source_target_pairs={{0,6},{1,7},{2,0},{3,1},{4,2},{5,3},{6,4},{7,5},{8,14},{9,15},{10,... | collective-permute-start | bytes 6291464 | tf_op jit(solution)/shard_map/ppermute | solution.py:31
  36.2 85.1 %collective-permute-start.26 = (bf16[256,4096]{1,0:T(8,128)(2,1)S(1)}, bf16[256,4096]{1,0:T(8,128)(2,1)}, u32[]{:S(2)}, u32[]{:S(2)}) collective-permute-start(bf16[256,4096]{1,0:T(8,128)(2,1)S(1)} %shard_map.148), channel_id=1, source_target_pairs={{0,7},{1,6},{2,1},{3,0},{4,3},{5,2},{6,5},{7,4},{8,15},{9,14},{10,... | collective-permute-start | bytes 6291464 | tf_op jit(solution)/shard_map/ppermute | solution.py:31
  94.5 23.4 %collective-permute-start.2 = (bf16[256,1024]{0,1:T(8,128)(2,1)}, bf16[256,1024]{0,1:T(8,128)(2,1)}, u32[]{:S(2)}, u32[]{:S(2)}) collective-permute-start(bf16[256,1024]{0,1:T(8,128)(2,1)} %bitcast.5), channel_id=1, source_target_pairs={{0,24},{1,25},{2,26},{3,27},{4,28},{5,29},{6,30},{7,31},{8,0},{9,1... | collective-permute-start | bytes 1572872 | tf_op jit(solution)/shard_map/ppermute | solution.py:31
  101.1 27.7 %collective-permute-start.1 = (bf16[256,1024]{0,1:T(8,128)(2,1)}, bf16[256,1024]{0,1:T(8,128)(2,1)}, u32[]{:S(2)}, u32[]{:S(2)}) collective-permute-start(bf16[256,1024]{0,1:T(8,128)(2,1)} %bitcast.65), channel_id=1, source_target_pairs={{0,16},{1,17},{2,18},{3,19},{4,20},{5,21},{6,22},{7,23},{8,24},{9,... | collective-permute-start | bytes 1572872 | tf_op jit(solution)/shard_map/ppermute | solution.py:31
  106.2 25.4 %collective-permute-start = (bf16[256,1024]{0,1:T(8,128)(2,1)}, bf16[256,1024]{0,1:T(8,128)(2,1)}, u32[]{:S(2)}, u32[]{:S(2)}) collective-permute-start(bf16[256,1024]{0,1:T(8,128)(2,1)} %bitcast.64), channel_id=1, source_target_pairs={{0,8},{1,9},{2,10},{3,11},{4,12},{5,13},{6,14},{7,15},{8,16},{9,17... | collective-permute-start | bytes 1572872 | tf_op jit(solution)/shard_map/ppermute | solution.py:31
  117.9 24.1 %collective-permute-start.7 = (bf16[256,1024]{0,1:T(8,128)(2,1)}, bf16[256,1024]{0,1:T(8,128)(2,1)}, u32[]{:S(2)}, u32[]{:S(2)}) collective-permute-start(bf16[256,1024]{0,1:T(8,128)(2,1)} %constant_dynamic-update-slice_fusion), channel_id=1, source_target_pairs={{0,24},{1,25},{2,26},{3,27},{4,28},{5,29},{6,30},{7,31},{8,0},{9,1... | collective-permute-start | bytes 1572872 | tf_op jit(solution)/shard_map/ppermute | solution.py:31
  121.3 22.0 %collective-permute-start.6 = (bf16[256,1024]{0,1:T(8,128)(2,1)}, bf16[256,1024]{0,1:T(8,128)(2,1)}, u32[]{:S(2)}, u32[]{:S(2)}) collective-permute-start(bf16[256,1024]{0,1:T(8,128)(2,1)} %constant_dynamic-update-slice_fusion), channel_id=1, source_target_pairs={{0,16},{1,17},{2,18},{3,19},{4,20},{5,21},{6,22},{7,23},{8,24},{9,... | collective-permute-start | bytes 1572872 | tf_op jit(solution)/shard_map/ppermute | solution.py:31
  121.3 39.4 %collective-permute-start.5 = (bf16[256,1024]{0,1:T(8,128)(2,1)}, bf16[256,1024]{0,1:T(8,128)(2,1)}, u32[]{:S(2)}, u32[]{:S(2)}) collective-permute-start(bf16[256,1024]{0,1:T(8,128)(2,1)} %constant_dynamic-update-slice_fusion), channel_id=1, source_target_pairs={{0,8},{1,9},{2,10},{3,11},{4,12},{5,13},{6,14},{7,15},{8,16},{9,17... | collective-permute-start | bytes 1572872 | tf_op jit(solution)/shard_map/ppermute | solution.py:31
  128.9 37.3 %collective-permute-start.20 = (bf16[256,1024]{1,0:T(8,128)(2,1)S(1)}, bf16[256,1024]{1,0:T(8,128)(2,1)S(1)}, u32[]{:S(2)}, u32[]{:S(2)}) collective-permute-start(bf16[256,1024]{1,0:T(8,128)(2,1)S(1)} %constant_dynamic-update-slice_fusion.2), channel_id=1, source_target_pairs={{0,96},{1,97},{2,98},{3,99},{4,100},{5,101},{6,102},{7,103},{8,104... | collective-permute-start | bytes 1572872 | tf_op jit(solution)/shard_map/ppermute | solution.py:31
  131.6 38.6 %collective-permute-start.19 = (bf16[256,1024]{1,0:T(8,128)(2,1)S(1)}, bf16[256,1024]{1,0:T(8,128)(2,1)S(1)}, u32[]{:S(2)}, u32[]{:S(2)}) collective-permute-start(bf16[256,1024]{1,0:T(8,128)(2,1)S(1)} %constant_dynamic-update-slice_fusion.2), channel_id=1, source_target_pairs={{0,64},{1,65},{2,66},{3,67},{4,68},{5,69},{6,70},{7,71},{8,72},{9,... | collective-permute-start | bytes 1572872 | tf_op jit(solution)/shard_map/ppermute | solution.py:31
  142.0 30.6 %collective-permute-start.18 = (bf16[256,1024]{1,0:T(8,128)(2,1)S(1)}, bf16[256,1024]{1,0:T(8,128)(2,1)S(1)}, u32[]{:S(2)}, u32[]{:S(2)}) collective-permute-start(bf16[256,1024]{1,0:T(8,128)(2,1)S(1)} %constant_dynamic-update-slice_fusion.2), channel_id=1, source_target_pairs={{0,32},{1,33},{2,34},{3,35},{4,36},{5,37},{6,38},{7,39},{8,40},{9,... | collective-permute-start | bytes 1572872 | tf_op jit(solution)/shard_map/ppermute | solution.py:31
  166.2 28.8 %collective-permute-start.13 = (bf16[256,1024]{1,0:T(8,128)(2,1)S(1)}, bf16[256,1024]{1,0:T(8,128)(2,1)S(1)}, u32[]{:S(2)}, u32[]{:S(2)}) collective-permute-start(bf16[256,1024]{1,0:T(8,128)(2,1)S(1)} %get-tuple-element.11), channel_id=1, source_target_pairs={{0,32},{1,33},{2,34},{3,35},{4,36},{5,37},{6,38},{7,39},{8,40},{9,... | collective-permute-start | bytes 1572872 | tf_op jit(solution)/shard_map/ppermute | solution.py:31
  170.2 38.3 %collective-permute-start.8 = (bf16[512,512]{1,0:T(8,128)(2,1)S(1)}, bf16[512,512]{1,0:T(8,128)(2,1)S(1)}, u32[]{:S(2)}, u32[]{:S(2)}) collective-permute-start(bf16[512,512]{1,0:T(8,128)(2,1)S(1)} %convolution_convert_fusion.7), channel_id=1, source_target_pairs={{0,64},{1,65},{2,66},{3,67},{4,68},{5,69},{6,70},{7,71},{8,72},{9,... | collective-permute-start | bytes 1572872 | tf_op jit(solution)/shard_map/ppermute | solution.py:31
  172.6 45.1 %collective-permute-start.9 = (bf16[512,512]{1,0:T(8,128)(2,1)}, bf16[512,512]{1,0:T(8,128)(2,1)}, u32[]{:S(2)}, u32[]{:S(2)}) collective-permute-start(bf16[512,512]{1,0:T(8,128)(2,1)} %convolution_convert_fusion.6), channel_id=1, source_target_pairs={{0,32},{1,33},{2,34},{3,35},{4,36},{5,37},{6,38},{7,39},{8,40},{9,... | collective-permute-start | bytes 1572872 | tf_op jit(solution)/shard_map/ppermute | solution.py:31
  181.5 36.2 %collective-permute-start.10 = (bf16[512,512]{1,0:T(8,128)(2,1)}, bf16[512,512]{1,0:T(8,128)(2,1)}, u32[]{:S(2)}, u32[]{:S(2)}) collective-permute-start(bf16[512,512]{1,0:T(8,128)(2,1)} %convolution_convert_fusion.5), channel_id=1, source_target_pairs={{0,96},{1,97},{2,98},{3,99},{4,100},{5,101},{6,102},{7,103},{8,104... | collective-permute-start | bytes 1572872 | tf_op jit(solution)/shard_map/ppermute | solution.py:31
  196.8 25.6 %collective-permute-start.21 = (bf16[512,512]{1,0:T(8,128)(2,1)}, bf16[512,512]{1,0:T(8,128)(2,1)S(1)}, u32[]{:S(2)}, u32[]{:S(2)}) collective-permute-start(bf16[512,512]{1,0:T(8,128)(2,1)} %convolution_convert_fusion.3), channel_id=1, source_target_pairs={{0,16},{1,17},{2,18},{3,19},{4,20},{5,21},{6,22},{7,23},{8,24},{9,... | collective-permute-start | bytes 1572872 | tf_op jit(solution)/shard_map/ppermute | solution.py:31
  206.9 21.7 %collective-permute-start.22 = (bf16[512,512]{1,0:T(8,128)(2,1)}, bf16[512,512]{1,0:T(8,128)(2,1)}, u32[]{:S(2)}, u32[]{:S(2)}) collective-permute-start(bf16[512,512]{1,0:T(8,128)(2,1)} %convolution_convert_fusion.2), channel_id=1, source_target_pairs={{0,8},{1,9},{2,10},{3,11},{4,12},{5,13},{6,14},{7,15},{8,16},{9,17... | collective-permute-start | bytes 1572872 | tf_op jit(solution)/shard_map/ppermute | solution.py:31
  221.0 80.5 %collective-permute-start.11 = (bf16[512,512]{1,0:T(8,128)(2,1)}, bf16[512,512]{1,0:T(8,128)(2,1)S(1)}, u32[]{:S(2)}, u32[]{:S(2)}) collective-permute-start(bf16[512,512]{1,0:T(8,128)(2,1)} %add_convert_fusion.1), channel_id=1, source_target_pairs={{0,2},{1,66},{2,4},{3,68},{4,6},{5,70},{6,0},{7,64},{8,10},{9,74},... | collective-permute-start | bytes 1572872 | tf_op jit(solution)/shard_map/ppermute | solution.py:31
  231.5 70.1 %collective-permute-start.24 = (bf16[512,512]{1,0:T(8,128)(2,1)}, bf16[512,512]{1,0:T(8,128)(2,1)S(1)}, u32[]{:S(2)}, u32[]{:S(2)}) collective-permute-start(bf16[512,512]{1,0:T(8,128)(2,1)} %add_convert_fusion), channel_id=1, source_target_pairs={{0,2},{1,67},{2,4},{3,69},{4,6},{5,71},{6,0},{7,65},{8,10},{9,75},... | collective-permute-start | bytes 1572872 | tf_op jit(solution)/shard_map/ppermute | solution.py:31
  273.9 27.1 %collective-permute-start.12 = (bf16[256,512]{1,0:T(8,128)(2,1)S(1)}, bf16[256,512]{1,0:T(8,128)(2,1)S(1)}, u32[]{:S(2)}, u32[]{:S(2)}) collective-permute-start(bf16[256,512]{1,0:T(8,128)(2,1)S(1)} %constant_dynamic-slice_fusion.6), channel_id=1, source_target_pairs={{0,1},{2,3},{4,5},{6,7},{8,9},{10,11},{12,13},{14,15},{16,17},{18,... | collective-permute-start | bytes 786440 | tf_op jit(solution)/shard_map/ppermute | solution.py:31
  (30 other events, 341.7 us)
Sparse Core Ops, SparseCore 0:
  128.0 144.8 all-reduce.2

commit v2 on v1

v2 whole, which is shorter than its diff:
```python
import itertools
import math

import jax
import jax.numpy as jnp
from jax import lax
from jax.experimental import pallas as pl
from jax.experimental.pallas import tpu as pltpu
from jax.sharding import PartitionSpec as P

D = 8192
HEAD = 128
BLOCK = 8
RING = 4
SECTIONS = 4

EPSILON = 1e-05
ROPE_BASE = 500000.0

AXES = ("dp", "pipe", "tensor")


def moved(block, rule):
    route = []
    for x, z, s, t in itertools.product(range(RING), range(RING), range(SECTIONS), range(2)):
        target = rule(x, z, s, t)
        if target is not None:
            a, b, c, d = target
            there = ((a % RING * RING + b % RING) * SECTIONS + c % SECTIONS) * 2 + d % 2
            route.append((((x * RING + z) * SECTIONS + s) * 2 + t, there))
    return lax.ppermute(block, AXES, route)


def both_sides(squares):
    return squares + moved(squares, lambda x, z, s, t: (x, z, s, 1 - t))


def frequencies():
    index_half = jnp.arange(HEAD // 2, dtype=jnp.float32)
    return jnp.exp(-(2.0 * index_half / HEAD) * math.log(ROPE_BASE))


def angles_of(position):
    angles = position.astype(jnp.float32)[:, None] * jnp.tile(frequencies(), 2)[None, :]
    sign = jnp.where(jnp.arange(HEAD) < HEAD // 2, 1.0, -1.0)
    return jnp.cos(angles), jnp.sin(angles) * sign


def derotate_kernel(key, value, cosine, sine, out):
    width = key.shape[1]
    for start in range(0, width, HEAD):
        head = key[:, start : start + HEAD].astype(jnp.float32)
        swapped = pltpu.roll(head, HEAD // 2, 1)
        out[:, start : start + HEAD] = (head * cosine[...] + swapped * sine[...]).astype(out.dtype)
    out[:, width:] = value[...]


def derotate(key, value, position):
    cosine, sine = angles_of(position)
    return pl.pallas_call(
        derotate_kernel,
        out_shape=jax.ShapeDtypeStruct((key.shape[0], 2 * key.shape[1]), jnp.bfloat16),
    )(key, value, cosine, sine)


def slot_selection(plan_row, owner, capacity_blocks, rows):
    block_count = plan_row.shape[0]
    block_ids = jnp.arange(block_count, dtype=jnp.int32)
    same_owner = plan_row[:, None] == plan_row[None, :]
    earlier = block_ids[None, :] < block_ids[:, None]
    block_rank = jnp.sum(jnp.where(same_owner & earlier, 1, 0), axis=1).astype(jnp.int32)
    slot_of_block = jnp.where(plan_row == owner, block_rank, -1)
    slot_of_row = jnp.repeat(slot_of_block, BLOCK) * BLOCK + jnp.tile(
        jnp.arange(BLOCK, dtype=jnp.int32), block_count
    )
    slot_of_row = jnp.where(jnp.repeat(slot_of_block, BLOCK) < 0, -1, slot_of_row)
    slot_ids = jnp.arange(capacity_blocks * BLOCK, dtype=jnp.int32)
    return (slot_ids[:, None] == slot_of_row[None, :]).astype(jnp.float32)


NT = (((1,), (1,)), ((), ()))
TN = (((0,), (0,)), ((), ()))
TILE = 1024


def feature_kernel(half, cots, scale, w_key, w_value, across, straight):
    rows, width = cots.shape[0], w_key.shape[1]
    tiles = D // 2 // TILE

    def step(key_tile, value_tile, out):
        total = lax.dot_general(
            cots[:, :width], key_tile[...], NT, preferred_element_type=jnp.float32
        )
        total = total + lax.dot_general(
            cots[:, width:], value_tile[...], NT, preferred_element_type=jnp.float32
        )
        out[...] = (total * scale[...]).astype(out.dtype)

    for side, out in ((1 - half[0], across), (half[0], straight)):
        weights = pl.BlockSpec((TILE, width), lambda i, side=side: (side * tiles + i, 0))
        pltpu.emit_pipeline(
            step,
            grid=(tiles,),
            in_specs=[weights, weights],
            out_specs=[pl.BlockSpec((rows, TILE), lambda i: (0, i))],
        )(w_key, w_value, out)


def feature_halves(cots, scale, w_key, w_value, half):
    rows = cots.shape[0]
    result = jax.ShapeDtypeStruct((rows, D // 2), jnp.bfloat16)
    return pl.pallas_call(
        feature_kernel,
        out_shape=(result, result),
        in_specs=[
            pl.BlockSpec(memory_space=pltpu.SMEM),
            pl.BlockSpec(memory_space=pltpu.VMEM),
            pl.BlockSpec(memory_space=pltpu.VMEM),
            pl.BlockSpec(memory_space=pltpu.HBM),
            pl.BlockSpec(memory_space=pltpu.HBM),
        ],
        out_specs=(pl.BlockSpec(memory_space=pltpu.HBM), pl.BlockSpec(memory_space=pltpu.HBM)),
        compiler_params=pltpu.CompilerParams(vmem_limit_bytes=32 * 1024 * 1024),
    )(
        jnp.reshape(half, (1,)),
        cots,
        scale,
        pltpu.with_memory_space_constraint(w_key, pltpu.HBM),
        pltpu.with_memory_space_constraint(w_value, pltpu.HBM),
    )


def on_device(
    stream,
    backup_stream,
    norm_gain,
    w_key,
    w_value,
    key_cot,
    value_cot,
    backup_key_cot,
    backup_value_cot,
    positions,
    failed,
    reroute_plan,
):
    section = lax.axis_index("pipe")
    member = lax.axis_index("dp")
    side = lax.axis_index("tensor")
    replicas = lax.axis_size("dp")
    at_x, at_z = member // RING, member % RING
    fallen = failed[section]
    plan_row = reroute_plan[section]
    rows = stream.shape[1]
    capacity_blocks = 2 * ((plan_row.shape[0] + replicas - 2) // (replicas - 1))
    width = w_key.shape[2]

    dead_stream, dead_key, dead_value = lax.psum(
        (backup_stream[0], backup_key_cot[0], backup_value_cot[0]), "dp"
    )

    values = stream[0].astype(jnp.float32)
    squares = both_sides(jnp.sum(values * values, axis=1))
    own_scale = lax.rsqrt(squares / D + EPSILON)[:, None]
    normed = (values * own_scale * norm_gain).astype(jnp.bfloat16)

    own_positions = lax.dynamic_slice_in_dim(positions[0], member * rows, rows, 0)
    cots = derotate(key_cot[0], value_cot[0], own_positions)
    near = moved(cots, lambda x, z, s, t: (x, z, s - 1, t))
    far = moved(cots, lambda x, z, s, t: (x, z, s - 1, 1 - t))

    late_cots, normed = lax.optimization_barrier((cots, normed))
    ones = jnp.ones((rows, 1), jnp.float32)
    across, straight = feature_halves(late_cots, ones, w_key[0], w_value[0], side)
    across = moved(across, lambda x, z, s, t: (x, z, s - 1, 1 - t))
    straight = moved(straight, lambda x, z, s, t: (x, z, s - 1, t))
    feature = straight.astype(jnp.float32) + across.astype(jnp.float32)
    stream_grad = (own_scale * (norm_gain * feature)).astype(jnp.bfloat16)

    fourth = normed.shape[1] // RING
    block = fourth // 2
    first = side == 0
    key_heads = [
        jnp.where(first, near[:, :width], far[:, :width]),
        jnp.where(first, far[:, :width], near[:, :width]),
    ]
    outgoing = jnp.stack(
        [
            jnp.concatenate(
                [normed[:, z * block : (z + 1) * block], normed[:, (RING + z) * block : (RING + z + 1) * block]]
                + key_heads,
                axis=1,
            )
            for z in range(RING)
        ]
    )
    z_rings = [[RING * x + z for z in range(RING)] for x in range(RING)]
    x_rings = [[RING * x + z for x in range(RING)] for z in range(RING)]
    arrived = lax.all_to_all(outgoing, "dp", 0, 0, axis_index_groups=z_rings)
    arrived = arrived.reshape(RING * rows, 2 * fourth)

    def product(lhs, rhs):
        return lax.dot_general(lhs, rhs, TN, preferred_element_type=jnp.float32).astype(jnp.bfloat16)

    parts = jnp.stack(
        [
            product(
                arrived[:, half * block : (half + 1) * block],
                arrived[:, fourth + head * width : fourth + (head + 1) * width],
            )
            for head in range(2)
            for half in range(2)
        ]
    )
    parts = lax.all_to_all(parts, "dp", 0, 0, axis_index_groups=x_rings)
    grad_key = jnp.sum(parts.astype(jnp.float32), axis=0).astype(jnp.bfloat16)
    grad_key = moved(grad_key, lambda x, z, s, t: (2 * t + x % 2, z, s + 1, x // 2))

    gathered = []
    for step in (2, 1, 3, 0):
        there = (at_x + step) % RING
        start = (2 * (there % 2) + there // 2) * fourth
        piece = jnp.concatenate(
            [lax.dynamic_slice_in_dim(normed, start, fourth, 1), near[:, width:], far[:, width:]],
            axis=1,
        )
        if step:
            piece = moved(piece, lambda x, z, s, t, step=step: (x + step, z, s, t))
        gathered.append(piece)
    gathered = jnp.concatenate(gathered, axis=0)
    dead_stream, dead_key, dead_value, gathered = lax.optimization_barrier(
        (dead_stream, dead_key, dead_value, gathered)
    )

    total = None
    for step in (2, 1, 3, 0):
        there = (at_z + step) % RING
        half, head = there % 2, (there // 2) ^ (at_x // 2)
        part = product(
            lax.dynamic_slice_in_dim(gathered, half * block, block, 1),
            lax.dynamic_slice_in_dim(gathered, fourth + head * width, width, 1),
        )
        if step:
            part = moved(part, lambda x, z, s, t, step=step: (x, z + step, s, t))
        part = part.astype(jnp.float32)
        total = part if total is None else total + part
    grad_value = moved(
        total.astype(jnp.bfloat16),
        lambda x, z, s, t: (2 * t + x % 2, 2 * (x // 2) + z % 2, s + 1, t ^ (z // 2) ^ (x // 2)),
    )

    dead_values = dead_stream.astype(jnp.float32)
    dead_squares = both_sides(jnp.sum(dead_values * dead_values, axis=1))
    dead_scale = lax.rsqrt(dead_squares / D + EPSILON)[:, None]
    dead_positions = lax.dynamic_slice_in_dim(positions[0], fallen * rows, rows, 0)
    dead_cots = derotate(dead_key, dead_value, dead_positions)

    home = member // (replicas // 2)
    start = (member % (replicas // 2)) * block
    dead_block = (
        lax.dynamic_slice_in_dim(dead_stream, start, block, 1).astype(jnp.float32)
        * dead_scale
        * lax.dynamic_slice_in_dim(norm_gain, start, block, 0)
    ).astype(jnp.bfloat16)
    lent = moved(dead_block, lambda x, z, s, t: (x, z, s, 1 - t) if t == x // 2 else None)
    dead_block = jnp.where(home == side, dead_block, lent)
    dead_part = lax.dot_general(dead_block, dead_cots, TN, preferred_element_type=jnp.float32)
    grad_key = grad_key.astype(jnp.float32) + dead_part[:, :width]
    grad_value = grad_value.astype(jnp.float32) + dead_part[:, width:]

    selection = slot_selection(plan_row, member, capacity_blocks, rows)
    slot_cots = jnp.dot(
        selection.astype(jnp.bfloat16), dead_cots, preferred_element_type=jnp.float32
    ).astype(jnp.bfloat16)
    slot_scale = jnp.sum(selection * jnp.reshape(dead_scale, (1, rows)), axis=1, keepdims=True)
    across, straight = feature_halves(slot_cots, slot_scale, w_key[0], w_value[0], side)
    across = moved(across, lambda x, z, s, t: (x, z, s - 1, 1 - t))
    straight = moved(straight, lambda x, z, s, t: (x, z, s - 1, t))
    feature = straight.astype(jnp.float32) + across.astype(jnp.float32)
    spill_grad = (norm_gain * feature).astype(jnp.bfloat16)

    return grad_key[None], grad_value[None], stream_grad[None], spill_grad[None]


def solution(mesh):
    return jax.shard_map(
        on_device,
        mesh=mesh,
        in_specs=(
            P("pipe", "dp", "tensor"),
            P("pipe", "dp", "tensor"),
            P("tensor"),
            P("pipe", None, "tensor"),
            P("pipe", None, "tensor"),
            P("pipe", "dp", "tensor"),
            P("pipe", "dp", "tensor"),
            P("pipe", "dp", "tensor"),
            P("pipe", "dp", "tensor"),
            P("pipe", None),
            P(),
            P(),
        ),
        out_specs=(
            P("pipe", "dp", "tensor"),
            P("pipe", "dp", "tensor"),
            P("pipe", "dp", "tensor"),
            P("pipe", "dp", "tensor"),
        ),
        check_vma=False,
    )
```

time: 322 us -> 285 us (0.89)
  local copies, waits for them, and re-layouts: 50.8 us -> 3.16 us
  blocking collectives: 36 us -> 0 us
  other arithmetic: 19.4 us -> 46.3 us
  Pallas kernels: 12.9 us -> 27.7 us
  starting transfers between devices: 49.5 us -> 37.9 us
  waiting for transfers between devices: 118 us -> 129 us
  matrix products: 16.5 us -> 24.4 us
    psum x1 -> x0, blocking collectives: 36 us -> none  [on_device(): scales = lax.rsqrt(lax.psum(squares, 'tensor') / D + EPSILON)]
    unnamed x53 -> x12, local copies, waits for them, and re-layouts: 33.8 us -> 0.03 us
    ppermute x29 -> x17, starting transfers between devices: 49.4 us -> 29.3 us  [moved(): return lax.ppermute(block, AXES, route)]
    concatenate x7 -> x2, other arithmetic: 5.69 us -> 20.8 us  [the longest x1 17.5 us: on_device(): gathered = jnp.concatenate(gathered, axis=0)]
    pallas_call x4, Pallas kernels: 12.9 us -> 27.7 us  [the longest x2 23.5 us: feature_halves(): pl.pallas_call(feature_kernel, out_shape=(result, result), in_specs=[pl.B...]
    convert_element_type x3 -> x0, local copies, waits for them, and re-layouts: 11.5 us -> none  [the longest x2 11.4 us: on_device(): values = stream[0].astype(jnp.float32)]
    ppermute x29 -> x17, waiting for transfers between devices: 76.1 us -> 86.2 us  [moved(): return lax.ppermute(block, AXES, route)]
    all_to_all x0 -> x2, starting transfers between devices: none -> 8.63 us  [the longest x1 5.02 us: on_device(): arrived = lax.all_to_all(outgoing, 'dp', 0, 0, axis_index_groups=z_rings)]
  transfers between devices with their start and end apart: 30 -> 20, of which waited for: 11 -> 5; matrix products, arithmetic and copies ran while one was open for 16% -> 23% of each run, Pallas kernels for 4% -> 9%
where the time goes in v2:
time: 285 us; the launch traced here: 284 us
  waiting for transfers between devices  129 us (45%)
  other arithmetic  46.3 us (16%)
  starting transfers between devices  37.9 us (13%)
  Pallas kernels  27.7 us (10%)
  matrix products  24.4 us (9%)
  between operations  15.2 us (5%)
  local copies, waits for them, and re-layouts  3.16 us (1%)
    ppermute x17, waiting for transfers between devices, moved(): return lax.ppermute(block, AXES, route)  86.2 us
    psum x1, waiting for transfers between devices, on_device(): lax.psum((backup_stream[0], backup_key_cot[0], backup_value_cot[0]), 'dp')  43.2 us
    ppermute x17, starting transfers between devices, moved(): return lax.ppermute(block, AXES, route)  29.3 us
    pallas_call x2, Pallas kernels, feature_halves(): pl.pallas_call(feature_kernel, out_shape=(result, result), in_specs=[pl.B...  23.5 us
    dot_general x8, matrix products, product(): lax.dot_general(lhs, rhs, TN, preferred_element_type=jnp.float32)  21.3 us
    concatenate x1, other arithmetic, on_device(): gathered = jnp.concatenate(gathered, axis=0)  17.5 us
  transfers between devices with their start and end apart: 20, of which 5 were waited for; matrix products, arithmetic and copies ran while one was open for 23% of the time, Pallas kernels for 9%

profile of v2, /device:TPU:25, one launch (start us, length us, event | category | flops | bytes accessed | tf_op | source)
XLA Modules:
  0.0 284.1 jit_solution(13489251303177895417)
XLA Ops:
  19.6 8.9 %collective-permute-done = f32[256]{0:T(256)S(1)} collective-permute-done((f32[256]{0:T(256)S(1)}, f32[256]{0:T(256)S(1)}, u32[]{:S(2)}, u32[]{:S(2)}) %collective-permute-start) | collective-permute-done | bytes 1056 | tf_op jit(solution)/shard_map/ppermute | solution.py:31
  29.3 12.3 %shard_map.149 = (bf16[256,4096]{1,0:T(8,128)(2,1)S(1)}, bf16[256,4096]{1,0:T(8,128)(2,1)}) custom-call(s32[1]{0:T(128)} %bitcast.21.half, bf16[256,1024]{1,0:T(8,128)(2,1)S(1)} %copy-done, f32[256,1]{1,0:T(8,128)S(1)} %broadcast_in_dim.68.scale, bf16[8192,512]{1,0:T(8,128)(2,1)} %bitcast.49, bf16[8192,512]{1,0:T(8,128)(2,1)} %bitcast.51), custom_call_target="tpu_custom_call" | custom-call | tf_op jit(solution)/shard_map/pallas_call | solution.py:112
  47.7 2.3 pad_maximum_fusion
  49.9 5.0 %all-to-all-start = ((bf16[4,256,2048]{2,1,0:T(8,128)(2,1)}), bf16[4,256,2048]{2,1,0:T(8,128)(2,1)}, u32[]{:S(2)}, u32[]{:S(2)}) async-start(bf16[4,256,2048]{2,1,0:T(8,128)(2,1)} %pad_maximum_fusion), calls=%async_computation | async-start | bytes 8388608 | tf_op jit(solution)/shard_map/all_to_all | solution.py:199
  55.0 3.3 %pad_maximum_fusion.12 = (bf16[256,2048]{1,0:T(8,128)(2,1)}, bf16[256,2048]{1,0:T(8,128)(2,1)}, bf16[256,2048]{1,0:T(8,128)(2,1)}) fusion(bf16[256,512]{1,0:T(8,128)(2,1)S(1)} %get-tuple-element.48, bf16[256,512]{1,0:T(8,128)(2,1)S(1)} %get-tuple-element.47, bf16[256,1024]{1,0:T(8,128)(2,1)} %get-tuple-element.37, bf16[256,1024]{1,0:T(8,128)(2,1)} %get-tuple-element.40, ...), kind=kLoop, calls=%fused_computation.21 | loop fusion | flops 7340032 | bytes 5242880 | tf_op jit(solution)/shard_map/concatenate | solution.py:223
  58.3 2.7 collective-permute-start.4
  61.3 2.4 collective-permute-start.6
  64.5 25.9 %collective-permute-done.4 = bf16[256,2048]{1,0:T(8,128)(2,1)} collective-permute-done((bf16[256,2048]{1,0:T(8,128)(2,1)}, bf16[256,2048]{1,0:T(8,128)(2,1)}, u32[]{:S(2)}, u32[]{:S(2)}) %collective-permute-start.4) | collective-permute-done | bytes 1048608 | tf_op jit(solution)/shard_map/ppermute | solution.py:31
  90.4 27.9 %collective-permute-done.5 = bf16[256,2048]{1,0:T(8,128)(2,1)} collective-permute-done((bf16[256,2048]{1,0:T(8,128)(2,1)}, bf16[256,2048]{1,0:T(8,128)(2,1)}, u32[]{:S(2)}, u32[]{:S(2)}) %collective-permute-start.5) | collective-permute-done | bytes 1048608 | tf_op jit(solution)/shard_map/ppermute | solution.py:31
  118.3 17.5 %maximum_maximum_fusion = bf16[1024,2048]{1,0:T(8,128)(2,1)} fusion(bf16[256,512]{1,0:T(8,128)(2,1)S(1)} %get-tuple-element.48, bf16[256,512]{1,0:T(8,128)(2,1)S(1)} %get-tuple-element.47, bf16[256,1024]{1,0:T(8,128)(2,1)S(1)} %get-tuple-element.38, bf16[256,2048]{1,0:T(8,128)(2,1)} %collective-permute-done.6, bf16[256,2048]{1,0:T(8,128)(2,1)} %collective-permute-done.5, ...), kind=kLoop, calls=%fused_computation.6 | loop fusion | flops 25165824 | bytes 8388608 | tf_op jit(solution)/shard_map/concatenate | solution.py:230
  135.8 4.6 %fusion.3 = bf16[1,256,4096]{2,1,0:T(8,128)(2,1)} fusion(bf16[256,4096]{1,0:T(8,128)(2,1)} %collective-permute-done.14, bf16[256,4096]{1,0:T(8,128)(2,1)} %collective-permute-done.13, f32[4096]{0:T(1024)S(1)} %copy-done.4, f32[256]{0:T(256)S(1)} %add_rsqrt_fusion.1), kind=kLoop, calls=%fused_computation.9 | loop fusion | flops 6291456 | bytes 6308864 | tf_op jit(solution)/shard_map/broadcast_in_dim | solution.py:282
  140.4 43.2 %all-reduce.3.cloned.1.call-done = (bf16[256,4096]{1,0:T(8,128)(2,1)}, bf16[256,512]{1,0:T(8,128)(2,1)}, bf16[256,512]{1,0:T(8,128)(2,1)}) async-done(((bf16[256,4096]{1,0:T(8,128)(2,1)}, bf16[256,512]{1,0:T(8,128)(2,1)}, bf16[256,512]{1,0:T(8,128)(2,1)}), (bf16[256,4096]{1,0:T(8,128)(2,1)}, bf16[256,512]{1,0:T(8,128)(2,1)}, bf16[256,512]{1,0:T(8,128)(2,1)})) %all-reduce.3.cloned.1.call-update) | async-done | bytes 2621456 | tf_op jit(solution)/shard_map/psum | solution.py:158
  186.9 3.1 %convolution_convert_fusion.3 = bf16[512,512]{1,0:T(8,128)(2,1)} fusion(bf16[1024,2048]{1,0:T(8,128)(2,1)} %maximum_maximum_fusion, s32[]{:T(128)S(6)} %select_n.245, s32[]{:T(128)S(6)} %select_n.242), kind=kOutput, calls=%fused_computation.29 | convolution fusion | flops 537133056 | bytes 2621448 | tf_op jit(solution)/shard_map/dot_general | solution.py:203
  201.9 3.6 %all-to-all-start.1 = ((bf16[4,512,512]{2,1,0:T(8,128)(2,1)}), bf16[4,512,512]{2,1,0:T(8,128)(2,1)S(1)}, u32[]{:S(2)}, u32[]{:S(2)}) async-start(bf16[4,512,512]{2,1,0:T(8,128)(2,1)} %pad_maximum_fusion.1), calls=%async_computation.1 | async-start | bytes 4194304 | tf_op jit(solution)/shard_map/all_to_all | solution.py:215
  205.5 3.1 %convolution_convert_fusion.1 = bf16[512,512]{1,0:T(8,128)(2,1)} fusion(bf16[1024,2048]{1,0:T(8,128)(2,1)} %maximum_maximum_fusion, s32[]{:T(128)S(6)} %select_n.255, s32[]{:T(128)S(6)} %select_n.253), kind=kOutput, calls=%fused_computation.27 | convolution fusion | flops 537133056 | bytes 2621448 | tf_op jit(solution)/shard_map/dot_general | solution.py:203
  209.6 3.1 %convolution_convert_fusion.2 = bf16[512,512]{1,0:T(8,128)(2,1)} fusion(bf16[1024,2048]{1,0:T(8,128)(2,1)} %maximum_maximum_fusion, s32[]{:T(128)S(6)} %select_n.250, s32[]{:T(128)S(6)} %select_n.248), kind=kOutput, calls=%fused_computation.28 | convolution fusion | flops 537133056 | bytes 2621448 | tf_op jit(solution)/shard_map/dot_general | solution.py:203
  219.1 11.3 %shard_map.150 = (bf16[48,4096]{1,0:T(8,128)(2,1)S(1)}, bf16[48,4096]{1,0:T(8,128)(2,1)S(1)}) custom-call(s32[1]{0:T(128)} %bitcast.21.half, bf16[48,1024]{1,0:T(8,128)(2,1)S(1)} %convolution_convert_fusion.8.cots, f32[48,1]{1,0:T(8,128)S(1)} %copy.18.scale, bf16[8192,512]{1,0:T(8,128)(2,1)} %bitcast.50, bf16[8192,512]{1,0:T(8,128)(2,1)} %bitcast.52), custom_call_target="tpu_custom_call" | custom-call | tf_op jit(solution)/shard_map/pallas_call | solution.py:112
  230.4 2.5 collective-permute-start.15
  232.9 3.9 %collective-permute-start.16 = (bf16[48,4096]{1,0:T(8,128)(2,1)S(1)}, bf16[48,4096]{1,0:T(8,128)(2,1)}, u32[]{:S(2)}, u32[]{:S(2)}) collective-permute-start(bf16[48,4096]{1,0:T(8,128)(2,1)S(1)} %get-tuple-element.23), channel_id=1, source_target_pairs={{0,7},{1,6},{2,1},{3,0},{4,3},{5,2},{6,5},{7,4},{8,15},{9,14},{10,... | collective-permute-start | bytes 1179656 | tf_op jit(solution)/shard_map/ppermute | solution.py:31
  238.6 2.9 %add_convert_fusion = bf16[512,512]{1,0:T(8,128)(2,1)} fusion(bf16[512,512]{1,0:T(8,128)(2,1)} %collective-permute-done.11, bf16[512,512]{1,0:T(8,128)(2,1)} %collective-permute-done.10, bf16[512,512]{1,0:T(8,128)(2,1)} %collective-permute-done.9, bf16[1024,2048]{1,0:T(8,128)(2,1)S(1)} %copy-done.3, s32[]{:T(128)S(6)} %select_n.260, s32[]{:T(128)S(6)} %select_n.258), kind=kOutput, calls=%fused_computation.47 | convolution fusion | flops 539230208 | bytes 4194312 | tf_op jit(solution)/shard_map/dot_general | solution.py:203
  241.5 2.4 collective-permute-start.12
  245.2 3.5 %collective-permute-start.3 = (bf16[512,512]{1,0:T(8,128)(2,1)}, bf16[512,512]{1,0:T(8,128)(2,1)S(1)}, u32[]{:S(2)}, u32[]{:S(2)}) collective-permute-start(bf16[512,512]{1,0:T(8,128)(2,1)} %reduce_sum.49), channel_id=1, source_target_pairs={{0,2},{1,66},{2,4},{3,68},{4,6},{5,70},{6,0},{7,64},{8,10},{9,74},... | collective-permute-start | bytes 1572872 | tf_op jit(solution)/shard_map/ppermute | solution.py:31
  250.6 23.4 %collective-permute-done.12 = bf16[512,512]{1,0:T(8,128)(2,1)S(1)} collective-permute-done((bf16[512,512]{1,0:T(8,128)(2,1)}, bf16[512,512]{1,0:T(8,128)(2,1)S(1)}, u32[]{:S(2)}, u32[]{:S(2)}) %collective-permute-start.12) | collective-permute-done | bytes 524320 | tf_op jit(solution)/shard_map/ppermute | solution.py:31
  274.1 3.2 %fusion.13 = (f32[1,512,512]{2,1,0:T(8,128)}, f32[1,512,512]{2,1,0:T(8,128)}) fusion(f32[512,1024]{1,0:T(8,128)} %fusion.32, bf16[512,512]{1,0:T(8,128)(2,1)S(1)} %collective-permute-done.12, bf16[512,512]{1,0:T(8,128)(2,1)S(1)} %collective-permute-done.3), kind=kLoop, calls=%fused_computation.44 | loop fusion | flops 1048576 | bytes 5242880 | tf_op jit(solution)/shard_map/broadcast_in_dim | solution.py:282
  (78 shorter events, 47.0 us)
Async XLA Ops:
  7.2 21.4 %copy-start.1 = (bf16[1,256,4096]{2,1,0:T(8,128)(2,1)S(1)}, bf16[1,256,4096]{2,1,0:T(8,128)(2,1)}, u32[]{:S(2)}) copy-start(bf16[1,256,4096]{2,1,0:T(8,128)(2,1)} %param.12) | copy-start | bytes 6291460
  7.2 21.4 %copy-start.4 = (f32[4096]{0:T(1024)S(1)}, f32[4096]{0:T(1024)}, u32[]{:S(2)}) copy-start(f32[4096]{0:T(1024)} %param.14) | copy-start | bytes 49156
  13.9 31.8 %collective-permute-start.2 = (bf16[256,1024]{1,0:T(8,128)(2,1)}, bf16[256,1024]{1,0:T(8,128)(2,1)}, u32[]{:S(2)}, u32[]{:S(2)}) collective-permute-start(bf16[256,1024]{1,0:T(8,128)(2,1)} %shard_map.147.cots), channel_id=1, source_target_pairs={{0,7},{1,6},{2,1},{3,0},{4,3},{5,2},{6,5},{7,4},{8,15},{9,14},{10,... | collective-permute-start | bytes 1572872 | tf_op jit(solution)/shard_map/ppermute | solution.py:31
  15.4 30.3 %collective-permute-start.1 = (bf16[256,1024]{1,0:T(8,128)(2,1)}, bf16[256,1024]{1,0:T(8,128)(2,1)}, u32[]{:S(2)}, u32[]{:S(2)}) collective-permute-start(bf16[256,1024]{1,0:T(8,128)(2,1)} %shard_map.147.cots), channel_id=1, source_target_pairs={{0,6},{1,7},{2,0},{3,1},{4,2},{5,3},{6,4},{7,5},{8,14},{9,15},{10,... | collective-permute-start | bytes 1572872 | tf_op jit(solution)/shard_map/ppermute | solution.py:31
  17.5 11.0 %collective-permute-start = (f32[256]{0:T(256)S(1)}, f32[256]{0:T(256)S(1)}, u32[]{:S(2)}, u32[]{:S(2)}) collective-permute-start(f32[256]{0:T(256)S(1)} %fusion), channel_id=1, source_target_pairs={{0,1},{1,0},{2,3},{3,2},{4,5},{5,4},{6,7},{7,6},{8,9},{9,8},{10,11... | collective-permute-start | bytes 3080 | tf_op jit(solution)/shard_map/ppermute | solution.py:31
  41.5 94.3 %collective-permute-start.13 = (bf16[256,4096]{1,0:T(8,128)(2,1)}, bf16[256,4096]{1,0:T(8,128)(2,1)}, u32[]{:S(2)}, u32[]{:S(2)}) collective-permute-start(bf16[256,4096]{1,0:T(8,128)(2,1)} %get-tuple-element.20), channel_id=1, source_target_pairs={{0,6},{1,7},{2,0},{3,1},{4,2},{5,3},{6,4},{7,5},{8,14},{9,15},{10,... | collective-permute-start | bytes 6291464 | tf_op jit(solution)/shard_map/ppermute | solution.py:31
  43.6 92.2 %collective-permute-start.14 = (bf16[256,4096]{1,0:T(8,128)(2,1)S(1)}, bf16[256,4096]{1,0:T(8,128)(2,1)}, u32[]{:S(2)}, u32[]{:S(2)}) collective-permute-start(bf16[256,4096]{1,0:T(8,128)(2,1)S(1)} %get-tuple-element.21), channel_id=1, source_target_pairs={{0,7},{1,6},{2,1},{3,0},{4,3},{5,2},{6,5},{7,4},{8,15},{9,14},{10,... | collective-permute-start | bytes 6291464 | tf_op jit(solution)/shard_map/ppermute | solution.py:31
  49.9 141.2 %all-to-all-start = ((bf16[4,256,2048]{2,1,0:T(8,128)(2,1)}), bf16[4,256,2048]{2,1,0:T(8,128)(2,1)}, u32[]{:S(2)}, u32[]{:S(2)}) async-start(bf16[4,256,2048]{2,1,0:T(8,128)(2,1)} %pad_maximum_fusion), calls=%async_computation | async-start | bytes 8388608 | tf_op jit(solution)/shard_map/all_to_all | solution.py:199
  55.0 128.6 %all-reduce.3.cloned.1.call-start = ((), (), s32[]{:S(2)}) async-start(), calls=%async_computation.2 | async-start | bytes 5242880 | tf_op jit(solution)/shard_map/psum | solution.py:158
  58.3 32.1 %collective-permute-start.4 = (bf16[256,2048]{1,0:T(8,128)(2,1)}, bf16[256,2048]{1,0:T(8,128)(2,1)}, u32[]{:S(2)}, u32[]{:S(2)}) collective-permute-start(bf16[256,2048]{1,0:T(8,128)(2,1)} %get-tuple-element.49), channel_id=1, source_target_pairs={{0,64},{1,65},{2,66},{3,67},{4,68},{5,69},{6,70},{7,71},{8,72},{9,... | collective-permute-start | bytes 3145736 | tf_op jit(solution)/shard_map/ppermute | solution.py:31
  61.0 57.3 %collective-permute-start.5 = (bf16[256,2048]{1,0:T(8,128)(2,1)}, bf16[256,2048]{1,0:T(8,128)(2,1)}, u32[]{:S(2)}, u32[]{:S(2)}) collective-permute-start(bf16[256,2048]{1,0:T(8,128)(2,1)} %get-tuple-element.50), channel_id=1, source_target_pairs={{0,32},{1,33},{2,34},{3,35},{4,36},{5,37},{6,38},{7,39},{8,40},{9,... | collective-permute-start | bytes 3145736 | tf_op jit(solution)/shard_map/ppermute | solution.py:31
  61.3 57.0 %collective-permute-start.6 = (bf16[256,2048]{1,0:T(8,128)(2,1)}, bf16[256,2048]{1,0:T(8,128)(2,1)}, u32[]{:S(2)}, u32[]{:S(2)}) collective-permute-start(bf16[256,2048]{1,0:T(8,128)(2,1)} %get-tuple-element.51), channel_id=1, source_target_pairs={{0,96},{1,97},{2,98},{3,99},{4,100},{5,101},{6,102},{7,103},{8,104... | collective-permute-start | bytes 3145736 | tf_op jit(solution)/shard_map/ppermute | solution.py:31
  185.7 29.6 %collective-permute-start.7 = (f32[256]{0:T(256)S(1)}, f32[256]{0:T(256)S(1)}, u32[]{:S(2)}, u32[]{:S(2)}) collective-permute-start(f32[256]{0:T(256)S(1)} %multiply_reduce_fusion), channel_id=1, source_target_pairs={{0,1},{1,0},{2,3},{3,2},{4,5},{5,4},{6,7},{7,6},{8,9},{9,8},{10,11... | collective-permute-start | bytes 3080 | tf_op jit(solution)/shard_map/ppermute | solution.py:31
  189.9 48.6 %collective-permute-start.9 = (bf16[512,512]{1,0:T(8,128)(2,1)}, bf16[512,512]{1,0:T(8,128)(2,1)}, u32[]{:S(2)}, u32[]{:S(2)}) collective-permute-start(bf16[512,512]{1,0:T(8,128)(2,1)} %convolution_convert_fusion.3), channel_id=1, source_target_pairs={{0,16},{1,17},{2,18},{3,19},{4,20},{5,21},{6,22},{7,23},{8,24},{9,... | collective-permute-start | bytes 1572872 | tf_op jit(solution)/shard_map/ppermute | solution.py:31
  201.9 42.0 %all-to-all-start.1 = ((bf16[4,512,512]{2,1,0:T(8,128)(2,1)}), bf16[4,512,512]{2,1,0:T(8,128)(2,1)S(1)}, u32[]{:S(2)}, u32[]{:S(2)}) async-start(bf16[4,512,512]{2,1,0:T(8,128)(2,1)} %pad_maximum_fusion.1), calls=%async_computation.1 | async-start | bytes 4194304 | tf_op jit(solution)/shard_map/all_to_all | solution.py:215
  208.6 30.0 %collective-permute-start.11 = (bf16[512,512]{1,0:T(8,128)(2,1)}, bf16[512,512]{1,0:T(8,128)(2,1)}, u32[]{:S(2)}, u32[]{:S(2)}) collective-permute-start(bf16[512,512]{1,0:T(8,128)(2,1)} %convolution_convert_fusion.1), channel_id=1, source_target_pairs={{0,24},{1,25},{2,26},{3,27},{4,28},{5,29},{6,30},{7,31},{8,0},{9,1... | collective-permute-start | bytes 1572872 | tf_op jit(solution)/shard_map/ppermute | solution.py:31
  212.7 25.9 %collective-permute-start.10 = (bf16[512,512]{1,0:T(8,128)(2,1)}, bf16[512,512]{1,0:T(8,128)(2,1)}, u32[]{:S(2)}, u32[]{:S(2)}) collective-permute-start(bf16[512,512]{1,0:T(8,128)(2,1)} %convolution_convert_fusion.2), channel_id=1, source_target_pairs={{0,8},{1,9},{2,10},{3,11},{4,12},{5,13},{6,14},{7,15},{8,16},{9,17... | collective-permute-start | bytes 1572872 | tf_op jit(solution)/shard_map/ppermute | solution.py:31
  216.3 16.5 %collective-permute-start.8 = (bf16[256,512]{1,0:T(8,128)(2,1)S(1)}, bf16[256,512]{1,0:T(8,128)(2,1)S(1)}, u32[]{:S(2)}, u32[]{:S(2)}) collective-permute-start(bf16[256,512]{1,0:T(8,128)(2,1)S(1)} %multiply_convert_fusion.2), channel_id=1, source_target_pairs={{0,1},{2,3},{4,5},{6,7},{8,9},{10,11},{12,13},{14,15},{16,17},{18,... | collective-permute-start | bytes 786440 | tf_op jit(solution)/shard_map/ppermute | solution.py:31
  219.1 17.6 %copy-start.2 = (bf16[256,1024]{1,0:T(8,128)(2,1)S(1)}, bf16[256,1024]{1,0:T(8,128)(2,1)}, u32[]{:S(2)}) copy-start(bf16[256,1024]{1,0:T(8,128)(2,1)} %shard_map.148) | copy-start | bytes 1572868
  219.1 19.5 %copy-start.3 = (bf16[1024,2048]{1,0:T(8,128)(2,1)S(1)}, bf16[1024,2048]{1,0:T(8,128)(2,1)}, u32[]{:S(2)}) copy-start(bf16[1024,2048]{1,0:T(8,128)(2,1)} %maximum_maximum_fusion) | copy-start | bytes 12582916
  230.4 18.3 %collective-permute-start.15 = (bf16[48,4096]{1,0:T(8,128)(2,1)S(1)}, bf16[48,4096]{1,0:T(8,128)(2,1)}, u32[]{:S(2)}, u32[]{:S(2)}) collective-permute-start(bf16[48,4096]{1,0:T(8,128)(2,1)S(1)} %get-tuple-element.22), channel_id=1, source_target_pairs={{0,6},{1,7},{2,0},{3,1},{4,2},{5,3},{6,4},{7,5},{8,14},{9,15},{10,... | collective-permute-start | bytes 1179656 | tf_op jit(solution)/shard_map/ppermute | solution.py:31
  232.9 15.8 %collective-permute-start.16 = (bf16[48,4096]{1,0:T(8,128)(2,1)S(1)}, bf16[48,4096]{1,0:T(8,128)(2,1)}, u32[]{:S(2)}, u32[]{:S(2)}) collective-permute-start(bf16[48,4096]{1,0:T(8,128)(2,1)S(1)} %get-tuple-element.23), channel_id=1, source_target_pairs={{0,7},{1,6},{2,1},{3,0},{4,3},{5,2},{6,5},{7,4},{8,15},{9,14},{10,... | collective-permute-start | bytes 1179656 | tf_op jit(solution)/shard_map/ppermute | solution.py:31
  241.5 32.5 %collective-permute-start.12 = (bf16[512,512]{1,0:T(8,128)(2,1)}, bf16[512,512]{1,0:T(8,128)(2,1)S(1)}, u32[]{:S(2)}, u32[]{:S(2)}) collective-permute-start(bf16[512,512]{1,0:T(8,128)(2,1)} %add_convert_fusion), channel_id=1, source_target_pairs={{0,2},{1,67},{2,4},{3,69},{4,6},{5,71},{6,0},{7,65},{8,10},{9,75},... | collective-permute-start | bytes 1572872 | tf_op jit(solution)/shard_map/ppermute | solution.py:31
  245.2 28.9 %collective-permute-start.3 = (bf16[512,512]{1,0:T(8,128)(2,1)}, bf16[512,512]{1,0:T(8,128)(2,1)S(1)}, u32[]{:S(2)}, u32[]{:S(2)}) collective-permute-start(bf16[512,512]{1,0:T(8,128)(2,1)} %reduce_sum.49), channel_id=1, source_target_pairs={{0,2},{1,66},{2,4},{3,68},{4,6},{5,70},{6,0},{7,64},{8,10},{9,74},... | collective-permute-start | bytes 1572872 | tf_op jit(solution)/shard_map/ppermute | solution.py:31
  (2 other events, 24.4 us)
Sparse Core Ops, SparseCore 0:
  63.8 119.6 all-reduce.2

commit v3 on v2

--- a/solution.py
+++ b/solution.py
@@ -128,6 +128,68 @@
         pltpu.with_memory_space_constraint(w_key, pltpu.HBM),
         pltpu.with_memory_space_constraint(w_value, pltpu.HBM),
     )
+
+
+def product_kernel(places, *refs):
+    *operands, out = refs
+    count = len(operands) // 2
+    total = None
+    for lhs, rhs in zip(operands[:count], operands[count:]):
+        lhs = lhs[...].reshape(-1, lhs.shape[-1])
+        rhs = rhs[...].reshape(-1, rhs.shape[-1])
+        part = lax.dot_general(lhs, rhs, TN, preferred_element_type=jnp.float32)
+        total = part if total is None else total + part
+    out[0] = total.astype(out.dtype)
+
+
+def products(gathered, block, halves, heads):
+    left = [
+        pl.BlockSpec((g.shape[0], g.shape[1], block), lambda i, at: (0, 0, at[0, i])) for g in gathered
+    ]
+    right = [
+        pl.BlockSpec((g.shape[0], g.shape[1], block), lambda i, at: (0, 0, at[1, i])) for g in gathered
+    ]
+    places = jnp.stack([jnp.stack(halves), jnp.stack(heads) + 2]).astype(jnp.int32)
+    return pl.pallas_call(
+        product_kernel,
+        out_shape=jax.ShapeDtypeStruct((RING, block, block), jnp.bfloat16),
+        grid_spec=pltpu.PrefetchScalarGridSpec(
+            num_scalar_prefetch=1,
+            grid=(RING,),
+            in_specs=left + right,
+            out_specs=pl.BlockSpec((1, block, block), lambda i, at: (i, 0, 0)),
+        ),
+        compiler_params=pltpu.CompilerParams(vmem_limit_bytes=32 * 1024 * 1024),
+    )(places, *gathered, *gathered)
+
+
+def pack_kernel(saved, key, value, out):
+    rows, piece = saved.shape
+    out[0, :rows, :] = saved[...]
+    start = rows
+    for source in (key, value):
+        for column in range(0, source.shape[1], piece):
+            out[0, start : start + source.shape[0], :] = source[:, column : column + piece]
+            start += source.shape[0]
+
+
+def packed(saved, key, value, replicas):
+    rows, features = saved.shape
+    piece, share, width = features // replicas, rows // replicas, key.shape[1]
+    height = rows + 2 * width // piece * share
+
+    def column(i):
+        x, z = i // RING, i % RING
+        return 2 * (x % 2 * RING + z) + x // 2
+
+    few = pl.BlockSpec((share, width), lambda i: (i, 0))
+    return pl.pallas_call(
+        pack_kernel,
+        out_shape=jax.ShapeDtypeStruct((replicas, height, piece), saved.dtype),
+        grid=(replicas,),
+        in_specs=[pl.BlockSpec((rows, piece), lambda i: (0, column(i))), few, few],
+        out_specs=pl.BlockSpec((1, height, piece), lambda i: (i, 0, 0)),
+    )(saved, key, value)
 
 
 def on_device(
@@ -155,30 +217,40 @@
     capacity_blocks = 2 * ((plan_row.shape[0] + replicas - 2) // (replicas - 1))
     width = w_key.shape[2]
 
-    dead_stream, dead_key, dead_value = lax.psum(
-        (backup_stream[0], backup_key_cot[0], backup_value_cot[0]), "dp"
-    )
-
-    values = stream[0].astype(jnp.float32)
-    squares = both_sides(jnp.sum(values * values, axis=1))
-    own_scale = lax.rsqrt(squares / D + EPSILON)[:, None]
-    normed = (values * own_scale * norm_gain).astype(jnp.bfloat16)
-
+    keeper = (fallen + 1) % replicas
+    fourth = stream.shape[2] // RING
+    block = fourth // 2
+    piece = block // 2
+    share = rows // replicas
+
+    saved = backup_stream[0]
+    saved_pieces = packed(saved, backup_key_cot[0], backup_value_cot[0], replicas)
     own_positions = lax.dynamic_slice_in_dim(positions[0], member * rows, rows, 0)
-    cots = derotate(key_cot[0], value_cot[0], own_positions)
+    key_first, saved_pieces = lax.optimization_barrier((key_cot[0], saved_pieces))
+    cots = derotate(key_first, value_cot[0], own_positions)
+    dead = lax.all_to_all(saved_pieces, "dp", 0, 0)
+    dead = lax.dynamic_index_in_dim(dead, keeper, 0, keepdims=False)
     near = moved(cots, lambda x, z, s, t: (x, z, s - 1, t))
     far = moved(cots, lambda x, z, s, t: (x, z, s - 1, 1 - t))
 
-    late_cots, normed = lax.optimization_barrier((cots, normed))
-    ones = jnp.ones((rows, 1), jnp.float32)
-    across, straight = feature_halves(late_cots, ones, w_key[0], w_value[0], side)
-    across = moved(across, lambda x, z, s, t: (x, z, s - 1, 1 - t))
-    straight = moved(straight, lambda x, z, s, t: (x, z, s - 1, t))
-    feature = straight.astype(jnp.float32) + across.astype(jnp.float32)
-    stream_grad = (own_scale * (norm_gain * feature)).astype(jnp.bfloat16)
-
-    fourth = normed.shape[1] // RING
-    block = fourth // 2
+    values = stream[0].astype(jnp.float32)
+    saved_values = saved.astype(jnp.float32)
+    squares = both_sides(
+        jnp.concatenate([jnp.sum(values * values, axis=1), jnp.sum(saved_values * saved_values, axis=1)])
+    )
+    scales = lax.rsqrt(squares / D + EPSILON)
+    own_scale = scales[:rows, None]
+    normed = (values * own_scale * norm_gain).astype(jnp.bfloat16)
+
+    gathered = []
+    for step in (2, 1, 3, 0):
+        there = (at_x + step) % RING
+        start = (2 * (there % 2) + there // 2) * fourth
+        tile = jnp.concatenate(
+            [lax.dynamic_slice_in_dim(normed, start, fourth, 1), near[:, width:], far[:, width:]],
+            axis=1,
+        )
+        gathered.append((tile, step))
     first = side == 0
     key_heads = [
         jnp.where(first, near[:, :width], far[:, :width]),
@@ -194,52 +266,65 @@
             for z in range(RING)
         ]
     )
+    tiles = [tile for tile, _ in gathered]
+    outgoing, dead, _ = lax.optimization_barrier((outgoing, dead, tiles))
+    gathered = [
+        moved(tile, lambda x, z, s, t, step=step: (x + step, z, s, t))[None] if step else tile[None]
+        for tile, (_, step) in zip(tiles, gathered)
+    ]
     z_rings = [[RING * x + z for z in range(RING)] for x in range(RING)]
     x_rings = [[RING * x + z for x in range(RING)] for z in range(RING)]
     arrived = lax.all_to_all(outgoing, "dp", 0, 0, axis_index_groups=z_rings)
-    arrived = arrived.reshape(RING * rows, 2 * fourth)
-
-    def product(lhs, rhs):
-        return lax.dot_general(lhs, rhs, TN, preferred_element_type=jnp.float32).astype(jnp.bfloat16)
-
-    parts = jnp.stack(
-        [
-            product(
-                arrived[:, half * block : (half + 1) * block],
-                arrived[:, fourth + head * width : fourth + (head + 1) * width],
-            )
-            for head in range(2)
-            for half in range(2)
-        ]
-    )
-    parts = lax.all_to_all(parts, "dp", 0, 0, axis_index_groups=x_rings)
-    grad_key = jnp.sum(parts.astype(jnp.float32), axis=0).astype(jnp.bfloat16)
-    grad_key = moved(grad_key, lambda x, z, s, t: (2 * t + x % 2, z, s + 1, x // 2))
-
-    gathered = []
-    for step in (2, 1, 3, 0):
-        there = (at_x + step) % RING
-        start = (2 * (there % 2) + there // 2) * fourth
-        piece = jnp.concatenate(
-            [lax.dynamic_slice_in_dim(normed, start, fourth, 1), near[:, width:], far[:, width:]],
-            axis=1,
-        )
-        if step:
-            piece = moved(piece, lambda x, z, s, t, step=step: (x + step, z, s, t))
-        gathered.append(piece)
-    gathered = jnp.concatenate(gathered, axis=0)
-    dead_stream, dead_key, dead_value, gathered = lax.optimization_barrier(
-        (dead_stream, dead_key, dead_value, gathered)
-    )
-
+
+    late_cots, tiles = lax.optimization_barrier((cots, tiles))
+    ones = jnp.ones((rows, 1), jnp.float32)
+    across, straight = feature_halves(late_cots, ones, w_key[0], w_value[0], side)
+    across, straight, dead = lax.optimization_barrier((across, straight, dead))
+    across = moved(across, lambda x, z, s, t: (x, z, s - 1, 1 - t))
+    straight = moved(straight, lambda x, z, s, t: (x, z, s - 1, t))
+    arrived, across, straight = lax.optimization_barrier((arrived, across, straight))
+    feature = straight.astype(jnp.float32) + across.astype(jnp.float32)
+    stream_grad = (own_scale * (norm_gain * feature)).astype(jnp.bfloat16)
+
+    saved_scale = scales[rows:]
+    scale_high = saved_scale.astype(jnp.bfloat16)
+    scale_low = (saved_scale - scale_high.astype(jnp.float32)).astype(jnp.bfloat16)
+    factors = jnp.concatenate([scale_high.reshape(share, -1), scale_low.reshape(share, -1)], axis=1)
+    factors = jnp.pad(factors, ((0, 0), (0, HEAD - factors.shape[1])))
+    dead_share = dead[rows:].reshape(-1, share, piece).transpose(1, 0, 2).reshape(share, -1)
+    shares = lax.all_gather(jnp.concatenate([dead_share, factors], axis=1), "dp")
+    gathered, shares = lax.optimization_barrier((gathered, shares))
+    dead_raw = shares[:, :, : 2 * width].reshape(rows, 2 * width)
+    factors = lax.dynamic_index_in_dim(shares[:, :, 2 * width :], keeper, 0, keepdims=False)
+    factors = factors.astype(jnp.float32)
+    dead_scale = (factors[:, :share] + factors[:, share : 2 * share]).reshape(rows)[:, None]
+    dead_positions = lax.dynamic_slice_in_dim(positions[0], fallen * rows, rows, 0)
+    dead_cots = derotate(dead_raw[:, :width], dead_raw[:, width:], dead_positions)
+
+    start = (at_x % 2 * RING + at_z) * block + at_x // 2 * piece
+    dead_piece = (
+        dead[:rows].astype(jnp.float32) * dead_scale * lax.dynamic_slice_in_dim(norm_gain, start, piece, 0)
+    ).astype(jnp.bfloat16)
+    sent = moved(
+        dead_piece, lambda x, z, s, t: (x, z, s, 1 - t) if x // 2 == t else (x + 2, z, s, t)
+    )
+    lent = moved(dead_piece, lambda x, z, s, t: None if x // 2 == t else (x + 2, z, s, 1 - t))
+    home = at_x // 2
+    same = jnp.where(home == side, dead_piece, sent)
+    other = jnp.where(home == side, sent, lent)
+    dead_block = jnp.concatenate(
+        [jnp.where(home == 0, same, other), jnp.where(home == 0, other, same)], axis=1
+    )
+    dead_part = lax.dot_general(dead_block, dead_cots, TN, preferred_element_type=jnp.float32)
+
+    steps = (2, 1, 3, 0)
+    there = [(at_z + step) % RING for step in steps]
+    value_parts = products(
+        gathered, block, [r % 2 for r in there], [(r // 2) ^ (at_x // 2) for r in there]
+    )
     total = None
-    for step in (2, 1, 3, 0):
-        there = (at_z + step) % RING
-        half, head = there % 2, (there // 2) ^ (at_x // 2)
-        part = product(
-            lax.dynamic_slice_in_dim(gathered, half * block, block, 1),
-            lax.dynamic_slice_in_dim(gathered, fourth + head * width, width, 1),
-        )
+    for place, step in enumerate(steps):
+        part = value_parts[place]
         if step:
             part = moved(part, lambda x, z, s, t, step=step: (x, z + step, s, t))
         part = part.astype(jnp.float32)
@@ -248,23 +333,11 @@
         total.astype(jnp.bfloat16),
         lambda x, z, s, t: (2 * t + x % 2, 2 * (x // 2) + z % 2, s + 1, t ^ (z // 2) ^ (x // 2)),
     )
-
-    dead_values = dead_stream.astype(jnp.float32)
-    dead_squares = both_sides(jnp.sum(dead_values * dead_values, axis=1))
-    dead_scale = lax.rsqrt(dead_squares / D + EPSILON)[:, None]
-    dead_positions = lax.dynamic_slice_in_dim(positions[0], fallen * rows, rows, 0)
-    dead_cots = derotate(dead_key, dead_value, dead_positions)
-
-    home = member // (replicas // 2)
-    start = (member % (replicas // 2)) * block
-    dead_block = (
-        lax.dynamic_slice_in_dim(dead_stream, start, block, 1).astype(jnp.float32)
-        * dead_scale
-        * lax.dynamic_slice_in_dim(norm_gain, start, block, 0)
-    ).astype(jnp.bfloat16)
-    lent = moved(dead_block, lambda x, z, s, t: (x, z, s, 1 - t) if t == x // 2 else None)
-    dead_block = jnp.where(home == side, dead_block, lent)
-    dead_part = lax.dot_general(dead_block, dead_cots, TN, preferred_element_type=jnp.float32)
+    static = [jnp.int32(r) for r in range(RING)]
+    key_parts = products([arrived], block, [r % 2 for r in static], [r // 2 for r in static])
+    parts = lax.all_to_all(key_parts, "dp", 0, 0, axis_index_groups=x_rings)
+    grad_key = jnp.sum(parts.astype(jnp.float32), axis=0).astype(jnp.bfloat16)
+    grad_key = moved(grad_key, lambda x, z, s, t: (2 * t + x % 2, z, s + 1, x // 2))
     grad_key = grad_key.astype(jnp.float32) + dead_part[:, :width]
     grad_value = grad_value.astype(jnp.float32) + dead_part[:, width:]
 
@@ -273,6 +346,7 @@
         selection.astype(jnp.bfloat16), dead_cots, preferred_element_type=jnp.float32
     ).astype(jnp.bfloat16)
     slot_scale = jnp.sum(selection * jnp.reshape(dead_scale, (1, rows)), axis=1, keepdims=True)
+    slot_cots, _ = lax.optimization_barrier((slot_cots, (key_parts, value_parts)))
     across, straight = feature_halves(slot_cots, slot_scale, w_key[0], w_value[0], side)
     across = moved(across, lambda x, z, s, t: (x, z, s - 1, 1 - t))
     straight = moved(straight, lambda x, z, s, t: (x, z, s - 1, t))

time: 285 us -> 235 us (0.82); the launches traced: 284 us -> 230 us
  waiting for transfers between devices: 129 us -> 45.1 us
  blocking collectives: 0 us -> 36 us
  Pallas kernels: 27.7 us -> 49.1 us
  matrix products: 24.4 us -> 3.07 us
  other arithmetic: 46.3 us -> 27.2 us
  starting transfers between devices: 37.9 us -> 55.1 us
  between operations: 15.2 us -> 2.82 us
  local copies, waits for them, and re-layouts: 3.16 us -> 11.9 us
    ppermute x17, waiting for transfers between devices: 86.2 us -> 21.7 us  [moved(): return lax.ppermute(block, AXES, route)]
    psum x1 -> x0, waiting for transfers between devices: 43.2 us -> none  [on_device(): lax.psum((backup_stream[0], backup_key_cot[0], backup_value_cot[0]), 'dp')]
    all_gather x0 -> x1, blocking collectives: none -> 36 us  [on_device(): lax.all_gather(jnp.concatenate([dead_share, factors], axis=1), 'dp')]
    all_to_all x1 -> x2, waiting for transfers between devices: 0.01 us -> 23.5 us  [the longest x1 23.5 us: on_device(): dead = lax.all_to_all(saved_pieces, 'dp', 0, 0)]
    dot_general x8 -> x0, matrix products: 21.3 us -> none  [product(): lax.dot_general(lhs, rhs, TN, preferred_element_type=jnp.float32)]
    pallas_call x0 -> x3, Pallas kernels: none -> 20.9 us  [the longest x2 11 us: products(): pl.pallas_call(product_kernel, out_shape=jax.ShapeDtypeStruct((RING, bloc...]
    concatenate x1 -> x3, other arithmetic: 17.5 us -> 0.09 us  [the longest x1 0.08 us: on_device(): jnp.concatenate([scale_high.reshape(share, -1), scale_low.reshape(share,...]
    ppermute x17, starting transfers between devices: 29.3 us -> 38 us  [moved(): return lax.ppermute(block, AXES, route)]
  transfers between devices with their start and end apart: 20 -> 20, of which waited for: 5 -> 4; matrix products, arithmetic and copies ran while one was open for 23% -> 12% of each run, Pallas kernels for 9% -> 16%
where the time goes in v3:
time: 235 us; the launch traced here: 230 us
  starting transfers between devices  55.1 us (23%)
  Pallas kernels  49.1 us (21%)
  waiting for transfers between devices  45.1 us (19%)
  blocking collectives  36 us (15%)
  other arithmetic  27.2 us (12%)
  local copies, waits for them, and re-layouts  11.9 us (5%)
  matrix products  3.07 us (1%)
  between operations  2.82 us (1%)
    ppermute x17, starting transfers between devices, moved(): return lax.ppermute(block, AXES, route)  38 us
    all_gather x1, blocking collectives, on_device(): lax.all_gather(jnp.concatenate([dead_share, factors], axis=1), 'dp')  36 us
    pallas_call x2, Pallas kernels, feature_halves(): pl.pallas_call(feature_kernel, out_shape=(result, result), in_specs=[pl.B...  24.1 us
    all_to_all x1, waiting for transfers between devices, on_device(): dead = lax.all_to_all(saved_pieces, 'dp', 0, 0)  23.5 us
    ppermute x17, waiting for transfers between devices, moved(): return lax.ppermute(block, AXES, route)  21.7 us
    pallas_call x2, Pallas kernels, products(): pl.pallas_call(product_kernel, out_shape=jax.ShapeDtypeStruct((RING, bloc...  11 us
    pallas_call x1, Pallas kernels, packed(): pl.pallas_call(pack_kernel, out_shape=jax.ShapeDtypeStruct((replicas, hei...  9.85 us
    all_to_all x1, starting transfers between devices, on_device(): dead = lax.all_to_all(saved_pieces, 'dp', 0, 0)  7.64 us
  transfers between devices with their start and end apart: 20, of which 4 were waited for; matrix products, arithmetic and copies ran while one was open for 12% of the time, Pallas kernels for 16%

profile of v3, /device:TPU:25, one launch (start us, length us, event | category | flops | bytes accessed | tf_op | source)
XLA Modules:
  0.0 230.4 jit_solution(11744529062177996472)
XLA Ops:
  2.7 9.8 %shard_map.147 = bf16[16,320,256]{2,1,0:T(8,128)(2,1)} custom-call(bf16[256,4096]{1,0:T(8,128)(2,1)} %bitcast.88, bf16[256,512]{1,0:T(8,128)(2,1)} %bitcast.92, bf16[256,512]{1,0:T(8,128)(2,1)} %bitcast.93), custom_call_target="tpu_custom_call" | custom-call | tf_op jit(solution)/shard_map/pallas_call | solution.py:186
  15.0 2.1 shard_map.148.cots
  18.6 2.5 %fusion = (f32[256]{0:T(256)S(1)}, f32[256]{0:T(256)S(1)}) fusion(bf16[1,256,4096]{2,1,0:T(8,128)(2,1)} %param.12, bf16[1,256,4096]{2,1,0:T(8,128)(2,1)S(1)} %copy-done.7), kind=kLoop, calls=%fused_computation.2 | loop fusion | flops 6290944 | bytes 4196352 | tf_op jit(solution)/shard_map/reduce_sum | solution.py:239
  21.1 2.1 collective-permute-start
  23.2 7.6 %all-to-all-start = ((bf16[16,320,256]{2,1,0:T(8,128)(2,1)}), bf16[16,320,256]{2,1,0:T(8,128)(2,1)}, u32[]{:S(2)}, u32[]{:S(2)}) async-start(bf16[16,320,256]{2,1,0:T(8,128)(2,1)} %shard_map.147), calls=%async_computation | async-start | bytes 5242880 | tf_op jit(solution)/shard_map/all_to_all | solution.py:231
  35.8 2.3 %pad_maximum_fusion = bf16[4,256,2048]{2,1,0:T(8,128)(2,1)} fusion(bf16[1,256,2048]{2,1,0:T(8,128)(2,1)S(1)} %get-tuple-element.74, bf16[1,256,2048]{2,1,0:T(8,128)(2,1)S(1)} %get-tuple-element.73, bf16[1,256,2048]{2,1,0:T(8,128)(2,1)S(1)} %get-tuple-element.72, bf16[1,256,2048]{2,1,0:T(8,128)(2,1)S(1)} %get-tuple-element.71), kind=kLoop, calls=%fused_computation.5 | loop fusion | flops 6291456 | bytes 8388608 | tf_op jit(solution)/shard_map/stack | solution.py:259
  38.2 23.5 %all-to-all-done = bf16[16,320,256]{2,1,0:T(8,128)(2,1)} async-done(((bf16[16,320,256]{2,1,0:T(8,128)(2,1)}), bf16[16,320,256]{2,1,0:T(8,128)(2,1)}, u32[]{:S(2)}, u32[]{:S(2)}) %all-to-all-start) | async-done | bytes 2621472 | tf_op jit(solution)/shard_map/all_to_all | solution.py:231
  62.6 4.9 %all-to-all-start.1 = ((bf16[4,256,2048]{2,1,0:T(8,128)(2,1)}), bf16[4,256,2048]{2,1,0:T(8,128)(2,1)}, u32[]{:S(2)}, u32[]{:S(2)}) async-start(bf16[4,256,2048]{2,1,0:T(8,128)(2,1)} %pad_maximum_fusion), calls=%async_computation.1 | async-start | bytes 8388608 | tf_op jit(solution)/shard_map/all_to_all | solution.py:277
  72.8 13.0 %shard_map.149 = (bf16[256,4096]{1,0:T(8,128)(2,1)}, bf16[256,4096]{1,0:T(8,128)(2,1)}) custom-call(s32[1]{0:T(128)} %bitcast.14.half, bf16[256,1024]{1,0:T(8,128)(2,1)S(1)} %copy-done.5, f32[256,1]{1,0:T(8,128)S(1)} %broadcast_in_dim.77.scale, bf16[8192,512]{1,0:T(8,128)(2,1)} %bitcast.84, bf16[8192,512]{1,0:T(8,128)(2,1)} %bitcast.86), custom_call_target="tpu_custom_call" | custom-call | tf_op jit(solution)/shard_map/pallas_call | solution.py:112
  85.9 7.9 %collective-permute-start.3 = (bf16[256,4096]{1,0:T(8,128)(2,1)}, bf16[256,4096]{1,0:T(8,128)(2,1)}, u32[]{:S(2)}, u32[]{:S(2)}) collective-permute-start(bf16[256,4096]{1,0:T(8,128)(2,1)} %get-tuple-element.32), channel_id=1, source_target_pairs={{0,7},{1,6},{2,1},{3,0},{4,3},{5,2},{6,5},{7,4},{8,15},{9,14},{10,... | collective-permute-start | bytes 6291464 | tf_op jit(solution)/shard_map/ppermute | solution.py:31
  93.9 36.0 %all-gather = bf16[256,1152]{1,0:T(8,128)(2,1)S(1)} all-gather(bf16[16,1152]{1,0:T(8,128)(2,1)S(1)} %pad_maximum_fusion.17), channel_id=2, replica_groups=mesh['dp'=16,'pipe'=4,'tensor'=2] {'dp'}, dimensions={0}, use_global_device_ids=true | all-gather | bytes 626688 | tf_op jit(solution)/shard_map/all_gather | solution.py:295
  132.8 7.3 %collective-permute-start.10 = (bf16[256,256]{1,0:T(8,128)(2,1)}, bf16[256,256]{1,0:T(8,128)(2,1)S(1)}, u32[]{:S(2)}, u32[]{:S(2)}) collective-permute-start(bf16[256,256]{1,0:T(8,128)(2,1)} %multiply_convert_fusion.2), channel_id=1, source_target_pairs={{1,64},{3,66},{5,68},{7,70},{9,72},{11,74},{13,76},{15,78},{17,80}... | collective-permute-start | bytes 393224 | tf_op jit(solution)/shard_map/ppermute | solution.py:31
  142.8 5.1 %shard_map.152 = bf16[4,512,512]{2,1,0:T(8,128)(2,1)S(1)} custom-call(s32[2,4]{1,0:T(2,128)S(1)} %pad_add_fusion.places, bf16[1,256,2048]{2,1,0:T(8,128)(2,1)} %bitcast.17.refs_0_.refs_4_, bf16[1,256,2048]{2,1,0:T(8,128)(2,1)S(1)} %bitcast.80, bf16[1,256,2048]{2,1,0:T(8,128)(2,1)S(1)} %bitcast.82, ...), custom_call_target="tpu_custom_call" | custom-call | tf_op jit(solution)/shard_map/pallas_call | solution.py:153
  151.3 2.1 shard_map.151
  157.8 5.9 %shard_map.150 = bf16[4,512,512]{2,1,0:T(8,128)(2,1)S(1)} custom-call(s32[2,4]{1,0:T(2,128)S(1)} %copy-done.6, bf16[4,256,2048]{2,1,0:T(8,128)(2,1)} %all-to-all-done.1.refs_0_.refs_1_, bf16[4,256,2048]{2,1,0:T(8,128)(2,1)} %all-to-all-done.1.refs_0_.refs_1_), custom_call_target="tpu_custom_call" | custom-call | tf_op jit(solution)/shard_map/pallas_call | solution.py:153
  165.1 4.6 %all-to-all-start.2 = ((bf16[4,512,512]{2,1,0:T(8,128)(2,1)}), bf16[4,512,512]{2,1,0:T(8,128)(2,1)}, u32[]{:S(2)}, u32[]{:S(2)}) async-start(bf16[4,512,512]{2,1,0:T(8,128)(2,1)} %copy-done), calls=%async_computation.2 | async-start | bytes 4194304 | tf_op jit(solution)/shard_map/all_to_all | solution.py:338
  173.6 2.4 %fusion.10 = bf16[512,512]{1,0:T(8,128)(2,1)} fusion(bf16[512,512]{1,0:T(8,128)(2,1)} %collective-permute-done.13, bf16[512,512]{1,0:T(8,128)(2,1)} %collective-permute-done.12, bf16[512,512]{1,0:T(8,128)(2,1)} %collective-permute-done.11, bf16[4,512,512]{2,1,0:T(8,128)(2,1)S(1)} %shard_map.152), kind=kLoop, calls=%fused_computation.35 | loop fusion | flops 2097152 | bytes 2621440 | tf_op jit(solution)/shard_map/convert_element_type | solution.py:333
  176.0 8.8 %collective-permute-start.14 = (bf16[512,512]{1,0:T(8,128)(2,1)}, bf16[512,512]{1,0:T(8,128)(2,1)}, u32[]{:S(2)}, u32[]{:S(2)}) collective-permute-start(bf16[512,512]{1,0:T(8,128)(2,1)} %fusion.10), channel_id=1, source_target_pairs={{0,2},{1,67},{2,4},{3,69},{4,6},{5,71},{6,0},{7,65},{8,10},{9,75},... | collective-permute-start | bytes 1572872 | tf_op jit(solution)/shard_map/ppermute | solution.py:31
  184.9 11.0 %shard_map.153 = (bf16[48,4096]{1,0:T(8,128)(2,1)S(1)}, bf16[48,4096]{1,0:T(8,128)(2,1)S(1)}) custom-call(s32[1]{0:T(128)} %bitcast.14.half, bf16[48,1024]{1,0:T(8,128)(2,1)S(1)} %convolution_convert_fusion.cots, f32[48,1]{1,0:T(8,128)S(1)} %copy.21.scale, bf16[8192,512]{1,0:T(8,128)(2,1)} %bitcast.85, bf16[8192,512]{1,0:T(8,128)(2,1)} %bitcast.87), custom_call_target="tpu_custom_call" | custom-call | tf_op jit(solution)/shard_map/pallas_call | solution.py:112
  196.0 2.1 collective-permute-start.16
  198.1 4.6 %fusion.3 = bf16[1,256,4096]{2,1,0:T(8,128)(2,1)} fusion(bf16[256,4096]{1,0:T(8,128)(2,1)} %collective-permute-done.3, bf16[256,4096]{1,0:T(8,128)(2,1)} %collective-permute-done.4, f32[4096]{0:T(1024)S(1)} %copy-done.12, f32[256]{0:T(256)S(1)} %get-tuple-element.85), kind=kLoop, calls=%fused_computation.8 | loop fusion | flops 6291456 | bytes 6308864 | tf_op jit(solution)/shard_map/broadcast_in_dim | solution.py:356
  202.7 2.3 %reduce_sum.50 = bf16[512,512]{1,0:T(8,128)(2,1)S(1)} reduce(bf16[4,512,512]{2,1,0:T(8,128)(2,1)} %all-to-all-done.2, bf16[]{:T(256)} %constant.345.clone.1), dimensions={0}, to_apply=%region_2.3 | reduce | flops 786432 | bytes 2621442 | tf_op jit(solution)/shard_map/reduce_sum | solution.py:339
  207.3 18.3 %collective-permute-done.16 = bf16[48,4096]{1,0:T(8,128)(2,1)} collective-permute-done((bf16[48,4096]{1,0:T(8,128)(2,1)S(1)}, bf16[48,4096]{1,0:T(8,128)(2,1)}, u32[]{:S(2)}, u32[]{:S(2)}) %collective-permute-start.16) | collective-permute-done | bytes 393248 | tf_op jit(solution)/shard_map/ppermute | solution.py:31
  227.6 2.7 %fusion.8 = (f32[1,512,512]{2,1,0:T(8,128)}, f32[1,512,512]{2,1,0:T(8,128)}) fusion(f32[512,1024]{1,0:T(8,128)S(1)} %copy-done.9, bf16[512,512]{1,0:T(8,128)(2,1)} %collective-permute-done.14, bf16[512,512]{1,0:T(8,128)(2,1)S(1)} %collective-permute-done.5), kind=kLoop, calls=%fused_computation.31 | loop fusion | flops 1048576 | bytes 5242880 | tf_op jit(solution)/shard_map/broadcast_in_dim | solution.py:356
  (106 shorter events, 38.3 us)
Async XLA Ops:
  2.7 15.9 %copy-start.7 = (bf16[1,256,4096]{2,1,0:T(8,128)(2,1)S(1)}, bf16[1,256,4096]{2,1,0:T(8,128)(2,1)}, u32[]{:S(2)}) copy-start(bf16[1,256,4096]{2,1,0:T(8,128)(2,1)} %param.13) | copy-start | bytes 6291460
  17.1 16.1 %collective-permute-start.2 = (bf16[256,1024]{1,0:T(8,128)(2,1)}, bf16[256,1024]{1,0:T(8,128)(2,1)S(1)}, u32[]{:S(2)}, u32[]{:S(2)}) collective-permute-start(bf16[256,1024]{1,0:T(8,128)(2,1)} %shard_map.148.cots), channel_id=1, source_target_pairs={{0,7},{1,6},{2,1},{3,0},{4,3},{5,2},{6,5},{7,4},{8,15},{9,14},{10,... | collective-permute-start | bytes 1572872 | tf_op jit(solution)/shard_map/ppermute | solution.py:31
  18.6 14.6 %collective-permute-start.1 = (bf16[256,1024]{1,0:T(8,128)(2,1)}, bf16[256,1024]{1,0:T(8,128)(2,1)S(1)}, u32[]{:S(2)}, u32[]{:S(2)}) collective-permute-start(bf16[256,1024]{1,0:T(8,128)(2,1)} %shard_map.148.cots), channel_id=1, source_target_pairs={{0,6},{1,7},{2,0},{3,1},{4,2},{5,3},{6,4},{7,5},{8,14},{9,15},{10,... | collective-permute-start | bytes 1572872 | tf_op jit(solution)/shard_map/ppermute | solution.py:31
  21.1 10.9 %copy-start.8 = (bf16[1,256,4096]{2,1,0:T(8,128)(2,1)S(1)}, bf16[1,256,4096]{2,1,0:T(8,128)(2,1)}, u32[]{:S(2)}) copy-start(bf16[1,256,4096]{2,1,0:T(8,128)(2,1)} %param.12) | copy-start | bytes 6291460
  21.1 10.9 %copy-start.12 = (f32[4096]{0:T(1024)S(1)}, f32[4096]{0:T(1024)}, u32[]{:S(2)}) copy-start(f32[4096]{0:T(1024)} %param.14) | copy-start | bytes 49156
  21.1 10.9 %collective-permute-start = (f32[512]{0:T(512)S(1)}, f32[512]{0:T(512)S(1)}, u32[]{:S(2)}, u32[]{:S(2)}) collective-permute-start(f32[512]{0:T(512)S(1)} %pad_maximum_fusion.18), channel_id=1, source_target_pairs={{0,1},{1,0},{2,3},{3,2},{4,5},{5,4},{6,7},{7,6},{8,9},{9,8},{10,11... | collective-permute-start | bytes 6152 | tf_op jit(solution)/shard_map/ppermute | solution.py:31
  23.2 38.4 %all-to-all-start = ((bf16[16,320,256]{2,1,0:T(8,128)(2,1)}), bf16[16,320,256]{2,1,0:T(8,128)(2,1)}, u32[]{:S(2)}, u32[]{:S(2)}) async-start(bf16[16,320,256]{2,1,0:T(8,128)(2,1)} %shard_map.147), calls=%async_computation | async-start | bytes 5242880 | tf_op jit(solution)/shard_map/all_to_all | solution.py:231
  62.6 95.2 %all-to-all-start.1 = ((bf16[4,256,2048]{2,1,0:T(8,128)(2,1)}), bf16[4,256,2048]{2,1,0:T(8,128)(2,1)}, u32[]{:S(2)}, u32[]{:S(2)}) async-start(bf16[4,256,2048]{2,1,0:T(8,128)(2,1)} %pad_maximum_fusion), calls=%async_computation.1 | async-start | bytes 8388608 | tf_op jit(solution)/shard_map/all_to_all | solution.py:277
  67.5 62.5 %collective-permute-start.7 = (bf16[256,2048]{1,0:T(8,128)(2,1)}, bf16[256,2048]{1,0:T(8,128)(2,1)S(1)}, u32[]{:S(2)}, u32[]{:S(2)}) collective-permute-start(bf16[256,2048]{1,0:T(8,128)(2,1)} %get-tuple-element.77), channel_id=1, source_target_pairs={{0,32},{1,33},{2,34},{3,35},{4,36},{5,37},{6,38},{7,39},{8,40},{9,... | collective-permute-start | bytes 3145736 | tf_op jit(solution)/shard_map/ppermute | solution.py:31
  69.2 60.8 %collective-permute-start.8 = (bf16[256,2048]{1,0:T(8,128)(2,1)}, bf16[256,2048]{1,0:T(8,128)(2,1)S(1)}, u32[]{:S(2)}, u32[]{:S(2)}) collective-permute-start(bf16[256,2048]{1,0:T(8,128)(2,1)} %get-tuple-element.78), channel_id=1, source_target_pairs={{0,96},{1,97},{2,98},{3,99},{4,100},{5,101},{6,102},{7,103},{8,104... | collective-permute-start | bytes 3145736 | tf_op jit(solution)/shard_map/ppermute | solution.py:31
  70.2 60.7 %collective-permute-start.6 = (bf16[256,2048]{1,0:T(8,128)(2,1)}, bf16[256,2048]{1,0:T(8,128)(2,1)}, u32[]{:S(2)}, u32[]{:S(2)}) collective-permute-start(bf16[256,2048]{1,0:T(8,128)(2,1)} %get-tuple-element.79), channel_id=1, source_target_pairs={{0,64},{1,65},{2,66},{3,67},{4,68},{5,69},{6,70},{7,71},{8,72},{9,... | collective-permute-start | bytes 3145736 | tf_op jit(solution)/shard_map/ppermute | solution.py:31
  85.9 71.9 %collective-permute-start.3 = (bf16[256,4096]{1,0:T(8,128)(2,1)}, bf16[256,4096]{1,0:T(8,128)(2,1)}, u32[]{:S(2)}, u32[]{:S(2)}) collective-permute-start(bf16[256,4096]{1,0:T(8,128)(2,1)} %get-tuple-element.32), channel_id=1, source_target_pairs={{0,7},{1,6},{2,1},{3,0},{4,3},{5,2},{6,5},{7,4},{8,15},{9,14},{10,... | collective-permute-start | bytes 6291464 | tf_op jit(solution)/shard_map/ppermute | solution.py:31
  93.8 64.0 %collective-permute-start.4 = (bf16[256,4096]{1,0:T(8,128)(2,1)}, bf16[256,4096]{1,0:T(8,128)(2,1)}, u32[]{:S(2)}, u32[]{:S(2)}) collective-permute-start(bf16[256,4096]{1,0:T(8,128)(2,1)} %get-tuple-element.33), channel_id=1, source_target_pairs={{0,6},{1,7},{2,0},{3,1},{4,2},{5,3},{6,4},{7,5},{8,14},{9,15},{10,... | collective-permute-start | bytes 6291464 | tf_op jit(solution)/shard_map/ppermute | solution.py:31
  132.8 21.9 %collective-permute-start.10 = (bf16[256,256]{1,0:T(8,128)(2,1)}, bf16[256,256]{1,0:T(8,128)(2,1)S(1)}, u32[]{:S(2)}, u32[]{:S(2)}) collective-permute-start(bf16[256,256]{1,0:T(8,128)(2,1)} %multiply_convert_fusion.2), channel_id=1, source_target_pairs={{1,64},{3,66},{5,68},{7,70},{9,72},{11,74},{13,76},{15,78},{17,80}... | collective-permute-start | bytes 393224 | tf_op jit(solution)/shard_map/ppermute | solution.py:31
  140.1 16.6 %collective-permute-start.9 = (bf16[256,256]{1,0:T(8,128)(2,1)}, bf16[256,256]{1,0:T(8,128)(2,1)}, u32[]{:S(2)}, u32[]{:S(2)}) collective-permute-start(bf16[256,256]{1,0:T(8,128)(2,1)} %multiply_convert_fusion.2), channel_id=1, source_target_pairs={{0,1},{1,65},{2,3},{3,67},{4,5},{5,69},{6,7},{7,71},{8,9},{9,73},{... | collective-permute-start | bytes 393224 | tf_op jit(solution)/shard_map/ppermute | solution.py:31
  149.2 22.4 %collective-permute-start.11 = (bf16[512,512]{1,0:T(8,128)(2,1)}, bf16[512,512]{1,0:T(8,128)(2,1)}, u32[]{:S(2)}, u32[]{:S(2)}) collective-permute-start(bf16[512,512]{1,0:T(8,128)(2,1)} %get-tuple-element.50), channel_id=1, source_target_pairs={{0,16},{1,17},{2,18},{3,19},{4,20},{5,21},{6,22},{7,23},{8,24},{9,... | collective-permute-start | bytes 1572872 | tf_op jit(solution)/shard_map/ppermute | solution.py:31
  154.7 16.9 %collective-permute-start.13 = (bf16[512,512]{1,0:T(8,128)(2,1)}, bf16[512,512]{1,0:T(8,128)(2,1)}, u32[]{:S(2)}, u32[]{:S(2)}) collective-permute-start(bf16[512,512]{1,0:T(8,128)(2,1)} %get-tuple-element.51), channel_id=1, source_target_pairs={{0,24},{1,25},{2,26},{3,27},{4,28},{5,29},{6,30},{7,31},{8,0},{9,1... | collective-permute-start | bytes 1572872 | tf_op jit(solution)/shard_map/ppermute | solution.py:31
  156.7 16.9 %collective-permute-start.12 = (bf16[512,512]{1,0:T(8,128)(2,1)}, bf16[512,512]{1,0:T(8,128)(2,1)}, u32[]{:S(2)}, u32[]{:S(2)}) collective-permute-start(bf16[512,512]{1,0:T(8,128)(2,1)} %get-tuple-element.52), channel_id=1, source_target_pairs={{0,8},{1,9},{2,10},{3,11},{4,12},{5,13},{6,14},{7,15},{8,16},{9,17... | collective-permute-start | bytes 1572872 | tf_op jit(solution)/shard_map/ppermute | solution.py:31
  165.1 37.6 %all-to-all-start.2 = ((bf16[4,512,512]{2,1,0:T(8,128)(2,1)}), bf16[4,512,512]{2,1,0:T(8,128)(2,1)}, u32[]{:S(2)}, u32[]{:S(2)}) async-start(bf16[4,512,512]{2,1,0:T(8,128)(2,1)} %copy-done), calls=%async_computation.2 | async-start | bytes 4194304 | tf_op jit(solution)/shard_map/all_to_all | solution.py:338
  176.0 51.6 %collective-permute-start.14 = (bf16[512,512]{1,0:T(8,128)(2,1)}, bf16[512,512]{1,0:T(8,128)(2,1)}, u32[]{:S(2)}, u32[]{:S(2)}) collective-permute-start(bf16[512,512]{1,0:T(8,128)(2,1)} %fusion.10), channel_id=1, source_target_pairs={{0,2},{1,67},{2,4},{3,69},{4,6},{5,71},{6,0},{7,65},{8,10},{9,75},... | collective-permute-start | bytes 1572872 | tf_op jit(solution)/shard_map/ppermute | solution.py:31
  195.9 11.4 %collective-permute-start.15 = (bf16[48,4096]{1,0:T(8,128)(2,1)S(1)}, bf16[48,4096]{1,0:T(8,128)(2,1)}, u32[]{:S(2)}, u32[]{:S(2)}) collective-permute-start(bf16[48,4096]{1,0:T(8,128)(2,1)S(1)} %get-tuple-element.44), channel_id=1, source_target_pairs={{0,6},{1,7},{2,0},{3,1},{4,2},{5,3},{6,4},{7,5},{8,14},{9,15},{10,... | collective-permute-start | bytes 1179656 | tf_op jit(solution)/shard_map/ppermute | solution.py:31
  196.0 29.7 %collective-permute-start.16 = (bf16[48,4096]{1,0:T(8,128)(2,1)S(1)}, bf16[48,4096]{1,0:T(8,128)(2,1)}, u32[]{:S(2)}, u32[]{:S(2)}) collective-permute-start(bf16[48,4096]{1,0:T(8,128)(2,1)S(1)} %get-tuple-element.45), channel_id=1, source_target_pairs={{0,7},{1,6},{2,1},{3,0},{4,3},{5,2},{6,5},{7,4},{8,15},{9,14},{10,... | collective-permute-start | bytes 1179656 | tf_op jit(solution)/shard_map/ppermute | solution.py:31
  202.7 25.0 %copy-start.9 = (f32[512,1024]{1,0:T(8,128)S(1)}, f32[512,1024]{1,0:T(8,128)}, u32[]{:S(2)}) copy-start(f32[512,1024]{1,0:T(8,128)} %fusion.12) | copy-start | bytes 6291460
  205.0 22.6 %collective-permute-start.5 = (bf16[512,512]{1,0:T(8,128)(2,1)S(1)}, bf16[512,512]{1,0:T(8,128)(2,1)S(1)}, u32[]{:S(2)}, u32[]{:S(2)}) collective-permute-start(bf16[512,512]{1,0:T(8,128)(2,1)S(1)} %reduce_sum.50), channel_id=1, source_target_pairs={{0,2},{1,66},{2,4},{3,68},{4,6},{5,70},{6,0},{7,64},{8,10},{9,74},... | collective-permute-start | bytes 1572872 | tf_op jit(solution)/shard_map/ppermute | solution.py:31
  (10 other events, 42.0 us)

commit v4 on v3

--- a/solution.py
+++ b/solution.py
@@ -163,33 +163,25 @@
     )(places, *gathered, *gathered)
 
 
-def pack_kernel(saved, key, value, out):
-    rows, piece = saved.shape
-    out[0, :rows, :] = saved[...]
-    start = rows
-    for source in (key, value):
-        for column in range(0, source.shape[1], piece):
-            out[0, start : start + source.shape[0], :] = source[:, column : column + piece]
-            start += source.shape[0]
-
-
-def packed(saved, key, value, replicas):
+def pack_kernel(saved, out):
+    piece = out.shape[-1]
+    for half in range(2):
+        for z in range(RING):
+            start = (2 * z + half) * piece
+            out[half, 0, z] = saved[:, start : start + piece]
+
+
+def packed(saved, replicas):
     rows, features = saved.shape
-    piece, share, width = features // replicas, rows // replicas, key.shape[1]
-    height = rows + 2 * width // piece * share
-
-    def column(i):
-        x, z = i // RING, i % RING
-        return 2 * (x % 2 * RING + z) + x // 2
-
-    few = pl.BlockSpec((share, width), lambda i: (i, 0))
-    return pl.pallas_call(
+    piece = features // replicas
+    out = pl.pallas_call(
         pack_kernel,
-        out_shape=jax.ShapeDtypeStruct((replicas, height, piece), saved.dtype),
-        grid=(replicas,),
-        in_specs=[pl.BlockSpec((rows, piece), lambda i: (0, column(i))), few, few],
-        out_specs=pl.BlockSpec((1, height, piece), lambda i: (i, 0, 0)),
-    )(saved, key, value)
+        out_shape=jax.ShapeDtypeStruct((2, 2, RING, rows, piece), saved.dtype),
+        grid=(2,),
+        in_specs=[pl.BlockSpec((rows, features // 2), lambda i: (0, i))],
+        out_specs=pl.BlockSpec((2, 1, RING, rows, piece), lambda i: (0, i, 0, 0, 0)),
+    )(saved)
+    return out.reshape(replicas, rows, piece)
 
 
 def on_device(
@@ -224,12 +216,12 @@
     share = rows // replicas
 
     saved = backup_stream[0]
-    saved_pieces = packed(saved, backup_key_cot[0], backup_value_cot[0], replicas)
+    saved_cots = jnp.concatenate([backup_key_cot[0], backup_value_cot[0]], axis=1)
+    share_rows = lax.all_to_all(saved_cots.reshape(replicas, share, -1), "dp", 0, 0)
+    share_rows = lax.dynamic_index_in_dim(share_rows, keeper, 0, keepdims=False)
+
     own_positions = lax.dynamic_slice_in_dim(positions[0], member * rows, rows, 0)
-    key_first, saved_pieces = lax.optimization_barrier((key_cot[0], saved_pieces))
-    cots = derotate(key_first, value_cot[0], own_positions)
-    dead = lax.all_to_all(saved_pieces, "dp", 0, 0)
-    dead = lax.dynamic_index_in_dim(dead, keeper, 0, keepdims=False)
+    cots = derotate(key_cot[0], value_cot[0], own_positions)
     near = moved(cots, lambda x, z, s, t: (x, z, s - 1, t))
     far = moved(cots, lambda x, z, s, t: (x, z, s - 1, 1 - t))
 
@@ -241,59 +233,51 @@
     scales = lax.rsqrt(squares / D + EPSILON)
     own_scale = scales[:rows, None]
     normed = (values * own_scale * norm_gain).astype(jnp.bfloat16)
-
-    gathered = []
-    for step in (2, 1, 3, 0):
-        there = (at_x + step) % RING
-        start = (2 * (there % 2) + there // 2) * fourth
-        tile = jnp.concatenate(
-            [lax.dynamic_slice_in_dim(normed, start, fourth, 1), near[:, width:], far[:, width:]],
-            axis=1,
-        )
-        gathered.append((tile, step))
-    first = side == 0
-    key_heads = [
-        jnp.where(first, near[:, :width], far[:, :width]),
-        jnp.where(first, far[:, :width], near[:, :width]),
-    ]
-    outgoing = jnp.stack(
-        [
-            jnp.concatenate(
-                [normed[:, z * block : (z + 1) * block], normed[:, (RING + z) * block : (RING + z + 1) * block]]
-                + key_heads,
-                axis=1,
-            )
-            for z in range(RING)
-        ]
-    )
-    tiles = [tile for tile, _ in gathered]
-    outgoing, dead, _ = lax.optimization_barrier((outgoing, dead, tiles))
-    gathered = [
-        moved(tile, lambda x, z, s, t, step=step: (x + step, z, s, t))[None] if step else tile[None]
-        for tile, (_, step) in zip(tiles, gathered)
-    ]
-    z_rings = [[RING * x + z for z in range(RING)] for x in range(RING)]
-    x_rings = [[RING * x + z for x in range(RING)] for z in range(RING)]
-    arrived = lax.all_to_all(outgoing, "dp", 0, 0, axis_index_groups=z_rings)
-
-    late_cots, tiles = lax.optimization_barrier((cots, tiles))
-    ones = jnp.ones((rows, 1), jnp.float32)
-    across, straight = feature_halves(late_cots, ones, w_key[0], w_value[0], side)
-    across, straight, dead = lax.optimization_barrier((across, straight, dead))
-    across = moved(across, lambda x, z, s, t: (x, z, s - 1, 1 - t))
-    straight = moved(straight, lambda x, z, s, t: (x, z, s - 1, t))
-    arrived, across, straight = lax.optimization_barrier((arrived, across, straight))
-    feature = straight.astype(jnp.float32) + across.astype(jnp.float32)
-    stream_grad = (own_scale * (norm_gain * feature)).astype(jnp.bfloat16)
 
     saved_scale = scales[rows:]
     scale_high = saved_scale.astype(jnp.bfloat16)
     scale_low = (saved_scale - scale_high.astype(jnp.float32)).astype(jnp.bfloat16)
     factors = jnp.concatenate([scale_high.reshape(share, -1), scale_low.reshape(share, -1)], axis=1)
     factors = jnp.pad(factors, ((0, 0), (0, HEAD - factors.shape[1])))
-    dead_share = dead[rows:].reshape(-1, share, piece).transpose(1, 0, 2).reshape(share, -1)
-    shares = lax.all_gather(jnp.concatenate([dead_share, factors], axis=1), "dp")
-    gathered, shares = lax.optimization_barrier((gathered, shares))
+    shares = jnp.concatenate([share_rows, factors], axis=1)
+    shares = lax.all_to_all(jnp.broadcast_to(shares, (replicas, *shares.shape)), "dp", 0, 0)
+
+    steps = (2, 1, 3, 0)
+
+    def along_x(tile, step):
+        return moved(tile, lambda x, z, s, t: (x + step, z, s, t)) if step else tile
+
+    def along_z(tile, step):
+        return moved(tile, lambda x, z, s, t: (x, z + step, s, t)) if step else tile
+
+    value_tiles, key_tiles = [], []
+    for step in steps:
+        there = (at_x + step) % RING
+        start = (2 * (there % 2) + there // 2) * fourth
+        value_tiles.append(
+            jnp.concatenate(
+                [lax.dynamic_slice_in_dim(normed, start, fourth, 1), near[:, width:], far[:, width:]],
+                axis=1,
+            )
+        )
+        start = (at_z + step) % RING * block
+        key_tiles.append(
+            jnp.concatenate(
+                [
+                    lax.dynamic_slice_in_dim(normed, start, block, 1),
+                    lax.dynamic_slice_in_dim(normed, RING * block + start, block, 1),
+                    near[:, :width],
+                    far[:, :width],
+                ],
+                axis=1,
+            )
+        )
+
+    saved_pieces, shares, _ = lax.optimization_barrier(
+        (packed(saved, replicas), shares, (value_tiles, key_tiles))
+    )
+    dead = lax.all_to_all(saved_pieces, "dp", 0, 0)
+
     dead_raw = shares[:, :, : 2 * width].reshape(rows, 2 * width)
     factors = lax.dynamic_index_in_dim(shares[:, :, 2 * width :], keeper, 0, keepdims=False)
     factors = factors.astype(jnp.float32)
@@ -301,9 +285,52 @@
     dead_positions = lax.dynamic_slice_in_dim(positions[0], fallen * rows, rows, 0)
     dead_cots = derotate(dead_raw[:, :width], dead_raw[:, width:], dead_positions)
 
+    selection = slot_selection(plan_row, member, capacity_blocks, rows)
+    slot_cots = jnp.dot(
+        selection.astype(jnp.bfloat16), dead_cots, preferred_element_type=jnp.float32
+    ).astype(jnp.bfloat16)
+    slot_scale = jnp.sum(selection * jnp.reshape(dead_scale, (1, rows)), axis=1, keepdims=True)
+    across, straight = feature_halves(
+        jnp.concatenate([cots, slot_cots], axis=0),
+        jnp.concatenate([jnp.ones((rows, 1), jnp.float32), slot_scale], axis=0),
+        w_key[0],
+        w_value[0],
+        side,
+    )
+    value_tiles[0], _ = lax.optimization_barrier((value_tiles[0], (across, straight)))
+    across = moved(across, lambda x, z, s, t: (x, z, s - 1, 1 - t))
+    straight = moved(straight, lambda x, z, s, t: (x, z, s - 1, t))
+
+    key_rows = [along_z(tile, step)[None] for tile, step in zip(key_tiles, steps)]
+    value_rows = [along_x(tile, step)[None] for tile, step in zip(value_tiles, steps)]
+
+    there = [(at_z + step) % RING for step in steps]
+    value_parts = products(
+        value_rows, block, [r % 2 for r in there], [(r // 2) ^ (at_x // 2) for r in there]
+    )
+    value_total = sum(
+        along_z(value_parts[place], step).astype(jnp.float32) for place, step in enumerate(steps)
+    )
+    grad_value = moved(
+        value_total.astype(jnp.bfloat16),
+        lambda x, z, s, t: (2 * t + x % 2, 2 * (x // 2) + z % 2, s + 1, t ^ (z // 2) ^ (x // 2)),
+    )
+    static = [jnp.int32(r) for r in range(RING)]
+    key_parts = products(key_rows, block, [r % 2 for r in static], [(r // 2) ^ side for r in static])
+    x_rings = [[RING * x + z for x in range(RING)] for z in range(RING)]
+    parts = lax.all_to_all(key_parts, "dp", 0, 0, axis_index_groups=x_rings)
+    key_total = jnp.sum(parts.astype(jnp.float32), axis=0).astype(jnp.bfloat16)
+    key_total, across, straight = lax.optimization_barrier((key_total, across, straight))
+    grad_key = moved(key_total, lambda x, z, s, t: (2 * t + x % 2, z, s + 1, x // 2))
+
+    feature = norm_gain * (straight.astype(jnp.float32) + across.astype(jnp.float32))
+    stream_grad = (own_scale * feature[:rows]).astype(jnp.bfloat16)
+    spill_grad = feature[rows:].astype(jnp.bfloat16)
+
     start = (at_x % 2 * RING + at_z) * block + at_x // 2 * piece
+    dead = lax.dynamic_index_in_dim(dead, keeper, 0, keepdims=False)
     dead_piece = (
-        dead[:rows].astype(jnp.float32) * dead_scale * lax.dynamic_slice_in_dim(norm_gain, start, piece, 0)
+        dead.astype(jnp.float32) * dead_scale * lax.dynamic_slice_in_dim(norm_gain, start, piece, 0)
     ).astype(jnp.bfloat16)
     sent = moved(
         dead_piece, lambda x, z, s, t: (x, z, s, 1 - t) if x // 2 == t else (x + 2, z, s, t)
@@ -316,42 +343,8 @@
         [jnp.where(home == 0, same, other), jnp.where(home == 0, other, same)], axis=1
     )
     dead_part = lax.dot_general(dead_block, dead_cots, TN, preferred_element_type=jnp.float32)
-
-    steps = (2, 1, 3, 0)
-    there = [(at_z + step) % RING for step in steps]
-    value_parts = products(
-        gathered, block, [r % 2 for r in there], [(r // 2) ^ (at_x // 2) for r in there]
-    )
-    total = None
-    for place, step in enumerate(steps):
-        part = value_parts[place]
-        if step:
-            part = moved(part, lambda x, z, s, t, step=step: (x, z + step, s, t))
-        part = part.astype(jnp.float32)
-        total = part if total is None else total + part
-    grad_value = moved(
-        total.astype(jnp.bfloat16),
-        lambda x, z, s, t: (2 * t + x % 2, 2 * (x // 2) + z % 2, s + 1, t ^ (z // 2) ^ (x // 2)),
-    )
-    static = [jnp.int32(r) for r in range(RING)]
-    key_parts = products([arrived], block, [r % 2 for r in static], [r // 2 for r in static])
-    parts = lax.all_to_all(key_parts, "dp", 0, 0, axis_index_groups=x_rings)
-    grad_key = jnp.sum(parts.astype(jnp.float32), axis=0).astype(jnp.bfloat16)
-    grad_key = moved(grad_key, lambda x, z, s, t: (2 * t + x % 2, z, s + 1, x // 2))
     grad_key = grad_key.astype(jnp.float32) + dead_part[:, :width]
     grad_value = grad_value.astype(jnp.float32) + dead_part[:, width:]
-
-    selection = slot_selection(plan_row, member, capacity_blocks, rows)
-    slot_cots = jnp.dot(
-        selection.astype(jnp.bfloat16), dead_cots, preferred_element_type=jnp.float32
-    ).astype(jnp.bfloat16)
-    slot_scale = jnp.sum(selection * jnp.reshape(dead_scale, (1, rows)), axis=1, keepdims=True)
-    slot_cots, _ = lax.optimization_barrier((slot_cots, (key_parts, value_parts)))
-    across, straight = feature_halves(slot_cots, slot_scale, w_key[0], w_value[0], side)
-    across = moved(across, lambda x, z, s, t: (x, z, s - 1, 1 - t))
-    straight = moved(straight, lambda x, z, s, t: (x, z, s - 1, t))
-    feature = straight.astype(jnp.float32) + across.astype(jnp.float32)
-    spill_grad = (norm_gain * feature).astype(jnp.bfloat16)
 
     return grad_key[None], grad_value[None], stream_grad[None], spill_grad[None]
 

time: 235 us -> 204 us (0.87); the launches traced: 230 us -> 202 us
  blocking collectives: 36 us -> 0 us
  Pallas kernels: 49.1 us -> 32.1 us
  waiting for transfers between devices: 45.1 us -> 61.1 us
  starting transfers between devices: 55.1 us -> 61.5 us
  local copies, waits for them, and re-layouts: 11.9 us -> 16.4 us
    ppermute x17 -> x18, waiting for transfers between devices: 21.7 us -> 58.5 us  [moved(): return lax.ppermute(block, AXES, route)]
    all_gather x1 -> x0, blocking collectives: 36 us -> none  [on_device(): lax.all_gather(jnp.concatenate([dead_share, factors], axis=1), 'dp')]
    all_to_all x1, waiting for transfers between devices: 23.5 us -> 0.01 us  [on_device(): dead = lax.all_to_all(saved_pieces, 'dp', 0, 0)]
    pallas_call x2 -> x1, Pallas kernels: 24.1 us -> 13.9 us  [feature_halves(): pl.pallas_call(feature_kernel, out_shape=(result, result), in_specs=[pl.B...]
    pallas_call x1, Pallas kernels: 9.85 us -> 2.78 us  [packed(): pl.pallas_call(pack_kernel, out_shape=jax.ShapeDtypeStruct((2, 2, RING, r...]
    all_to_all x1 -> x2, starting transfers between devices: 4.9 us -> 11.9 us  [the longest x1 7.65 us: on_device(): lax.all_to_all(saved_cots.reshape(replicas, share, -1), 'dp', 0, 0)]
    mul x0 -> x1, other arithmetic: none -> 3.39 us  [on_device(): norm_gain * (straight.astype(jnp.float32) + across.astype(jnp.float32))]
    all_to_all x1, starting transfers between devices: 7.64 us -> 4.44 us  [on_device(): dead = lax.all_to_all(saved_pieces, 'dp', 0, 0)]
  transfers between devices with their start and end apart: 20 -> 22, of which waited for: 4 -> 6; matrix products, arithmetic and copies ran while one was open for 12% -> 18% of each run, Pallas kernels for 16% -> 15%
where the time goes in v4:
time: 204 us; the launch traced here: 202 us
  starting transfers between devices  61.5 us (30%)
  waiting for transfers between devices  61.1 us (30%)
  Pallas kernels  32.1 us (16%)
  other arithmetic  26.4 us (13%)
  local copies, waits for them, and re-layouts  16.4 us (8%)
  between operations  2.66 us (1%)
    ppermute x18, waiting for transfers between devices, moved(): return lax.ppermute(block, AXES, route)  58.5 us
    ppermute x18, starting transfers between devices, moved(): return lax.ppermute(block, AXES, route)  40.6 us
    pallas_call x1, Pallas kernels, feature_halves(): pl.pallas_call(feature_kernel, out_shape=(result, result), in_specs=[pl.B...  13.9 us
    pallas_call x2, Pallas kernels, products(): pl.pallas_call(product_kernel, out_shape=jax.ShapeDtypeStruct((RING, bloc...  11.2 us
    all_to_all x1, starting transfers between devices, on_device(): lax.all_to_all(saved_cots.reshape(replicas, share, -1), 'dp', 0, 0)  7.65 us
    all_to_all x1, starting transfers between devices, on_device(): parts = lax.all_to_all(key_parts, 'dp', 0, 0, axis_index_groups=x_rings)  4.59 us
    all_to_all x1, starting transfers between devices, on_device(): dead = lax.all_to_all(saved_pieces, 'dp', 0, 0)  4.44 us
    all_to_all x1, starting transfers between devices, on_device(): lax.all_to_all(jnp.broadcast_to(shares, (replicas, *shares.shape)), 'dp',...  4.25 us
  transfers between devices with their start and end apart: 22, of which 6 were waited for; matrix products, arithmetic and copies ran while one was open for 18% of the time, Pallas kernels for 15%

profile of v4, /device:TPU:25, one launch (start us, length us, event | category | flops | bytes accessed | tf_op | source)
XLA Modules:
  0.0 201.8 jit_solution(693723164872758143)
XLA Ops:
  5.1 2.1 %shard_map.147 = bf16[256,1024]{1,0:T(8,128)(2,1)} custom-call(bf16[256,512]{1,0:T(8,128)(2,1)} %bitcast.88, bf16[256,512]{1,0:T(8,128)(2,1)} %bitcast.89, f32[256,128]{1,0:T(8,128)} %get-tuple-element.63.cosine, f32[256,128]{1,0:T(8,128)} %get-tuple-element.64.sine), custom_call_target="tpu_custom_call" | custom-call | tf_op jit(solution)/shard_map/pallas_call | solution.py:60
  8.8 3.1 %fusion = (f32[256]{0:T(256)S(1)}, f32[256]{0:T(256)S(1)}) fusion(bf16[1,256,4096]{2,1,0:T(8,128)(2,1)} %param.12, bf16[1,256,4096]{2,1,0:T(8,128)(2,1)} %param.13), kind=kLoop, calls=%fused_computation.3 | loop fusion | flops 6290944 | bytes 4196352 | tf_op jit(solution)/shard_map/reduce_sum | solution.py:231
  14.9 7.6 %all-to-all-start.1 = ((bf16[16,16,1024]{2,1,0:T(8,128)(2,1)}), bf16[16,16,1024]{2,1,0:T(8,128)(2,1)}, u32[]{:S(2)}, u32[]{:S(2)}) async-start(bf16[16,16,1024]{2,1,0:T(8,128)(2,1)} %pad_maximum_fusion.17), calls=%async_computation.1 | async-start | bytes 1048576 | tf_op jit(solution)/shard_map/all_to_all | solution.py:220
  23.9 2.8 %shard_map.149 = bf16[2,2,4,256,256]{4,3,2,1,0:T(8,128)(2,1)} custom-call(bf16[256,4096]{1,0:T(8,128)(2,1)} %bitcast.85), custom_call_target="tpu_custom_call" | custom-call | tf_op jit(solution)/shard_map/pallas_call | solution.py:177
  29.3 2.5 %all-to-all-done.1 = bf16[16,16,1024]{2,1,0:T(8,128)(2,1)} async-done(((bf16[16,16,1024]{2,1,0:T(8,128)(2,1)}), bf16[16,16,1024]{2,1,0:T(8,128)(2,1)}, u32[]{:S(2)}, u32[]{:S(2)}) %all-to-all-start.1) | async-done | bytes 524320 | tf_op jit(solution)/shard_map/all_to_all | solution.py:220
  33.4 4.2 %all-to-all-start.2 = ((bf16[16,16,1152]{2,1,0:T(8,128)(2,1)}), bf16[16,16,1152]{2,1,0:T(8,128)(2,1)}, u32[]{:S(2)}, u32[]{:S(2)}) async-start(bf16[16,16,1152]{2,1,0:T(8,128)(2,1)} %broadcast_in_dim.99), calls=%async_computation.2 | async-start | bytes 1179648 | tf_op jit(solution)/shard_map/all_to_all | solution.py:243
  53.4 4.4 %all-to-all-start.3 = ((bf16[16,256,256]{2,1,0:T(8,128)(2,1)}), bf16[16,256,256]{2,1,0:T(8,128)(2,1)}, u32[]{:S(2)}, u32[]{:S(2)}) async-start(bf16[16,256,256]{2,1,0:T(8,128)(2,1)} %bitcast.86), calls=%async_computation.3 | async-start | bytes 4194304 | tf_op jit(solution)/shard_map/all_to_all | solution.py:279
  64.5 13.9 %shard_map.151 = (bf16[304,4096]{1,0:T(8,128)(2,1)}, bf16[304,4096]{1,0:T(8,128)(2,1)}) custom-call(s32[1]{0:T(128)} %bitcast.12.half, bf16[304,1024]{1,0:T(8,128)(2,1)S(1)} %pad_maximum_fusion.16.cots, f32[304,1]{1,0:T(8,128)S(1)} %concatenate.79.scale, bf16[8192,512]{1,0:T(8,128)(2,1)} %bitcast.83, bf16[8192,512]{1,0:T(8,128)(2,1)} %bitcast.84), custom_call_target="tpu_custom_call" | custom-call | tf_op jit(solution)/shard_map/pallas_call | solution.py:112
  78.4 2.7 %collective-permute-start.11 = (bf16[256,2048]{1,0:T(8,128)(2,1)}, bf16[256,2048]{1,0:T(8,128)(2,1)}, u32[]{:S(2)}, u32[]{:S(2)}) collective-permute-start(bf16[256,2048]{1,0:T(8,128)(2,1)} %get-tuple-element.17), channel_id=1, source_target_pairs={{0,64},{1,65},{2,66},{3,67},{4,68},{5,69},{6,70},{7,71},{8,72},{9,... | collective-permute-start | bytes 3145736 | tf_op jit(solution)/shard_map/ppermute | solution.py:31
  81.2 6.4 %collective-permute-start.6 = (bf16[304,4096]{1,0:T(8,128)(2,1)}, bf16[304,4096]{1,0:T(8,128)(2,1)}, u32[]{:S(2)}, u32[]{:S(2)}) collective-permute-start(bf16[304,4096]{1,0:T(8,128)(2,1)} %get-tuple-element.13), channel_id=1, source_target_pairs={{0,7},{1,6},{2,1},{3,0},{4,3},{5,2},{6,5},{7,4},{8,15},{9,14},{10,... | collective-permute-start | bytes 7471112 | tf_op jit(solution)/shard_map/ppermute | solution.py:31
  87.6 27.5 %collective-permute-done.3 = bf16[256,2048]{1,0:T(8,128)(2,1)} collective-permute-done((bf16[256,2048]{1,0:T(8,128)(2,1)}, bf16[256,2048]{1,0:T(8,128)(2,1)}, u32[]{:S(2)}, u32[]{:S(2)}) %collective-permute-start.3) | collective-permute-done | bytes 1048608 | tf_op jit(solution)/shard_map/ppermute | solution.py:31
  117.1 5.4 %shard_map.148 = bf16[4,512,512]{2,1,0:T(8,128)(2,1)S(1)} custom-call(s32[2,4]{1,0:T(2,128)S(1)} %pad_add_fusion.places, bf16[1,256,2048]{2,1,0:T(8,128)(2,1)} %bitcast.8.refs_0_.refs_4_, bf16[1,256,2048]{2,1,0:T(8,128)(2,1)S(1)} %bitcast.81, bf16[1,256,2048]{2,1,0:T(8,128)(2,1)} %bitcast.10.refs_2_.refs_6_, ...), custom_call_target="tpu_custom_call" | custom-call | tf_op jit(solution)/shard_map/pallas_call | solution.py:153
  123.8 5.8 %shard_map.152 = bf16[4,512,512]{2,1,0:T(8,128)(2,1)S(1)} custom-call(s32[2,4]{1,0:T(2,128)S(1)} %pad_add_fusion.1.places, bf16[1,256,2048]{2,1,0:T(8,128)(2,1)} %bitcast.38.refs_0_.refs_4_, bf16[1,256,2048]{2,1,0:T(8,128)(2,1)} %bitcast.39.refs_1_.refs_5_, bf16[1,256,2048]{2,1,0:T(8,128)(2,1)} %bitcast.40.refs_2_.refs_6_, ...), custom_call_target="tpu_custom_call" | custom-call | tf_op jit(solution)/shard_map/pallas_call | solution.py:153
  131.0 4.6 %all-to-all-start = ((bf16[4,512,512]{2,1,0:T(8,128)(2,1)}), bf16[4,512,512]{2,1,0:T(8,128)(2,1)}, u32[]{:S(2)}, u32[]{:S(2)}) async-start(bf16[4,512,512]{2,1,0:T(8,128)(2,1)} %copy-done.2), calls=%async_computation | async-start | bytes 4194304 | tf_op jit(solution)/shard_map/all_to_all | solution.py:321
  136.8 3.0 %collective-permute-start.14 = (bf16[512,512]{1,0:T(8,128)(2,1)}, bf16[512,512]{1,0:T(8,128)(2,1)S(1)}, u32[]{:S(2)}, u32[]{:S(2)}) collective-permute-start(bf16[512,512]{1,0:T(8,128)(2,1)} %get-tuple-element.24), channel_id=1, source_target_pairs={{0,16},{1,17},{2,18},{3,19},{4,20},{5,21},{6,22},{7,23},{8,24},{9,... | collective-permute-start | bytes 1572872 | tf_op jit(solution)/shard_map/ppermute | solution.py:31
  142.6 9.6 %collective-permute-done.14 = bf16[512,512]{1,0:T(8,128)(2,1)S(1)} collective-permute-done((bf16[512,512]{1,0:T(8,128)(2,1)}, bf16[512,512]{1,0:T(8,128)(2,1)S(1)}, u32[]{:S(2)}, u32[]{:S(2)}) %collective-permute-start.14) | collective-permute-done | bytes 524320 | tf_op jit(solution)/shard_map/ppermute | solution.py:31
  152.2 5.8 %collective-permute-start.10 = (bf16[256,256]{1,0:T(8,128)(2,1)S(1)}, bf16[256,256]{1,0:T(8,128)(2,1)S(1)}, u32[]{:S(2)}, u32[]{:S(2)}) collective-permute-start(bf16[256,256]{1,0:T(8,128)(2,1)S(1)} %fusion.14), channel_id=1, source_target_pairs={{1,64},{3,66},{5,68},{7,70},{9,72},{11,74},{13,76},{15,78},{17,80}... | collective-permute-start | bytes 393224 | tf_op jit(solution)/shard_map/ppermute | solution.py:31
  158.0 7.2 %collective-permute-done.16 = bf16[512,512]{1,0:T(8,128)(2,1)} collective-permute-done((bf16[512,512]{1,0:T(8,128)(2,1)}, bf16[512,512]{1,0:T(8,128)(2,1)}, u32[]{:S(2)}, u32[]{:S(2)}) %collective-permute-start.16) | collective-permute-done | bytes 524320 | tf_op jit(solution)/shard_map/ppermute | solution.py:31
  165.2 2.6 %collective-permute-start.9 = (bf16[256,256]{1,0:T(8,128)(2,1)S(1)}, bf16[256,256]{1,0:T(8,128)(2,1)S(1)}, u32[]{:S(2)}, u32[]{:S(2)}) collective-permute-start(bf16[256,256]{1,0:T(8,128)(2,1)S(1)} %fusion.14), channel_id=1, source_target_pairs={{0,1},{1,65},{2,3},{3,67},{4,5},{5,69},{6,7},{7,71},{8,9},{9,73},{... | collective-permute-start | bytes 393224 | tf_op jit(solution)/shard_map/ppermute | solution.py:31
  167.8 2.3 %fusion.7 = bf16[512,512]{1,0:T(8,128)(2,1)} fusion(bf16[512,512]{1,0:T(8,128)(2,1)} %collective-permute-done.16, bf16[512,512]{1,0:T(8,128)(2,1)} %collective-permute-done.15, bf16[512,512]{1,0:T(8,128)(2,1)S(1)} %collective-permute-done.14, bf16[4,512,512]{2,1,0:T(8,128)(2,1)S(1)} %copy-done.1), kind=kLoop, calls=%fused_computation.32 | loop fusion | flops 2097152 | bytes 2621440 | tf_op jit(solution)/shard_map/convert_element_type | solution.py:315
  173.5 2.2 %reduce_sum.50 = bf16[512,512]{1,0:T(8,128)(2,1)S(1)} reduce(bf16[4,512,512]{2,1,0:T(8,128)(2,1)} %all-to-all-done, bf16[]{:T(256)} %constant.353.clone.1), dimensions={0}, to_apply=%region_2.3 | reduce | flops 786432 | bytes 2621442 | tf_op jit(solution)/shard_map/reduce_sum | solution.py:322
  175.7 4.3 %collective-permute-start.8 = (bf16[512,512]{1,0:T(8,128)(2,1)S(1)}, bf16[512,512]{1,0:T(8,128)(2,1)S(1)}, u32[]{:S(2)}, u32[]{:S(2)}) collective-permute-start(bf16[512,512]{1,0:T(8,128)(2,1)S(1)} %reduce_sum.50), channel_id=1, source_target_pairs={{0,2},{1,66},{2,4},{3,68},{4,6},{5,70},{6,0},{7,64},{8,10},{9,74},... | collective-permute-start | bytes 1572872 | tf_op jit(solution)/shard_map/ppermute | solution.py:31
  180.0 3.4 %add_multiply_fusion = f32[304,4096]{1,0:T(8,128)S(1)} fusion(bf16[304,4096]{1,0:T(8,128)(2,1)} %collective-permute-done.6, bf16[304,4096]{1,0:T(8,128)(2,1)} %collective-permute-done.7, f32[4096]{0:T(1024)S(1)} %copy-done.11), kind=kLoop, calls=%fused_computation.2 | loop fusion | flops 4980736 | bytes 9977856 | tf_op jit(solution)/shard_map/mul | solution.py:326
  185.9 13.9 %collective-permute-done.17 = bf16[512,512]{1,0:T(8,128)(2,1)S(1)} collective-permute-done((bf16[512,512]{1,0:T(8,128)(2,1)}, bf16[512,512]{1,0:T(8,128)(2,1)S(1)}, u32[]{:S(2)}, u32[]{:S(2)}) %collective-permute-start.17) | collective-permute-done | bytes 524320 | tf_op jit(solution)/shard_map/ppermute | solution.py:31
  (112 shorter events, 51.8 us)
Async XLA Ops:
  7.3 30.4 %collective-permute-start.2 = (bf16[256,1024]{1,0:T(8,128)(2,1)}, bf16[256,1024]{1,0:T(8,128)(2,1)}, u32[]{:S(2)}, u32[]{:S(2)}) collective-permute-start(bf16[256,1024]{1,0:T(8,128)(2,1)} %shard_map.147), channel_id=1, source_target_pairs={{0,7},{1,6},{2,1},{3,0},{4,3},{5,2},{6,5},{7,4},{8,15},{9,14},{10,... | collective-permute-start | bytes 1572872 | tf_op jit(solution)/shard_map/ppermute | solution.py:31
  8.8 30.0 %collective-permute-start.1 = (bf16[256,1024]{1,0:T(8,128)(2,1)}, bf16[256,1024]{1,0:T(8,128)(2,1)}, u32[]{:S(2)}, u32[]{:S(2)}) collective-permute-start(bf16[256,1024]{1,0:T(8,128)(2,1)} %shard_map.147), channel_id=1, source_target_pairs={{0,6},{1,7},{2,0},{3,1},{4,2},{5,3},{6,4},{7,5},{8,14},{9,15},{10,... | collective-permute-start | bytes 1572872 | tf_op jit(solution)/shard_map/ppermute | solution.py:31
  11.9 14.8 %collective-permute-start = (f32[512]{0:T(512)S(1)}, f32[512]{0:T(512)S(1)}, u32[]{:S(2)}, u32[]{:S(2)}) collective-permute-start(f32[512]{0:T(512)S(1)} %pad_maximum_fusion.19), channel_id=1, source_target_pairs={{0,1},{1,0},{2,3},{3,2},{4,5},{5,4},{6,7},{7,6},{8,9},{9,8},{10,11... | collective-permute-start | bytes 6152 | tf_op jit(solution)/shard_map/ppermute | solution.py:31
  14.9 16.9 %all-to-all-start.1 = ((bf16[16,16,1024]{2,1,0:T(8,128)(2,1)}), bf16[16,16,1024]{2,1,0:T(8,128)(2,1)}, u32[]{:S(2)}, u32[]{:S(2)}) async-start(bf16[16,16,1024]{2,1,0:T(8,128)(2,1)} %pad_maximum_fusion.17), calls=%async_computation.1 | async-start | bytes 1048576 | tf_op jit(solution)/shard_map/all_to_all | solution.py:220
  33.4 17.2 %all-to-all-start.2 = ((bf16[16,16,1152]{2,1,0:T(8,128)(2,1)}), bf16[16,16,1152]{2,1,0:T(8,128)(2,1)}, u32[]{:S(2)}, u32[]{:S(2)}) async-start(bf16[16,16,1152]{2,1,0:T(8,128)(2,1)} %broadcast_in_dim.99), calls=%async_computation.2 | async-start | bytes 1179648 | tf_op jit(solution)/shard_map/all_to_all | solution.py:243
  41.8 36.6 %collective-permute-start.4 = (bf16[256,2048]{1,0:T(8,128)(2,1)}, bf16[256,2048]{1,0:T(8,128)(2,1)S(1)}, u32[]{:S(2)}, u32[]{:S(2)}) collective-permute-start(bf16[256,2048]{1,0:T(8,128)(2,1)} %get-tuple-element.44), channel_id=1, source_target_pairs={{0,8},{1,9},{2,10},{3,11},{4,12},{5,13},{6,14},{7,15},{8,16},{9,17... | collective-permute-start | bytes 3145736 | tf_op jit(solution)/shard_map/ppermute | solution.py:31
  43.0 38.2 %collective-permute-start.5 = (bf16[256,2048]{1,0:T(8,128)(2,1)}, bf16[256,2048]{1,0:T(8,128)(2,1)}, u32[]{:S(2)}, u32[]{:S(2)}) collective-permute-start(bf16[256,2048]{1,0:T(8,128)(2,1)} %get-tuple-element.45), channel_id=1, source_target_pairs={{0,24},{1,25},{2,26},{3,27},{4,28},{5,29},{6,30},{7,31},{8,0},{9,1... | collective-permute-start | bytes 3145736 | tf_op jit(solution)/shard_map/ppermute | solution.py:31
  44.5 70.6 %collective-permute-start.3 = (bf16[256,2048]{1,0:T(8,128)(2,1)}, bf16[256,2048]{1,0:T(8,128)(2,1)}, u32[]{:S(2)}, u32[]{:S(2)}) collective-permute-start(bf16[256,2048]{1,0:T(8,128)(2,1)} %get-tuple-element.46), channel_id=1, source_target_pairs={{0,16},{1,17},{2,18},{3,19},{4,20},{5,21},{6,22},{7,23},{8,24},{9,... | collective-permute-start | bytes 3145736 | tf_op jit(solution)/shard_map/ppermute | solution.py:31
  48.0 75.9 %collective-permute-start.12 = (bf16[256,2048]{1,0:T(8,128)(2,1)}, bf16[256,2048]{1,0:T(8,128)(2,1)}, u32[]{:S(2)}, u32[]{:S(2)}) collective-permute-start(bf16[256,2048]{1,0:T(8,128)(2,1)} %get-tuple-element.40), channel_id=1, source_target_pairs={{0,32},{1,33},{2,34},{3,35},{4,36},{5,37},{6,38},{7,39},{8,40},{9,... | collective-permute-start | bytes 3145736 | tf_op jit(solution)/shard_map/ppermute | solution.py:31
  49.2 74.6 %collective-permute-start.13 = (bf16[256,2048]{1,0:T(8,128)(2,1)}, bf16[256,2048]{1,0:T(8,128)(2,1)}, u32[]{:S(2)}, u32[]{:S(2)}) collective-permute-start(bf16[256,2048]{1,0:T(8,128)(2,1)} %get-tuple-element.41), channel_id=1, source_target_pairs={{0,96},{1,97},{2,98},{3,99},{4,100},{5,101},{6,102},{7,103},{8,104... | collective-permute-start | bytes 3145736 | tf_op jit(solution)/shard_map/ppermute | solution.py:31
  53.4 77.6 %all-to-all-start.3 = ((bf16[16,256,256]{2,1,0:T(8,128)(2,1)}), bf16[16,256,256]{2,1,0:T(8,128)(2,1)}, u32[]{:S(2)}, u32[]{:S(2)}) async-start(bf16[16,256,256]{2,1,0:T(8,128)(2,1)} %bitcast.86), calls=%async_computation.3 | async-start | bytes 4194304 | tf_op jit(solution)/shard_map/all_to_all | solution.py:279
  64.5 52.5 %copy-start.13 = (s32[1,4]{1,0:T(1,128)S(1)}, s32[1,4]{1,0:T(1,128)}, u32[]{:S(2)}) copy-start(s32[1,4]{1,0:T(1,128)} %constant.331.clone.1) | copy-start | bytes 52
  78.4 45.4 %collective-permute-start.11 = (bf16[256,2048]{1,0:T(8,128)(2,1)}, bf16[256,2048]{1,0:T(8,128)(2,1)}, u32[]{:S(2)}, u32[]{:S(2)}) collective-permute-start(bf16[256,2048]{1,0:T(8,128)(2,1)} %get-tuple-element.17), channel_id=1, source_target_pairs={{0,64},{1,65},{2,66},{3,67},{4,68},{5,69},{6,70},{7,71},{8,72},{9,... | collective-permute-start | bytes 3145736 | tf_op jit(solution)/shard_map/ppermute | solution.py:31
  81.2 94.5 %collective-permute-start.6 = (bf16[304,4096]{1,0:T(8,128)(2,1)}, bf16[304,4096]{1,0:T(8,128)(2,1)}, u32[]{:S(2)}, u32[]{:S(2)}) collective-permute-start(bf16[304,4096]{1,0:T(8,128)(2,1)} %get-tuple-element.13), channel_id=1, source_target_pairs={{0,7},{1,6},{2,1},{3,0},{4,3},{5,2},{6,5},{7,4},{8,15},{9,14},{10,... | collective-permute-start | bytes 7471112 | tf_op jit(solution)/shard_map/ppermute | solution.py:31
  115.0 60.6 %collective-permute-start.7 = (bf16[304,4096]{1,0:T(8,128)(2,1)}, bf16[304,4096]{1,0:T(8,128)(2,1)}, u32[]{:S(2)}, u32[]{:S(2)}) collective-permute-start(bf16[304,4096]{1,0:T(8,128)(2,1)} %get-tuple-element.14), channel_id=1, source_target_pairs={{0,6},{1,7},{2,0},{3,1},{4,2},{5,3},{6,4},{7,5},{8,14},{9,15},{10,... | collective-permute-start | bytes 7471112 | tf_op jit(solution)/shard_map/ppermute | solution.py:31
  131.0 42.4 %all-to-all-start = ((bf16[4,512,512]{2,1,0:T(8,128)(2,1)}), bf16[4,512,512]{2,1,0:T(8,128)(2,1)}, u32[]{:S(2)}, u32[]{:S(2)}) async-start(bf16[4,512,512]{2,1,0:T(8,128)(2,1)} %copy-done.2), calls=%async_computation | async-start | bytes 4194304 | tf_op jit(solution)/shard_map/all_to_all | solution.py:321
  136.8 36.2 %copy-start.4 = (bf16[256,1024]{1,0:T(8,128)(2,1)S(1)}, bf16[256,1024]{1,0:T(8,128)(2,1)}, u32[]{:S(2)}) copy-start(bf16[256,1024]{1,0:T(8,128)(2,1)} %shard_map.150) | copy-start | bytes 1572868
  136.8 15.4 %collective-permute-start.14 = (bf16[512,512]{1,0:T(8,128)(2,1)}, bf16[512,512]{1,0:T(8,128)(2,1)S(1)}, u32[]{:S(2)}, u32[]{:S(2)}) collective-permute-start(bf16[512,512]{1,0:T(8,128)(2,1)} %get-tuple-element.24), channel_id=1, source_target_pairs={{0,16},{1,17},{2,18},{3,19},{4,20},{5,21},{6,22},{7,23},{8,24},{9,... | collective-permute-start | bytes 1572872 | tf_op jit(solution)/shard_map/ppermute | solution.py:31
  139.8 25.4 %collective-permute-start.16 = (bf16[512,512]{1,0:T(8,128)(2,1)}, bf16[512,512]{1,0:T(8,128)(2,1)}, u32[]{:S(2)}, u32[]{:S(2)}) collective-permute-start(bf16[512,512]{1,0:T(8,128)(2,1)} %get-tuple-element.25), channel_id=1, source_target_pairs={{0,24},{1,25},{2,26},{3,27},{4,28},{5,29},{6,30},{7,31},{8,0},{9,1... | collective-permute-start | bytes 1572872 | tf_op jit(solution)/shard_map/ppermute | solution.py:31
  140.9 26.9 %collective-permute-start.15 = (bf16[512,512]{1,0:T(8,128)(2,1)}, bf16[512,512]{1,0:T(8,128)(2,1)}, u32[]{:S(2)}, u32[]{:S(2)}) collective-permute-start(bf16[512,512]{1,0:T(8,128)(2,1)} %get-tuple-element.26), channel_id=1, source_target_pairs={{0,8},{1,9},{2,10},{3,11},{4,12},{5,13},{6,14},{7,15},{8,16},{9,17... | collective-permute-start | bytes 1572872 | tf_op jit(solution)/shard_map/ppermute | solution.py:31
  152.2 19.8 %collective-permute-start.10 = (bf16[256,256]{1,0:T(8,128)(2,1)S(1)}, bf16[256,256]{1,0:T(8,128)(2,1)S(1)}, u32[]{:S(2)}, u32[]{:S(2)}) collective-permute-start(bf16[256,256]{1,0:T(8,128)(2,1)S(1)} %fusion.14), channel_id=1, source_target_pairs={{1,64},{3,66},{5,68},{7,70},{9,72},{11,74},{13,76},{15,78},{17,80}... | collective-permute-start | bytes 393224 | tf_op jit(solution)/shard_map/ppermute | solution.py:31
  165.2 6.8 %collective-permute-start.9 = (bf16[256,256]{1,0:T(8,128)(2,1)S(1)}, bf16[256,256]{1,0:T(8,128)(2,1)S(1)}, u32[]{:S(2)}, u32[]{:S(2)}) collective-permute-start(bf16[256,256]{1,0:T(8,128)(2,1)S(1)} %fusion.14), channel_id=1, source_target_pairs={{0,1},{1,65},{2,3},{3,67},{4,5},{5,69},{6,7},{7,71},{8,9},{9,73},{... | collective-permute-start | bytes 393224 | tf_op jit(solution)/shard_map/ppermute | solution.py:31
  170.1 29.8 %collective-permute-start.17 = (bf16[512,512]{1,0:T(8,128)(2,1)}, bf16[512,512]{1,0:T(8,128)(2,1)S(1)}, u32[]{:S(2)}, u32[]{:S(2)}) collective-permute-start(bf16[512,512]{1,0:T(8,128)(2,1)} %fusion.7), channel_id=1, source_target_pairs={{0,2},{1,67},{2,4},{3,69},{4,6},{5,71},{6,0},{7,65},{8,10},{9,75},... | collective-permute-start | bytes 1572872 | tf_op jit(solution)/shard_map/ppermute | solution.py:31
  175.7 24.5 %collective-permute-start.8 = (bf16[512,512]{1,0:T(8,128)(2,1)S(1)}, bf16[512,512]{1,0:T(8,128)(2,1)S(1)}, u32[]{:S(2)}, u32[]{:S(2)}) collective-permute-start(bf16[512,512]{1,0:T(8,128)(2,1)S(1)} %reduce_sum.50), channel_id=1, source_target_pairs={{0,2},{1,66},{2,4},{3,68},{4,6},{5,70},{6,0},{7,64},{8,10},{9,74},... | collective-permute-start | bytes 1572872 | tf_op jit(solution)/shard_map/ppermute | solution.py:31
  (12 other events, 62.0 us)

commit v5 on v4

--- a/solution.py
+++ b/solution.py
@@ -163,25 +163,34 @@
     )(places, *gathered, *gathered)
 
 
-def pack_kernel(saved, out):
-    piece = out.shape[-1]
+def pack_kernel(saved, key, value, out):
+    rows, piece = saved.shape[0], out.shape[-1]
+    share = key.shape[0] // (4 * RING)
     for half in range(2):
         for z in range(RING):
             start = (2 * z + half) * piece
-            out[half, 0, z] = saved[:, start : start + piece]
-
-
-def packed(saved, replicas):
+            out[half, 0, z, :rows] = saved[:, start : start + piece]
+            at = rows
+            mine = pl.ds(((2 * half + pl.program_id(0)) * RING + z) * share, share)
+            for source in (key, value):
+                for column in range(0, source.shape[1], piece):
+                    out[half, 0, z, at : at + share] = source[mine, column : column + piece]
+                    at += share
+
+
+def packed(saved, key, value, replicas):
     rows, features = saved.shape
-    piece = features // replicas
+    piece, share = features // replicas, rows // replicas
+    height = rows + 2 * key.shape[1] // piece * share
+    whole = pl.BlockSpec(key.shape, lambda i: (0, 0))
     out = pl.pallas_call(
         pack_kernel,
-        out_shape=jax.ShapeDtypeStruct((2, 2, RING, rows, piece), saved.dtype),
+        out_shape=jax.ShapeDtypeStruct((2, 2, RING, height, piece), saved.dtype),
         grid=(2,),
-        in_specs=[pl.BlockSpec((rows, features // 2), lambda i: (0, i))],
-        out_specs=pl.BlockSpec((2, 1, RING, rows, piece), lambda i: (0, i, 0, 0, 0)),
-    )(saved)
-    return out.reshape(replicas, rows, piece)
+        in_specs=[pl.BlockSpec((rows, features // 2), lambda i: (0, i)), whole, whole],
+        out_specs=pl.BlockSpec((2, 1, RING, height, piece), lambda i: (0, i, 0, 0, 0)),
+    )(saved, key, value)
+    return out.reshape(replicas, height, piece)
 
 
 def on_device(
@@ -216,15 +225,17 @@
     share = rows // replicas
 
     saved = backup_stream[0]
-    saved_cots = jnp.concatenate([backup_key_cot[0], backup_value_cot[0]], axis=1)
-    share_rows = lax.all_to_all(saved_cots.reshape(replicas, share, -1), "dp", 0, 0)
-    share_rows = lax.dynamic_index_in_dim(share_rows, keeper, 0, keepdims=False)
+    dead = lax.all_to_all(
+        packed(saved, backup_key_cot[0], backup_value_cot[0], replicas), "dp", 0, 0
+    )
 
     own_positions = lax.dynamic_slice_in_dim(positions[0], member * rows, rows, 0)
     cots = derotate(key_cot[0], value_cot[0], own_positions)
     near = moved(cots, lambda x, z, s, t: (x, z, s - 1, t))
     far = moved(cots, lambda x, z, s, t: (x, z, s - 1, 1 - t))
 
+    other_gain = moved(norm_gain, lambda x, z, s, t: (x, z, s, 1 - t))
+
     values = stream[0].astype(jnp.float32)
     saved_values = saved.astype(jnp.float32)
     squares = both_sides(
@@ -232,15 +243,8 @@
     )
     scales = lax.rsqrt(squares / D + EPSILON)
     own_scale = scales[:rows, None]
+    own_scale, other_gain = lax.optimization_barrier((own_scale, other_gain))
     normed = (values * own_scale * norm_gain).astype(jnp.bfloat16)
-
-    saved_scale = scales[rows:]
-    scale_high = saved_scale.astype(jnp.bfloat16)
-    scale_low = (saved_scale - scale_high.astype(jnp.float32)).astype(jnp.bfloat16)
-    factors = jnp.concatenate([scale_high.reshape(share, -1), scale_low.reshape(share, -1)], axis=1)
-    factors = jnp.pad(factors, ((0, 0), (0, HEAD - factors.shape[1])))
-    shares = jnp.concatenate([share_rows, factors], axis=1)
-    shares = lax.all_to_all(jnp.broadcast_to(shares, (replicas, *shares.shape)), "dp", 0, 0)
 
     steps = (2, 1, 3, 0)
 
@@ -273,31 +277,22 @@
             )
         )
 
-    saved_pieces, shares, _ = lax.optimization_barrier(
-        (packed(saved, replicas), shares, (value_tiles, key_tiles))
-    )
-    dead = lax.all_to_all(saved_pieces, "dp", 0, 0)
-
-    dead_raw = shares[:, :, : 2 * width].reshape(rows, 2 * width)
-    factors = lax.dynamic_index_in_dim(shares[:, :, 2 * width :], keeper, 0, keepdims=False)
-    factors = factors.astype(jnp.float32)
-    dead_scale = (factors[:, :share] + factors[:, share : 2 * share]).reshape(rows)[:, None]
-    dead_positions = lax.dynamic_slice_in_dim(positions[0], fallen * rows, rows, 0)
-    dead_cots = derotate(dead_raw[:, :width], dead_raw[:, width:], dead_positions)
-
-    selection = slot_selection(plan_row, member, capacity_blocks, rows)
-    slot_cots = jnp.dot(
-        selection.astype(jnp.bfloat16), dead_cots, preferred_element_type=jnp.float32
-    ).astype(jnp.bfloat16)
-    slot_scale = jnp.sum(selection * jnp.reshape(dead_scale, (1, rows)), axis=1, keepdims=True)
+    value_tiles, key_tiles = lax.optimization_barrier((value_tiles, key_tiles))
+    dead, late_cots, _ = lax.optimization_barrier((dead, cots, (value_tiles, key_tiles)))
+    saved_scale = scales[rows:]
+    scale_high = saved_scale.astype(jnp.bfloat16)
+    scale_low = (saved_scale - scale_high.astype(jnp.float32)).astype(jnp.bfloat16)
+    factors = jnp.concatenate([scale_high.reshape(share, -1), scale_low.reshape(share, -1)], axis=1)
+    factors = jnp.pad(factors, ((0, 0), (0, HEAD - factors.shape[1])))
+    dead = lax.dynamic_index_in_dim(dead, keeper, 0, keepdims=False)
+    share_rows = dead[rows:].reshape(-1, share, piece).transpose(1, 0, 2).reshape(share, -1)
+    shares = jnp.concatenate([share_rows, factors], axis=1)
+    shares = lax.all_to_all(jnp.broadcast_to(shares, (replicas, *shares.shape)), "dp", 0, 0)
+
     across, straight = feature_halves(
-        jnp.concatenate([cots, slot_cots], axis=0),
-        jnp.concatenate([jnp.ones((rows, 1), jnp.float32), slot_scale], axis=0),
-        w_key[0],
-        w_value[0],
-        side,
-    )
-    value_tiles[0], _ = lax.optimization_barrier((value_tiles[0], (across, straight)))
+        late_cots, jnp.ones((rows, 1), jnp.float32), w_key[0], w_value[0], side
+    )
+    value_tiles[2], _ = lax.optimization_barrier((value_tiles[2], (across, straight)))
     across = moved(across, lambda x, z, s, t: (x, z, s - 1, 1 - t))
     straight = moved(straight, lambda x, z, s, t: (x, z, s - 1, t))
 
@@ -305,6 +300,14 @@
     value_rows = [along_x(tile, step)[None] for tile, step in zip(value_tiles, steps)]
 
     there = [(at_z + step) % RING for step in steps]
+    dead_piece = dead[:rows]
+    sent = moved(
+        dead_piece, lambda x, z, s, t: (x, z, s, 1 - t) if x // 2 == t else (x + 2, z, s, t)
+    )
+    lent = moved(dead_piece, lambda x, z, s, t: None if x // 2 == t else (x + 2, z, s, 1 - t))
+    value_rows, key_rows, shares, sent, lent = lax.optimization_barrier(
+        (value_rows, key_rows, shares, sent, lent)
+    )
     value_parts = products(
         value_rows, block, [r % 2 for r in there], [(r // 2) ^ (at_x // 2) for r in there]
     )
@@ -324,24 +327,41 @@
     grad_key = moved(key_total, lambda x, z, s, t: (2 * t + x % 2, z, s + 1, x // 2))
 
     feature = norm_gain * (straight.astype(jnp.float32) + across.astype(jnp.float32))
-    stream_grad = (own_scale * feature[:rows]).astype(jnp.bfloat16)
-    spill_grad = feature[rows:].astype(jnp.bfloat16)
-
-    start = (at_x % 2 * RING + at_z) * block + at_x // 2 * piece
-    dead = lax.dynamic_index_in_dim(dead, keeper, 0, keepdims=False)
-    dead_piece = (
-        dead.astype(jnp.float32) * dead_scale * lax.dynamic_slice_in_dim(norm_gain, start, piece, 0)
+    stream_grad = (own_scale * feature).astype(jnp.bfloat16)
+
+    dead_raw = shares[:, :, : 2 * width].reshape(rows, 2 * width)
+    factors = lax.dynamic_index_in_dim(shares[:, :, 2 * width :], keeper, 0, keepdims=False)
+    factors = factors.astype(jnp.float32)
+    dead_scale = (factors[:, :share] + factors[:, share : 2 * share]).reshape(rows)[:, None]
+    dead_positions = lax.dynamic_slice_in_dim(positions[0], fallen * rows, rows, 0)
+    dead_cots = derotate(dead_raw[:, :width], dead_raw[:, width:], dead_positions)
+
+    selection = slot_selection(plan_row, member, capacity_blocks, rows)
+    slot_cots = jnp.dot(
+        selection.astype(jnp.bfloat16), dead_cots, preferred_element_type=jnp.float32
     ).astype(jnp.bfloat16)
-    sent = moved(
-        dead_piece, lambda x, z, s, t: (x, z, s, 1 - t) if x // 2 == t else (x + 2, z, s, t)
-    )
-    lent = moved(dead_piece, lambda x, z, s, t: None if x // 2 == t else (x + 2, z, s, 1 - t))
+    slot_scale = jnp.sum(selection * jnp.reshape(dead_scale, (1, rows)), axis=1, keepdims=True)
+    slot_cots, _ = lax.optimization_barrier((slot_cots, (key_parts, value_parts)))
+    across, straight = feature_halves(slot_cots, slot_scale, w_key[0], w_value[0], side)
+    across, straight, value_total = lax.optimization_barrier((across, straight, value_total))
+    across = moved(across, lambda x, z, s, t: (x, z, s - 1, 1 - t))
+    straight = moved(straight, lambda x, z, s, t: (x, z, s - 1, t))
+    feature = straight.astype(jnp.float32) + across.astype(jnp.float32)
+    spill_grad = (norm_gain * feature).astype(jnp.bfloat16)
+
     home = at_x // 2
+    start = (at_x % 2 * RING + at_z) * block
+    gain = jnp.where(
+        home == side,
+        lax.dynamic_slice_in_dim(norm_gain, start, block, 0),
+        lax.dynamic_slice_in_dim(other_gain, start, block, 0),
+    )
     same = jnp.where(home == side, dead_piece, sent)
     other = jnp.where(home == side, sent, lent)
     dead_block = jnp.concatenate(
         [jnp.where(home == 0, same, other), jnp.where(home == 0, other, same)], axis=1
     )
+    dead_block = (dead_block.astype(jnp.float32) * dead_scale * gain).astype(jnp.bfloat16)
     dead_part = lax.dot_general(dead_block, dead_cots, TN, preferred_element_type=jnp.float32)
     grad_key = grad_key.astype(jnp.float32) + dead_part[:, :width]
     grad_value = grad_value.astype(jnp.float32) + dead_part[:, width:]

time: 204 us -> 208 us (1.020)
  Pallas kernels: 32.1 us -> 41.9 us
  waiting for transfers between devices: 61.1 us -> 52.4 us
  starting transfers between devices: 61.5 us -> 68.6 us
  other arithmetic: 26.4 us -> 21.8 us
    ppermute x18 -> x21, waiting for transfers between devices: 58.5 us -> 32.1 us  [moved(): return lax.ppermute(block, AXES, route)]
    all_to_all x2 -> x1, waiting for transfers between devices: 2.52 us -> 20.3 us  [on_device(): lax.all_to_all(packed(saved, backup_key_cot[0], backup_value_cot[0], repl...]
    ppermute x18 -> x21, starting transfers between devices: 40.6 us -> 50.7 us  [moved(): return lax.ppermute(block, AXES, route)]
    pallas_call x1 -> x2, Pallas kernels: 13.9 us -> 22.6 us  [feature_halves(): pl.pallas_call(feature_kernel, out_shape=(result, result), in_specs=[pl.B...]
    all_to_all x2 -> x1, starting transfers between devices: 12.1 us -> 7.64 us  [on_device(): lax.all_to_all(packed(saved, backup_key_cot[0], backup_value_cot[0], repl...]
    mul x1 -> x0, other arithmetic: 3.39 us -> none  [on_device(): norm_gain * (straight.astype(jnp.float32) + across.astype(jnp.float32))]
    convert_element_type x2 -> x0, other arithmetic: 3.27 us -> none  [the longest x1 2.27 us: on_device(): value_total.astype(jnp.bfloat16)]
    broadcast_in_dim x2 -> x1, other arithmetic: 3.92 us -> 0.87 us  [on_device(): spill_grad[None]]
  transfers between devices with their start and end apart: 22 -> 24, of which waited for: 6 -> 6; matrix products, arithmetic and copies ran while one was open for 18% -> 14% of each run, Pallas kernels for 15% -> 19%
where the time goes in v5:
time: 208 us; the launch traced here: 205 us
  starting transfers between devices  68.6 us (33%)
  waiting for transfers between devices  52.4 us (25%)
  Pallas kernels  41.9 us (20%)
  other arithmetic  21.8 us (10%)
  local copies, waits for them, and re-layouts  14.7 us (7%)
  matrix products  3.17 us (2%)
  between operations  2.59 us (1%)
    ppermute x21, starting transfers between devices, moved(): return lax.ppermute(block, AXES, route)  50.7 us
    ppermute x21, waiting for transfers between devices, moved(): return lax.ppermute(block, AXES, route)  32.1 us
    pallas_call x2, Pallas kernels, feature_halves(): pl.pallas_call(feature_kernel, out_shape=(result, result), in_specs=[pl.B...  22.6 us
    all_to_all x1, waiting for transfers between devices, on_device(): lax.all_to_all(packed(saved, backup_key_cot[0], backup_value_cot[0], repl...  20.3 us
    pallas_call x2, Pallas kernels, products(): pl.pallas_call(product_kernel, out_shape=jax.ShapeDtypeStruct((RING, bloc...  12.2 us
    all_to_all x1, starting transfers between devices, on_device(): lax.all_to_all(packed(saved, backup_key_cot[0], backup_value_cot[0], repl...  7.64 us
    all_to_all x1, starting transfers between devices, on_device(): lax.all_to_all(jnp.broadcast_to(shares, (replicas, *shares.shape)), 'dp',...  6.06 us
    unnamed x22, local copies, waits for them, and re-layouts  5.08 us
  transfers between devices with their start and end apart: 24, of which 6 were waited for; matrix products, arithmetic and copies ran while one was open for 14% of the time, Pallas kernels for 19%

profile of v5, /device:TPU:25, one launch (start us, length us, event | category | flops | bytes accessed | tf_op | source)
XLA Modules:
  0.0 205.1 jit_solution(11680136033159232937)
XLA Ops:
  14.6 3.0 %shard_map.148 = bf16[2,2,4,320,256]{4,3,2,1,0:T(8,128)(2,1)} custom-call(bf16[256,4096]{1,0:T(8,128)(2,1)} %bitcast.94, bf16[256,512]{1,0:T(8,128)(2,1)} %bitcast.98, bf16[256,512]{1,0:T(8,128)(2,1)} %bitcast.99), custom_call_target="tpu_custom_call" | custom-call | tf_op jit(solution)/shard_map/pallas_call | solution.py:186
  17.5 7.6 %all-to-all-start = ((bf16[16,320,256]{2,1,0:T(8,128)(2,1)}), bf16[16,320,256]{2,1,0:T(8,128)(2,1)}, u32[]{:S(2)}, u32[]{:S(2)}) async-start(bf16[16,320,256]{2,1,0:T(8,128)(2,1)} %bitcast.93), calls=%async_computation | async-start | bytes 5242880 | tf_op jit(solution)/shard_map/all_to_all | solution.py:228
  30.7 2.5 %collective-permute-start.4 = (bf16[256,2048]{1,0:T(8,128)(2,1)}, bf16[256,2048]{1,0:T(8,128)(2,1)S(1)}, u32[]{:S(2)}, u32[]{:S(2)}) collective-permute-start(bf16[256,2048]{1,0:T(8,128)(2,1)} %get-tuple-element.39), channel_id=1, source_target_pairs={{0,64},{1,65},{2,66},{3,67},{4,68},{5,69},{6,70},{7,71},{8,72},{9,... | collective-permute-start | bytes 3145736 | tf_op jit(solution)/shard_map/ppermute | solution.py:31
  33.9 2.7 %collective-permute-start.7 = (bf16[256,2048]{1,0:T(8,128)(2,1)}, bf16[256,2048]{1,0:T(8,128)(2,1)}, u32[]{:S(2)}, u32[]{:S(2)}) collective-permute-start(bf16[256,2048]{1,0:T(8,128)(2,1)} %get-tuple-element.43), channel_id=1, source_target_pairs={{0,16},{1,17},{2,18},{3,19},{4,20},{5,21},{6,22},{7,23},{8,24},{9,... | collective-permute-start | bytes 3145736 | tf_op jit(solution)/shard_map/ppermute | solution.py:31
  37.7 2.4 %collective-permute-start.9 = (bf16[256,2048]{1,0:T(8,128)(2,1)}, bf16[256,2048]{1,0:T(8,128)(2,1)}, u32[]{:S(2)}, u32[]{:S(2)}) collective-permute-start(bf16[256,2048]{1,0:T(8,128)(2,1)} %get-tuple-element.45), channel_id=1, source_target_pairs={{0,24},{1,25},{2,26},{3,27},{4,28},{5,29},{6,30},{7,31},{8,0},{9,1... | collective-permute-start | bytes 3145736 | tf_op jit(solution)/shard_map/ppermute | solution.py:31
  40.1 20.3 %all-to-all-done = bf16[16,320,256]{2,1,0:T(8,128)(2,1)} async-done(((bf16[16,320,256]{2,1,0:T(8,128)(2,1)}), bf16[16,320,256]{2,1,0:T(8,128)(2,1)}, u32[]{:S(2)}, u32[]{:S(2)}) %all-to-all-start) | async-done | bytes 2621472 | tf_op jit(solution)/shard_map/all_to_all | solution.py:228
  61.5 11.5 %shard_map.149 = (bf16[256,4096]{1,0:T(8,128)(2,1)S(1)}, bf16[256,4096]{1,0:T(8,128)(2,1)S(1)}) custom-call(s32[1]{0:T(128)} %bitcast.12.half, bf16[256,1024]{1,0:T(8,128)(2,1)S(1)} %copy-done.1, f32[256,1]{1,0:T(8,128)S(1)} %broadcast_in_dim.97.scale, bf16[8192,512]{1,0:T(8,128)(2,1)} %bitcast.89, bf16[8192,512]{1,0:T(8,128)(2,1)} %bitcast.91), custom_call_target="tpu_custom_call" | custom-call | tf_op jit(solution)/shard_map/pallas_call | solution.py:112
  75.7 3.5 %collective-permute-done.4 = bf16[256,2048]{1,0:T(8,128)(2,1)S(1)} collective-permute-done((bf16[256,2048]{1,0:T(8,128)(2,1)}, bf16[256,2048]{1,0:T(8,128)(2,1)S(1)}, u32[]{:S(2)}, u32[]{:S(2)}) %collective-permute-start.4) | collective-permute-done | bytes 1048608 | tf_op jit(solution)/shard_map/ppermute | solution.py:31
  81.5 6.1 %all-to-all-start.1 = ((bf16[16,16,1152]{2,1,0:T(8,128)(2,1)}), bf16[16,16,1152]{2,1,0:T(8,128)(2,1)}, u32[]{:S(2)}, u32[]{:S(2)}) async-start(bf16[16,16,1152]{2,1,0:T(8,128)(2,1)} %broadcast_in_dim.104), calls=%async_computation.1 | async-start | bytes 1179648 | tf_op jit(solution)/shard_map/all_to_all | solution.py:290
  88.5 12.7 %collective-permute-done.5 = bf16[256,2048]{1,0:T(8,128)(2,1)} collective-permute-done((bf16[256,2048]{1,0:T(8,128)(2,1)}, bf16[256,2048]{1,0:T(8,128)(2,1)}, u32[]{:S(2)}, u32[]{:S(2)}) %collective-permute-start.5) | collective-permute-done | bytes 1048608 | tf_op jit(solution)/shard_map/ppermute | solution.py:31
  102.8 3.6 %collective-permute-start.11 = (bf16[256,256]{1,0:T(8,128)(2,1)S(1)}, bf16[256,256]{1,0:T(8,128)(2,1)}, u32[]{:S(2)}, u32[]{:S(2)}) collective-permute-start(bf16[256,256]{1,0:T(8,128)(2,1)S(1)} %dynamic-slice_bitcast_fusion), channel_id=1, source_target_pairs={{1,64},{3,66},{5,68},{7,70},{9,72},{11,74},{13,76},{15,78},{17,80}... | collective-permute-start | bytes 393224 | tf_op jit(solution)/shard_map/ppermute | solution.py:31
  106.6 4.9 %collective-permute-start.12 = (bf16[256,4096]{1,0:T(8,128)(2,1)}, bf16[256,4096]{1,0:T(8,128)(2,1)}, u32[]{:S(2)}, u32[]{:S(2)}) collective-permute-start(bf16[256,4096]{1,0:T(8,128)(2,1)} %copy-done.3), channel_id=1, source_target_pairs={{0,7},{1,6},{2,1},{3,0},{4,3},{5,2},{6,5},{7,4},{8,15},{9,14},{10,... | collective-permute-start | bytes 6291464 | tf_op jit(solution)/shard_map/ppermute | solution.py:31
  111.5 3.5 %collective-permute-start.13 = (bf16[256,4096]{1,0:T(8,128)(2,1)}, bf16[256,4096]{1,0:T(8,128)(2,1)}, u32[]{:S(2)}, u32[]{:S(2)}) collective-permute-start(bf16[256,4096]{1,0:T(8,128)(2,1)} %copy-done.2), channel_id=1, source_target_pairs={{0,6},{1,7},{2,0},{3,1},{4,2},{5,3},{6,4},{7,5},{8,14},{9,15},{10,... | collective-permute-start | bytes 6291464 | tf_op jit(solution)/shard_map/ppermute | solution.py:31
  117.8 5.5 %shard_map.152 = bf16[4,512,512]{2,1,0:T(8,128)(2,1)S(1)} custom-call(s32[2,4]{1,0:T(2,128)S(1)} %pad_add_fusion.1.places, bf16[1,256,2048]{2,1,0:T(8,128)(2,1)S(1)} %bitcast.87, bf16[1,256,2048]{2,1,0:T(8,128)(2,1)} %bitcast.11.refs_1_.refs_5_, bf16[1,256,2048]{2,1,0:T(8,128)(2,1)} %bitcast.18.refs_2_.refs_6_, bf16[1,256,2048]{2,1,0:T(8,128)(2,1)S(1)} %bitcast.85, ...), custom_call_target="tpu_custom_call" | custom-call | tf_op jit(solution)/shard_map/pallas_call | solution.py:153
  125.8 2.7 %collective-permute-start.17 = (bf16[512,512]{1,0:T(8,128)(2,1)}, bf16[512,512]{1,0:T(8,128)(2,1)}, u32[]{:S(2)}, u32[]{:S(2)}) collective-permute-start(bf16[512,512]{1,0:T(8,128)(2,1)} %get-tuple-element.77), channel_id=1, source_target_pairs={{0,24},{1,25},{2,26},{3,27},{4,28},{5,29},{6,30},{7,31},{8,0},{9,1... | collective-permute-start | bytes 1572872 | tf_op jit(solution)/shard_map/ppermute | solution.py:31
  130.4 6.6 %shard_map.150 = bf16[4,512,512]{2,1,0:T(8,128)(2,1)} custom-call(s32[2,4]{1,0:T(2,128)S(1)} %pad_add_fusion.places, bf16[1,256,2048]{2,1,0:T(8,128)(2,1)} %bitcast.20.refs_0_.refs_4_, bf16[1,256,2048]{2,1,0:T(8,128)(2,1)} %bitcast.21.refs_1_.refs_5_, bf16[1,256,2048]{2,1,0:T(8,128)(2,1)} %bitcast.22.refs_2_.refs_6_, bf16[1,256,2048]{2,1,0:T(8,128)(2,1)S(1)} %bitcast.83, ...), custom_call_target="tpu_custom_call" | custom-call | tf_op jit(solution)/shard_map/pallas_call | solution.py:153
  137.1 4.2 %all-to-all-start.2 = ((bf16[4,512,512]{2,1,0:T(8,128)(2,1)}), bf16[4,512,512]{2,1,0:T(8,128)(2,1)S(1)}, u32[]{:S(2)}, u32[]{:S(2)}) async-start(bf16[4,512,512]{2,1,0:T(8,128)(2,1)} %shard_map.150), calls=%async_computation.2 | async-start | bytes 4194304 | tf_op jit(solution)/shard_map/all_to_all | solution.py:324
  145.7 11.0 %shard_map.153 = (bf16[48,4096]{1,0:T(8,128)(2,1)S(1)}, bf16[48,4096]{1,0:T(8,128)(2,1)S(1)}) custom-call(s32[1]{0:T(128)} %bitcast.12.half, bf16[48,1024]{1,0:T(8,128)(2,1)S(1)} %convolution_convert_fusion.cots, f32[48,1]{1,0:T(8,128)S(1)} %copy.21.scale, bf16[8192,512]{1,0:T(8,128)(2,1)} %bitcast.90, bf16[8192,512]{1,0:T(8,128)(2,1)} %bitcast.92), custom_call_target="tpu_custom_call" | custom-call | tf_op jit(solution)/shard_map/pallas_call | solution.py:112
  158.6 9.4 %collective-permute-start.20 = (bf16[48,4096]{1,0:T(8,128)(2,1)S(1)}, bf16[48,4096]{1,0:T(8,128)(2,1)S(1)}, u32[]{:S(2)}, u32[]{:S(2)}) collective-permute-start(bf16[48,4096]{1,0:T(8,128)(2,1)S(1)} %get-tuple-element.71), channel_id=1, source_target_pairs={{0,7},{1,6},{2,1},{3,0},{4,3},{5,2},{6,5},{7,4},{8,15},{9,14},{10,... | collective-permute-start | bytes 1179656 | tf_op jit(solution)/shard_map/ppermute | solution.py:31
  170.9 4.7 %collective-permute-start.18 = (bf16[512,512]{1,0:T(8,128)(2,1)S(1)}, bf16[512,512]{1,0:T(8,128)(2,1)S(1)}, u32[]{:S(2)}, u32[]{:S(2)}) collective-permute-start(bf16[512,512]{1,0:T(8,128)(2,1)S(1)} %convert_add_fusion), channel_id=1, source_target_pairs={{0,2},{1,67},{2,4},{3,69},{4,6},{5,71},{6,0},{7,65},{8,10},{9,75},... | collective-permute-start | bytes 1572872 | tf_op jit(solution)/shard_map/ppermute | solution.py:31
  175.6 2.7 %collective-permute-done.20 = bf16[48,4096]{1,0:T(8,128)(2,1)S(1)} collective-permute-done((bf16[48,4096]{1,0:T(8,128)(2,1)S(1)}, bf16[48,4096]{1,0:T(8,128)(2,1)S(1)}, u32[]{:S(2)}, u32[]{:S(2)}) %collective-permute-start.20) | collective-permute-done | bytes 393248 | tf_op jit(solution)/shard_map/ppermute | solution.py:31
  180.9 5.4 %collective-permute-start.14 = (bf16[512,512]{1,0:T(8,128)(2,1)}, bf16[512,512]{1,0:T(8,128)(2,1)S(1)}, u32[]{:S(2)}, u32[]{:S(2)}) collective-permute-start(bf16[512,512]{1,0:T(8,128)(2,1)} %reduce_sum.50), channel_id=1, source_target_pairs={{0,2},{1,66},{2,4},{3,68},{4,6},{5,70},{6,0},{7,64},{8,10},{9,74},... | collective-permute-start | bytes 1572872 | tf_op jit(solution)/shard_map/ppermute | solution.py:31
  186.3 4.6 %fusion.3 = bf16[1,256,4096]{2,1,0:T(8,128)(2,1)} fusion(bf16[256,4096]{1,0:T(8,128)(2,1)} %collective-permute-done.12, bf16[256,4096]{1,0:T(8,128)(2,1)} %collective-permute-done.13, f32[4096]{0:T(1024)S(1)} %copy-done.8, f32[256]{0:T(256)S(1)} %get-tuple-element.110), kind=kLoop, calls=%fused_computation.7 | loop fusion | flops 6291456 | bytes 6308864 | tf_op jit(solution)/shard_map/broadcast_in_dim | solution.py:369
  190.9 12.5 %collective-permute-done.18 = bf16[512,512]{1,0:T(8,128)(2,1)S(1)} collective-permute-done((bf16[512,512]{1,0:T(8,128)(2,1)S(1)}, bf16[512,512]{1,0:T(8,128)(2,1)S(1)}, u32[]{:S(2)}, u32[]{:S(2)}) %collective-permute-start.18) | collective-permute-done | bytes 524320 | tf_op jit(solution)/shard_map/ppermute | solution.py:31
  (110 shorter events, 49.0 us)
Async XLA Ops:
  7.4 19.3 %collective-permute-start.3 = (bf16[256,1024]{1,0:T(8,128)(2,1)}, bf16[256,1024]{1,0:T(8,128)(2,1)S(1)}, u32[]{:S(2)}, u32[]{:S(2)}) collective-permute-start(bf16[256,1024]{1,0:T(8,128)(2,1)} %shard_map.147.cots), channel_id=1, source_target_pairs={{0,7},{1,6},{2,1},{3,0},{4,3},{5,2},{6,5},{7,4},{8,15},{9,14},{10,... | collective-permute-start | bytes 1572872 | tf_op jit(solution)/shard_map/ppermute | solution.py:31
  8.9 17.9 %collective-permute-start.2 = (bf16[256,1024]{1,0:T(8,128)(2,1)}, bf16[256,1024]{1,0:T(8,128)(2,1)S(1)}, u32[]{:S(2)}, u32[]{:S(2)}) collective-permute-start(bf16[256,1024]{1,0:T(8,128)(2,1)} %shard_map.147.cots), channel_id=1, source_target_pairs={{0,6},{1,7},{2,0},{3,1},{4,2},{5,3},{6,4},{7,5},{8,14},{9,15},{10,... | collective-permute-start | bytes 1572872 | tf_op jit(solution)/shard_map/ppermute | solution.py:31
  11.5 14.0 %collective-permute-start = (f32[512]{0:T(512)S(1)}, f32[512]{0:T(512)S(1)}, u32[]{:S(2)}, u32[]{:S(2)}) collective-permute-start(f32[512]{0:T(512)S(1)} %pad_maximum_fusion.17), channel_id=1, source_target_pairs={{0,1},{1,0},{2,3},{3,2},{4,5},{5,4},{6,7},{7,6},{8,9},{9,8},{10,11... | collective-permute-start | bytes 6152 | tf_op jit(solution)/shard_map/ppermute | solution.py:31
  13.6 11.9 %collective-permute-start.1 = (f32[4096]{0:T(1024)S(1)}, f32[4096]{0:T(1024)S(1)}, u32[]{:S(2)}, u32[]{:S(2)}) collective-permute-start(f32[4096]{0:T(1024)S(1)} %copy-done.8), channel_id=1, source_target_pairs={{0,1},{1,0},{2,3},{3,2},{4,5},{5,4},{6,7},{7,6},{8,9},{9,8},{10,11... | collective-permute-start | bytes 49160 | tf_op jit(solution)/shard_map/ppermute | solution.py:31
  17.5 42.9 %all-to-all-start = ((bf16[16,320,256]{2,1,0:T(8,128)(2,1)}), bf16[16,320,256]{2,1,0:T(8,128)(2,1)}, u32[]{:S(2)}, u32[]{:S(2)}) async-start(bf16[16,320,256]{2,1,0:T(8,128)(2,1)} %bitcast.93), calls=%async_computation | async-start | bytes 5242880 | tf_op jit(solution)/shard_map/all_to_all | solution.py:228
  30.7 48.6 %collective-permute-start.4 = (bf16[256,2048]{1,0:T(8,128)(2,1)}, bf16[256,2048]{1,0:T(8,128)(2,1)S(1)}, u32[]{:S(2)}, u32[]{:S(2)}) collective-permute-start(bf16[256,2048]{1,0:T(8,128)(2,1)} %get-tuple-element.39), channel_id=1, source_target_pairs={{0,64},{1,65},{2,66},{3,67},{4,68},{5,69},{6,70},{7,71},{8,72},{9,... | collective-permute-start | bytes 3145736 | tf_op jit(solution)/shard_map/ppermute | solution.py:31
  33.6 67.6 %collective-permute-start.5 = (bf16[256,2048]{1,0:T(8,128)(2,1)}, bf16[256,2048]{1,0:T(8,128)(2,1)}, u32[]{:S(2)}, u32[]{:S(2)}) collective-permute-start(bf16[256,2048]{1,0:T(8,128)(2,1)} %get-tuple-element.40), channel_id=1, source_target_pairs={{0,32},{1,33},{2,34},{3,35},{4,36},{5,37},{6,38},{7,39},{8,40},{9,... | collective-permute-start | bytes 3145736 | tf_op jit(solution)/shard_map/ppermute | solution.py:31
  33.9 68.8 %collective-permute-start.7 = (bf16[256,2048]{1,0:T(8,128)(2,1)}, bf16[256,2048]{1,0:T(8,128)(2,1)}, u32[]{:S(2)}, u32[]{:S(2)}) collective-permute-start(bf16[256,2048]{1,0:T(8,128)(2,1)} %get-tuple-element.43), channel_id=1, source_target_pairs={{0,16},{1,17},{2,18},{3,19},{4,20},{5,21},{6,22},{7,23},{8,24},{9,... | collective-permute-start | bytes 3145736 | tf_op jit(solution)/shard_map/ppermute | solution.py:31
  37.4 69.2 %collective-permute-start.8 = (bf16[256,2048]{1,0:T(8,128)(2,1)}, bf16[256,2048]{1,0:T(8,128)(2,1)}, u32[]{:S(2)}, u32[]{:S(2)}) collective-permute-start(bf16[256,2048]{1,0:T(8,128)(2,1)} %get-tuple-element.44), channel_id=1, source_target_pairs={{0,8},{1,9},{2,10},{3,11},{4,12},{5,13},{6,14},{7,15},{8,16},{9,17... | collective-permute-start | bytes 3145736 | tf_op jit(solution)/shard_map/ppermute | solution.py:31
  37.7 73.7 %collective-permute-start.9 = (bf16[256,2048]{1,0:T(8,128)(2,1)}, bf16[256,2048]{1,0:T(8,128)(2,1)}, u32[]{:S(2)}, u32[]{:S(2)}) collective-permute-start(bf16[256,2048]{1,0:T(8,128)(2,1)} %get-tuple-element.45), channel_id=1, source_target_pairs={{0,24},{1,25},{2,26},{3,27},{4,28},{5,29},{6,30},{7,31},{8,0},{9,1... | collective-permute-start | bytes 3145736 | tf_op jit(solution)/shard_map/ppermute | solution.py:31
  79.3 35.7 %collective-permute-start.6 = (bf16[256,2048]{1,0:T(8,128)(2,1)}, bf16[256,2048]{1,0:T(8,128)(2,1)}, u32[]{:S(2)}, u32[]{:S(2)}) collective-permute-start(bf16[256,2048]{1,0:T(8,128)(2,1)} %get-tuple-element.50), channel_id=1, source_target_pairs={{0,96},{1,97},{2,98},{3,99},{4,100},{5,101},{6,102},{7,103},{8,104... | collective-permute-start | bytes 3145736 | tf_op jit(solution)/shard_map/ppermute | solution.py:31
  81.5 33.5 %all-to-all-start.1 = ((bf16[16,16,1152]{2,1,0:T(8,128)(2,1)}), bf16[16,16,1152]{2,1,0:T(8,128)(2,1)}, u32[]{:S(2)}, u32[]{:S(2)}) async-start(bf16[16,16,1152]{2,1,0:T(8,128)(2,1)} %broadcast_in_dim.104), calls=%async_computation.1 | async-start | bytes 1179648 | tf_op jit(solution)/shard_map/all_to_all | solution.py:290
  101.2 13.7 %collective-permute-start.10 = (bf16[256,256]{1,0:T(8,128)(2,1)S(1)}, bf16[256,256]{1,0:T(8,128)(2,1)S(1)}, u32[]{:S(2)}, u32[]{:S(2)}) collective-permute-start(bf16[256,256]{1,0:T(8,128)(2,1)S(1)} %dynamic-slice_bitcast_fusion), channel_id=1, source_target_pairs={{0,1},{1,65},{2,3},{3,67},{4,5},{5,69},{6,7},{7,71},{8,9},{9,73},{... | collective-permute-start | bytes 393224 | tf_op jit(solution)/shard_map/ppermute | solution.py:31
  102.8 12.1 %collective-permute-start.11 = (bf16[256,256]{1,0:T(8,128)(2,1)S(1)}, bf16[256,256]{1,0:T(8,128)(2,1)}, u32[]{:S(2)}, u32[]{:S(2)}) collective-permute-start(bf16[256,256]{1,0:T(8,128)(2,1)S(1)} %dynamic-slice_bitcast_fusion), channel_id=1, source_target_pairs={{1,64},{3,66},{5,68},{7,70},{9,72},{11,74},{13,76},{15,78},{17,80}... | collective-permute-start | bytes 393224 | tf_op jit(solution)/shard_map/ppermute | solution.py:31
  106.6 74.3 %collective-permute-start.12 = (bf16[256,4096]{1,0:T(8,128)(2,1)}, bf16[256,4096]{1,0:T(8,128)(2,1)}, u32[]{:S(2)}, u32[]{:S(2)}) collective-permute-start(bf16[256,4096]{1,0:T(8,128)(2,1)} %copy-done.3), channel_id=1, source_target_pairs={{0,7},{1,6},{2,1},{3,0},{4,3},{5,2},{6,5},{7,4},{8,15},{9,14},{10,... | collective-permute-start | bytes 6291464 | tf_op jit(solution)/shard_map/ppermute | solution.py:31
  111.5 69.5 %collective-permute-start.13 = (bf16[256,4096]{1,0:T(8,128)(2,1)}, bf16[256,4096]{1,0:T(8,128)(2,1)}, u32[]{:S(2)}, u32[]{:S(2)}) collective-permute-start(bf16[256,4096]{1,0:T(8,128)(2,1)} %copy-done.2), channel_id=1, source_target_pairs={{0,6},{1,7},{2,0},{3,1},{4,2},{5,3},{6,4},{7,5},{8,14},{9,15},{10,... | collective-permute-start | bytes 6291464 | tf_op jit(solution)/shard_map/ppermute | solution.py:31
  125.8 30.9 %collective-permute-start.17 = (bf16[512,512]{1,0:T(8,128)(2,1)}, bf16[512,512]{1,0:T(8,128)(2,1)}, u32[]{:S(2)}, u32[]{:S(2)}) collective-permute-start(bf16[512,512]{1,0:T(8,128)(2,1)} %get-tuple-element.77), channel_id=1, source_target_pairs={{0,24},{1,25},{2,26},{3,27},{4,28},{5,29},{6,30},{7,31},{8,0},{9,1... | collective-permute-start | bytes 1572872 | tf_op jit(solution)/shard_map/ppermute | solution.py:31
  128.5 28.2 %collective-permute-start.16 = (bf16[512,512]{1,0:T(8,128)(2,1)}, bf16[512,512]{1,0:T(8,128)(2,1)}, u32[]{:S(2)}, u32[]{:S(2)}) collective-permute-start(bf16[512,512]{1,0:T(8,128)(2,1)} %get-tuple-element.78), channel_id=1, source_target_pairs={{0,8},{1,9},{2,10},{3,11},{4,12},{5,13},{6,14},{7,15},{8,16},{9,17... | collective-permute-start | bytes 1572872 | tf_op jit(solution)/shard_map/ppermute | solution.py:31
  128.5 28.2 %collective-permute-start.15 = (bf16[512,512]{1,0:T(8,128)(2,1)}, bf16[512,512]{1,0:T(8,128)(2,1)}, u32[]{:S(2)}, u32[]{:S(2)}) collective-permute-start(bf16[512,512]{1,0:T(8,128)(2,1)} %get-tuple-element.76), channel_id=1, source_target_pairs={{0,16},{1,17},{2,18},{3,19},{4,20},{5,21},{6,22},{7,23},{8,24},{9,... | collective-permute-start | bytes 1572872 | tf_op jit(solution)/shard_map/ppermute | solution.py:31
  137.1 42.6 %all-to-all-start.2 = ((bf16[4,512,512]{2,1,0:T(8,128)(2,1)}), bf16[4,512,512]{2,1,0:T(8,128)(2,1)S(1)}, u32[]{:S(2)}, u32[]{:S(2)}) async-start(bf16[4,512,512]{2,1,0:T(8,128)(2,1)} %shard_map.150), calls=%async_computation.2 | async-start | bytes 4194304 | tf_op jit(solution)/shard_map/all_to_all | solution.py:324
  158.6 19.6 %collective-permute-start.20 = (bf16[48,4096]{1,0:T(8,128)(2,1)S(1)}, bf16[48,4096]{1,0:T(8,128)(2,1)S(1)}, u32[]{:S(2)}, u32[]{:S(2)}) collective-permute-start(bf16[48,4096]{1,0:T(8,128)(2,1)S(1)} %get-tuple-element.71), channel_id=1, source_target_pairs={{0,7},{1,6},{2,1},{3,0},{4,3},{5,2},{6,5},{7,4},{8,15},{9,14},{10,... | collective-permute-start | bytes 1179656 | tf_op jit(solution)/shard_map/ppermute | solution.py:31
  168.0 10.8 %collective-permute-start.19 = (bf16[48,4096]{1,0:T(8,128)(2,1)S(1)}, bf16[48,4096]{1,0:T(8,128)(2,1)S(1)}, u32[]{:S(2)}, u32[]{:S(2)}) collective-permute-start(bf16[48,4096]{1,0:T(8,128)(2,1)S(1)} %get-tuple-element.70), channel_id=1, source_target_pairs={{0,6},{1,7},{2,0},{3,1},{4,2},{5,3},{6,4},{7,5},{8,14},{9,15},{10,... | collective-permute-start | bytes 1179656 | tf_op jit(solution)/shard_map/ppermute | solution.py:31
  170.9 32.5 %collective-permute-start.18 = (bf16[512,512]{1,0:T(8,128)(2,1)S(1)}, bf16[512,512]{1,0:T(8,128)(2,1)S(1)}, u32[]{:S(2)}, u32[]{:S(2)}) collective-permute-start(bf16[512,512]{1,0:T(8,128)(2,1)S(1)} %convert_add_fusion), channel_id=1, source_target_pairs={{0,2},{1,67},{2,4},{3,69},{4,6},{5,71},{6,0},{7,65},{8,10},{9,75},... | collective-permute-start | bytes 1572872 | tf_op jit(solution)/shard_map/ppermute | solution.py:31
  180.9 22.5 %collective-permute-start.14 = (bf16[512,512]{1,0:T(8,128)(2,1)}, bf16[512,512]{1,0:T(8,128)(2,1)S(1)}, u32[]{:S(2)}, u32[]{:S(2)}) collective-permute-start(bf16[512,512]{1,0:T(8,128)(2,1)} %reduce_sum.50), channel_id=1, source_target_pairs={{0,2},{1,66},{2,4},{3,68},{4,6},{5,70},{6,0},{7,64},{8,10},{9,74},... | collective-permute-start | bytes 1572872 | tf_op jit(solution)/shard_map/ppermute | solution.py:31
  (11 other events, 95.6 us)

commit v6 on v4

--- a/solution.py
+++ b/solution.py
@@ -80,7 +80,7 @@
 
 NT = (((1,), (1,)), ((), ()))
 TN = (((0,), (0,)), ((), ()))
-TILE = 1024
+TILE = 2048
 
 
 def feature_kernel(half, cots, scale, w_key, w_value, across, straight):
@@ -120,7 +120,7 @@
             pl.BlockSpec(memory_space=pltpu.HBM),
         ],
         out_specs=(pl.BlockSpec(memory_space=pltpu.HBM), pl.BlockSpec(memory_space=pltpu.HBM)),
-        compiler_params=pltpu.CompilerParams(vmem_limit_bytes=32 * 1024 * 1024),
+        compiler_params=pltpu.CompilerParams(vmem_limit_bytes=40 * 1024 * 1024),
     )(
         jnp.reshape(half, (1,)),
         cots,
@@ -159,7 +159,7 @@
             in_specs=left + right,
             out_specs=pl.BlockSpec((1, block, block), lambda i, at: (i, 0, 0)),
         ),
-        compiler_params=pltpu.CompilerParams(vmem_limit_bytes=32 * 1024 * 1024),
+        compiler_params=pltpu.CompilerParams(vmem_limit_bytes=40 * 1024 * 1024),
     )(places, *gathered, *gathered)
 
 
@@ -320,7 +320,6 @@
     x_rings = [[RING * x + z for x in range(RING)] for z in range(RING)]
     parts = lax.all_to_all(key_parts, "dp", 0, 0, axis_index_groups=x_rings)
     key_total = jnp.sum(parts.astype(jnp.float32), axis=0).astype(jnp.bfloat16)
-    key_total, across, straight = lax.optimization_barrier((key_total, across, straight))
     grad_key = moved(key_total, lambda x, z, s, t: (2 * t + x % 2, z, s + 1, x // 2))
 
     feature = norm_gain * (straight.astype(jnp.float32) + across.astype(jnp.float32))

time: 204 us -> 204 us (level)
  transfers between devices with their start and end apart: 22 -> 22, of which waited for: 6 -> 6; matrix products, arithmetic and copies ran while one was open for 18% -> 18% of each run, Pallas kernels for 15% -> 14%
where the time goes in v6:
time: 204 us; the launch traced here: 202 us
  waiting for transfers between devices  62.3 us (31%)
  starting transfers between devices  61.5 us (30%)
  Pallas kernels  30.8 us (15%)
  other arithmetic  26.4 us (13%)
  local copies, waits for them, and re-layouts  16.4 us (8%)
  between operations  2.65 us (1%)
    ppermute x18, waiting for transfers between devices, moved(): return lax.ppermute(block, AXES, route)  59.8 us
    ppermute x18, starting transfers between devices, moved(): return lax.ppermute(block, AXES, route)  40.7 us
    pallas_call x1, Pallas kernels, feature_halves(): pl.pallas_call(feature_kernel, out_shape=(result, result), in_specs=[pl.B...  12.6 us
    pallas_call x2, Pallas kernels, products(): pl.pallas_call(product_kernel, out_shape=jax.ShapeDtypeStruct((RING, bloc...  11.2 us
    all_to_all x1, starting transfers between devices, on_device(): lax.all_to_all(saved_cots.reshape(replicas, share, -1), 'dp', 0, 0)  7.59 us
    all_to_all x1, starting transfers between devices, on_device(): parts = lax.all_to_all(key_parts, 'dp', 0, 0, axis_index_groups=x_rings)  4.59 us
    all_to_all x1, starting transfers between devices, on_device(): dead = lax.all_to_all(saved_pieces, 'dp', 0, 0)  4.44 us
    all_to_all x1, starting transfers between devices, on_device(): lax.all_to_all(jnp.broadcast_to(shares, (replicas, *shares.shape)), 'dp',...  4.25 us
  transfers between devices with their start and end apart: 22, of which 6 were waited for; matrix products, arithmetic and copies ran while one was open for 18% of the time, Pallas kernels for 14%

profile of v6, /device:TPU:25, one launch (start us, length us, event | category | flops | bytes accessed | tf_op | source)
XLA Modules:
  0.0 201.8 jit_solution(10818054594359573314)
XLA Ops:
  5.1 2.1 %shard_map.147 = bf16[256,1024]{1,0:T(8,128)(2,1)} custom-call(bf16[256,512]{1,0:T(8,128)(2,1)} %bitcast.88, bf16[256,512]{1,0:T(8,128)(2,1)} %bitcast.89, f32[256,128]{1,0:T(8,128)} %get-tuple-element.57.cosine, f32[256,128]{1,0:T(8,128)} %get-tuple-element.58.sine), custom_call_target="tpu_custom_call" | custom-call | tf_op jit(solution)/shard_map/pallas_call | solution.py:60
  8.8 3.1 %fusion = (f32[256]{0:T(256)S(1)}, f32[256]{0:T(256)S(1)}) fusion(bf16[1,256,4096]{2,1,0:T(8,128)(2,1)} %param.12, bf16[1,256,4096]{2,1,0:T(8,128)(2,1)} %param.13), kind=kLoop, calls=%fused_computation.3 | loop fusion | flops 6290944 | bytes 4196352 | tf_op jit(solution)/shard_map/reduce_sum | solution.py:231
  14.9 7.6 %all-to-all-start.1 = ((bf16[16,16,1024]{2,1,0:T(8,128)(2,1)}), bf16[16,16,1024]{2,1,0:T(8,128)(2,1)}, u32[]{:S(2)}, u32[]{:S(2)}) async-start(bf16[16,16,1024]{2,1,0:T(8,128)(2,1)} %pad_maximum_fusion.17), calls=%async_computation.1 | async-start | bytes 1048576 | tf_op jit(solution)/shard_map/all_to_all | solution.py:220
  23.9 2.8 %shard_map.149 = bf16[2,2,4,256,256]{4,3,2,1,0:T(8,128)(2,1)} custom-call(bf16[256,4096]{1,0:T(8,128)(2,1)} %bitcast.85), custom_call_target="tpu_custom_call" | custom-call | tf_op jit(solution)/shard_map/pallas_call | solution.py:177
  29.3 2.5 %all-to-all-done.1 = bf16[16,16,1024]{2,1,0:T(8,128)(2,1)} async-done(((bf16[16,16,1024]{2,1,0:T(8,128)(2,1)}), bf16[16,16,1024]{2,1,0:T(8,128)(2,1)}, u32[]{:S(2)}, u32[]{:S(2)}) %all-to-all-start.1) | async-done | bytes 524320 | tf_op jit(solution)/shard_map/all_to_all | solution.py:220
  33.4 4.2 %all-to-all-start.2 = ((bf16[16,16,1152]{2,1,0:T(8,128)(2,1)}), bf16[16,16,1152]{2,1,0:T(8,128)(2,1)}, u32[]{:S(2)}, u32[]{:S(2)}) async-start(bf16[16,16,1152]{2,1,0:T(8,128)(2,1)} %broadcast_in_dim.93), calls=%async_computation.2 | async-start | bytes 1179648 | tf_op jit(solution)/shard_map/all_to_all | solution.py:243
  53.4 4.4 %all-to-all-start.3 = ((bf16[16,256,256]{2,1,0:T(8,128)(2,1)}), bf16[16,256,256]{2,1,0:T(8,128)(2,1)}, u32[]{:S(2)}, u32[]{:S(2)}) async-start(bf16[16,256,256]{2,1,0:T(8,128)(2,1)} %bitcast.86), calls=%async_computation.3 | async-start | bytes 4194304 | tf_op jit(solution)/shard_map/all_to_all | solution.py:279
  64.5 12.6 %shard_map.151 = (bf16[304,4096]{1,0:T(8,128)(2,1)}, bf16[304,4096]{1,0:T(8,128)(2,1)}) custom-call(s32[1]{0:T(128)} %bitcast.33.half, bf16[304,1024]{1,0:T(8,128)(2,1)S(1)} %pad_maximum_fusion.16.cots, f32[304,1]{1,0:T(8,128)S(1)} %concatenate.80.scale, bf16[8192,512]{1,0:T(8,128)(2,1)} %bitcast.83, bf16[8192,512]{1,0:T(8,128)(2,1)} %bitcast.84), custom_call_target="tpu_custom_call" | custom-call | tf_op jit(solution)/shard_map/pallas_call | solution.py:112
  77.2 2.7 %collective-permute-start.9 = (bf16[256,2048]{1,0:T(8,128)(2,1)}, bf16[256,2048]{1,0:T(8,128)(2,1)}, u32[]{:S(2)}, u32[]{:S(2)}) collective-permute-start(bf16[256,2048]{1,0:T(8,128)(2,1)} %get-tuple-element.13), channel_id=1, source_target_pairs={{0,64},{1,65},{2,66},{3,67},{4,68},{5,69},{6,70},{7,71},{8,72},{9,... | collective-permute-start | bytes 3145736 | tf_op jit(solution)/shard_map/ppermute | solution.py:31
  79.9 6.4 %collective-permute-start.17 = (bf16[304,4096]{1,0:T(8,128)(2,1)}, bf16[304,4096]{1,0:T(8,128)(2,1)}, u32[]{:S(2)}, u32[]{:S(2)}) collective-permute-start(bf16[304,4096]{1,0:T(8,128)(2,1)} %get-tuple-element.11), channel_id=1, source_target_pairs={{0,7},{1,6},{2,1},{3,0},{4,3},{5,2},{6,5},{7,4},{8,15},{9,14},{10,... | collective-permute-start | bytes 7471112 | tf_op jit(solution)/shard_map/ppermute | solution.py:31
  86.3 28.7 %collective-permute-done.3 = bf16[256,2048]{1,0:T(8,128)(2,1)} collective-permute-done((bf16[256,2048]{1,0:T(8,128)(2,1)}, bf16[256,2048]{1,0:T(8,128)(2,1)}, u32[]{:S(2)}, u32[]{:S(2)}) %collective-permute-start.3) | collective-permute-done | bytes 1048608 | tf_op jit(solution)/shard_map/ppermute | solution.py:31
  117.1 5.4 %shard_map.148 = bf16[4,512,512]{2,1,0:T(8,128)(2,1)S(1)} custom-call(s32[2,4]{1,0:T(2,128)S(1)} %pad_add_fusion.places, bf16[1,256,2048]{2,1,0:T(8,128)(2,1)} %bitcast.8.refs_0_.refs_4_, bf16[1,256,2048]{2,1,0:T(8,128)(2,1)S(1)} %bitcast.81, bf16[1,256,2048]{2,1,0:T(8,128)(2,1)} %bitcast.10.refs_2_.refs_6_, ...), custom_call_target="tpu_custom_call" | custom-call | tf_op jit(solution)/shard_map/pallas_call | solution.py:153
  123.8 5.8 %shard_map.152 = bf16[4,512,512]{2,1,0:T(8,128)(2,1)S(1)} custom-call(s32[2,4]{1,0:T(2,128)S(1)} %pad_add_fusion.1.places, bf16[1,256,2048]{2,1,0:T(8,128)(2,1)} %bitcast.38.refs_0_.refs_4_, bf16[1,256,2048]{2,1,0:T(8,128)(2,1)} %bitcast.39.refs_1_.refs_5_, bf16[1,256,2048]{2,1,0:T(8,128)(2,1)} %bitcast.40.refs_2_.refs_6_, ...), custom_call_target="tpu_custom_call" | custom-call | tf_op jit(solution)/shard_map/pallas_call | solution.py:153
  131.0 4.6 %all-to-all-start = ((bf16[4,512,512]{2,1,0:T(8,128)(2,1)}), bf16[4,512,512]{2,1,0:T(8,128)(2,1)}, u32[]{:S(2)}, u32[]{:S(2)}) async-start(bf16[4,512,512]{2,1,0:T(8,128)(2,1)} %copy-done.2), calls=%async_computation | async-start | bytes 4194304 | tf_op jit(solution)/shard_map/all_to_all | solution.py:321
  136.8 3.0 %collective-permute-start.12 = (bf16[512,512]{1,0:T(8,128)(2,1)}, bf16[512,512]{1,0:T(8,128)(2,1)S(1)}, u32[]{:S(2)}, u32[]{:S(2)}) collective-permute-start(bf16[512,512]{1,0:T(8,128)(2,1)} %get-tuple-element.18), channel_id=1, source_target_pairs={{0,16},{1,17},{2,18},{3,19},{4,20},{5,21},{6,22},{7,23},{8,24},{9,... | collective-permute-start | bytes 1572872 | tf_op jit(solution)/shard_map/ppermute | solution.py:31
  142.6 9.6 %collective-permute-done.12 = bf16[512,512]{1,0:T(8,128)(2,1)S(1)} collective-permute-done((bf16[512,512]{1,0:T(8,128)(2,1)}, bf16[512,512]{1,0:T(8,128)(2,1)S(1)}, u32[]{:S(2)}, u32[]{:S(2)}) %collective-permute-start.12) | collective-permute-done | bytes 524320 | tf_op jit(solution)/shard_map/ppermute | solution.py:31
  152.2 5.8 %collective-permute-start.8 = (bf16[256,256]{1,0:T(8,128)(2,1)S(1)}, bf16[256,256]{1,0:T(8,128)(2,1)S(1)}, u32[]{:S(2)}, u32[]{:S(2)}) collective-permute-start(bf16[256,256]{1,0:T(8,128)(2,1)S(1)} %fusion.14), channel_id=1, source_target_pairs={{1,64},{3,66},{5,68},{7,70},{9,72},{11,74},{13,76},{15,78},{17,80}... | collective-permute-start | bytes 393224 | tf_op jit(solution)/shard_map/ppermute | solution.py:31
  158.0 7.2 %collective-permute-done.14 = bf16[512,512]{1,0:T(8,128)(2,1)} collective-permute-done((bf16[512,512]{1,0:T(8,128)(2,1)}, bf16[512,512]{1,0:T(8,128)(2,1)}, u32[]{:S(2)}, u32[]{:S(2)}) %collective-permute-start.14) | collective-permute-done | bytes 524320 | tf_op jit(solution)/shard_map/ppermute | solution.py:31
  165.2 2.6 %collective-permute-start.7 = (bf16[256,256]{1,0:T(8,128)(2,1)S(1)}, bf16[256,256]{1,0:T(8,128)(2,1)S(1)}, u32[]{:S(2)}, u32[]{:S(2)}) collective-permute-start(bf16[256,256]{1,0:T(8,128)(2,1)S(1)} %fusion.14), channel_id=1, source_target_pairs={{0,1},{1,65},{2,3},{3,67},{4,5},{5,69},{6,7},{7,71},{8,9},{9,73},{... | collective-permute-start | bytes 393224 | tf_op jit(solution)/shard_map/ppermute | solution.py:31
  167.8 2.3 %fusion.7 = bf16[512,512]{1,0:T(8,128)(2,1)} fusion(bf16[512,512]{1,0:T(8,128)(2,1)} %collective-permute-done.14, bf16[512,512]{1,0:T(8,128)(2,1)} %collective-permute-done.13, bf16[512,512]{1,0:T(8,128)(2,1)S(1)} %collective-permute-done.12, bf16[4,512,512]{2,1,0:T(8,128)(2,1)S(1)} %copy-done.1), kind=kLoop, calls=%fused_computation.32 | loop fusion | flops 2097152 | bytes 2621440 | tf_op jit(solution)/shard_map/convert_element_type | solution.py:315
  173.5 2.2 %reduce_sum.50 = bf16[512,512]{1,0:T(8,128)(2,1)S(1)} reduce(bf16[4,512,512]{2,1,0:T(8,128)(2,1)} %all-to-all-done, bf16[]{:T(256)} %constant.353.clone.1), dimensions={0}, to_apply=%region_2.3 | reduce | flops 786432 | bytes 2621442 | tf_op jit(solution)/shard_map/reduce_sum | solution.py:322
  175.7 4.3 %collective-permute-start.6 = (bf16[512,512]{1,0:T(8,128)(2,1)S(1)}, bf16[512,512]{1,0:T(8,128)(2,1)S(1)}, u32[]{:S(2)}, u32[]{:S(2)}) collective-permute-start(bf16[512,512]{1,0:T(8,128)(2,1)S(1)} %reduce_sum.50), channel_id=1, source_target_pairs={{0,2},{1,66},{2,4},{3,68},{4,6},{5,70},{6,0},{7,64},{8,10},{9,74},... | collective-permute-start | bytes 1572872 | tf_op jit(solution)/shard_map/ppermute | solution.py:31
  179.9 3.4 %add_multiply_fusion = f32[304,4096]{1,0:T(8,128)S(1)} fusion(bf16[304,4096]{1,0:T(8,128)(2,1)} %collective-permute-done.17, bf16[304,4096]{1,0:T(8,128)(2,1)} %collective-permute-done.16, f32[4096]{0:T(1024)S(1)} %copy-done.11), kind=kLoop, calls=%fused_computation.2 | loop fusion | flops 4980736 | bytes 9977856 | tf_op jit(solution)/shard_map/mul | solution.py:325
  185.9 14.0 %collective-permute-done.15 = bf16[512,512]{1,0:T(8,128)(2,1)S(1)} collective-permute-done((bf16[512,512]{1,0:T(8,128)(2,1)}, bf16[512,512]{1,0:T(8,128)(2,1)S(1)}, u32[]{:S(2)}, u32[]{:S(2)}) %collective-permute-start.15) | collective-permute-done | bytes 524320 | tf_op jit(solution)/shard_map/ppermute | solution.py:31
  (112 shorter events, 51.9 us)
Async XLA Ops:
  7.3 30.4 %collective-permute-start.2 = (bf16[256,1024]{1,0:T(8,128)(2,1)}, bf16[256,1024]{1,0:T(8,128)(2,1)}, u32[]{:S(2)}, u32[]{:S(2)}) collective-permute-start(bf16[256,1024]{1,0:T(8,128)(2,1)} %shard_map.147), channel_id=1, source_target_pairs={{0,7},{1,6},{2,1},{3,0},{4,3},{5,2},{6,5},{7,4},{8,15},{9,14},{10,... | collective-permute-start | bytes 1572872 | tf_op jit(solution)/shard_map/ppermute | solution.py:31
  8.8 29.9 %collective-permute-start.1 = (bf16[256,1024]{1,0:T(8,128)(2,1)}, bf16[256,1024]{1,0:T(8,128)(2,1)}, u32[]{:S(2)}, u32[]{:S(2)}) collective-permute-start(bf16[256,1024]{1,0:T(8,128)(2,1)} %shard_map.147), channel_id=1, source_target_pairs={{0,6},{1,7},{2,0},{3,1},{4,2},{5,3},{6,4},{7,5},{8,14},{9,15},{10,... | collective-permute-start | bytes 1572872 | tf_op jit(solution)/shard_map/ppermute | solution.py:31
  12.0 14.7 %collective-permute-start = (f32[512]{0:T(512)S(1)}, f32[512]{0:T(512)S(1)}, u32[]{:S(2)}, u32[]{:S(2)}) collective-permute-start(f32[512]{0:T(512)S(1)} %pad_maximum_fusion.19), channel_id=1, source_target_pairs={{0,1},{1,0},{2,3},{3,2},{4,5},{5,4},{6,7},{7,6},{8,9},{9,8},{10,11... | collective-permute-start | bytes 6152 | tf_op jit(solution)/shard_map/ppermute | solution.py:31
  14.9 16.9 %all-to-all-start.1 = ((bf16[16,16,1024]{2,1,0:T(8,128)(2,1)}), bf16[16,16,1024]{2,1,0:T(8,128)(2,1)}, u32[]{:S(2)}, u32[]{:S(2)}) async-start(bf16[16,16,1024]{2,1,0:T(8,128)(2,1)} %pad_maximum_fusion.17), calls=%async_computation.1 | async-start | bytes 1048576 | tf_op jit(solution)/shard_map/all_to_all | solution.py:220
  33.4 17.2 %all-to-all-start.2 = ((bf16[16,16,1152]{2,1,0:T(8,128)(2,1)}), bf16[16,16,1152]{2,1,0:T(8,128)(2,1)}, u32[]{:S(2)}, u32[]{:S(2)}) async-start(bf16[16,16,1152]{2,1,0:T(8,128)(2,1)} %broadcast_in_dim.93), calls=%async_computation.2 | async-start | bytes 1179648 | tf_op jit(solution)/shard_map/all_to_all | solution.py:243
  41.8 35.4 %collective-permute-start.4 = (bf16[256,2048]{1,0:T(8,128)(2,1)}, bf16[256,2048]{1,0:T(8,128)(2,1)S(1)}, u32[]{:S(2)}, u32[]{:S(2)}) collective-permute-start(bf16[256,2048]{1,0:T(8,128)(2,1)} %get-tuple-element.38), channel_id=1, source_target_pairs={{0,8},{1,9},{2,10},{3,11},{4,12},{5,13},{6,14},{7,15},{8,16},{9,17... | collective-permute-start | bytes 3145736 | tf_op jit(solution)/shard_map/ppermute | solution.py:31
  43.0 36.9 %collective-permute-start.5 = (bf16[256,2048]{1,0:T(8,128)(2,1)}, bf16[256,2048]{1,0:T(8,128)(2,1)}, u32[]{:S(2)}, u32[]{:S(2)}) collective-permute-start(bf16[256,2048]{1,0:T(8,128)(2,1)} %get-tuple-element.39), channel_id=1, source_target_pairs={{0,24},{1,25},{2,26},{3,27},{4,28},{5,29},{6,30},{7,31},{8,0},{9,1... | collective-permute-start | bytes 3145736 | tf_op jit(solution)/shard_map/ppermute | solution.py:31
  44.5 70.6 %collective-permute-start.3 = (bf16[256,2048]{1,0:T(8,128)(2,1)}, bf16[256,2048]{1,0:T(8,128)(2,1)}, u32[]{:S(2)}, u32[]{:S(2)}) collective-permute-start(bf16[256,2048]{1,0:T(8,128)(2,1)} %get-tuple-element.40), channel_id=1, source_target_pairs={{0,16},{1,17},{2,18},{3,19},{4,20},{5,21},{6,22},{7,23},{8,24},{9,... | collective-permute-start | bytes 3145736 | tf_op jit(solution)/shard_map/ppermute | solution.py:31
  48.0 75.9 %collective-permute-start.10 = (bf16[256,2048]{1,0:T(8,128)(2,1)}, bf16[256,2048]{1,0:T(8,128)(2,1)}, u32[]{:S(2)}, u32[]{:S(2)}) collective-permute-start(bf16[256,2048]{1,0:T(8,128)(2,1)} %get-tuple-element.34), channel_id=1, source_target_pairs={{0,32},{1,33},{2,34},{3,35},{4,36},{5,37},{6,38},{7,39},{8,40},{9,... | collective-permute-start | bytes 3145736 | tf_op jit(solution)/shard_map/ppermute | solution.py:31
  49.2 74.6 %collective-permute-start.11 = (bf16[256,2048]{1,0:T(8,128)(2,1)}, bf16[256,2048]{1,0:T(8,128)(2,1)}, u32[]{:S(2)}, u32[]{:S(2)}) collective-permute-start(bf16[256,2048]{1,0:T(8,128)(2,1)} %get-tuple-element.35), channel_id=1, source_target_pairs={{0,96},{1,97},{2,98},{3,99},{4,100},{5,101},{6,102},{7,103},{8,104... | collective-permute-start | bytes 3145736 | tf_op jit(solution)/shard_map/ppermute | solution.py:31
  53.4 77.6 %all-to-all-start.3 = ((bf16[16,256,256]{2,1,0:T(8,128)(2,1)}), bf16[16,256,256]{2,1,0:T(8,128)(2,1)}, u32[]{:S(2)}, u32[]{:S(2)}) async-start(bf16[16,256,256]{2,1,0:T(8,128)(2,1)} %bitcast.86), calls=%async_computation.3 | async-start | bytes 4194304 | tf_op jit(solution)/shard_map/all_to_all | solution.py:279
  64.5 52.5 %copy-start.13 = (s32[1,4]{1,0:T(1,128)S(1)}, s32[1,4]{1,0:T(1,128)}, u32[]{:S(2)}) copy-start(s32[1,4]{1,0:T(1,128)} %constant.331.clone.1) | copy-start | bytes 52
  77.2 46.7 %collective-permute-start.9 = (bf16[256,2048]{1,0:T(8,128)(2,1)}, bf16[256,2048]{1,0:T(8,128)(2,1)}, u32[]{:S(2)}, u32[]{:S(2)}) collective-permute-start(bf16[256,2048]{1,0:T(8,128)(2,1)} %get-tuple-element.13), channel_id=1, source_target_pairs={{0,64},{1,65},{2,66},{3,67},{4,68},{5,69},{6,70},{7,71},{8,72},{9,... | collective-permute-start | bytes 3145736 | tf_op jit(solution)/shard_map/ppermute | solution.py:31
  79.9 100.0 %collective-permute-start.17 = (bf16[304,4096]{1,0:T(8,128)(2,1)}, bf16[304,4096]{1,0:T(8,128)(2,1)}, u32[]{:S(2)}, u32[]{:S(2)}) collective-permute-start(bf16[304,4096]{1,0:T(8,128)(2,1)} %get-tuple-element.11), channel_id=1, source_target_pairs={{0,7},{1,6},{2,1},{3,0},{4,3},{5,2},{6,5},{7,4},{8,15},{9,14},{10,... | collective-permute-start | bytes 7471112 | tf_op jit(solution)/shard_map/ppermute | solution.py:31
  115.0 64.9 %collective-permute-start.16 = (bf16[304,4096]{1,0:T(8,128)(2,1)}, bf16[304,4096]{1,0:T(8,128)(2,1)}, u32[]{:S(2)}, u32[]{:S(2)}) collective-permute-start(bf16[304,4096]{1,0:T(8,128)(2,1)} %get-tuple-element.12), channel_id=1, source_target_pairs={{0,6},{1,7},{2,0},{3,1},{4,2},{5,3},{6,4},{7,5},{8,14},{9,15},{10,... | collective-permute-start | bytes 7471112 | tf_op jit(solution)/shard_map/ppermute | solution.py:31
  131.0 42.4 %all-to-all-start = ((bf16[4,512,512]{2,1,0:T(8,128)(2,1)}), bf16[4,512,512]{2,1,0:T(8,128)(2,1)}, u32[]{:S(2)}, u32[]{:S(2)}) async-start(bf16[4,512,512]{2,1,0:T(8,128)(2,1)} %copy-done.2), calls=%async_computation | async-start | bytes 4194304 | tf_op jit(solution)/shard_map/all_to_all | solution.py:321
  136.8 36.2 %copy-start.4 = (bf16[256,1024]{1,0:T(8,128)(2,1)S(1)}, bf16[256,1024]{1,0:T(8,128)(2,1)}, u32[]{:S(2)}) copy-start(bf16[256,1024]{1,0:T(8,128)(2,1)} %shard_map.150) | copy-start | bytes 1572868
  136.8 15.4 %collective-permute-start.12 = (bf16[512,512]{1,0:T(8,128)(2,1)}, bf16[512,512]{1,0:T(8,128)(2,1)S(1)}, u32[]{:S(2)}, u32[]{:S(2)}) collective-permute-start(bf16[512,512]{1,0:T(8,128)(2,1)} %get-tuple-element.18), channel_id=1, source_target_pairs={{0,16},{1,17},{2,18},{3,19},{4,20},{5,21},{6,22},{7,23},{8,24},{9,... | collective-permute-start | bytes 1572872 | tf_op jit(solution)/shard_map/ppermute | solution.py:31
  139.8 25.4 %collective-permute-start.14 = (bf16[512,512]{1,0:T(8,128)(2,1)}, bf16[512,512]{1,0:T(8,128)(2,1)}, u32[]{:S(2)}, u32[]{:S(2)}) collective-permute-start(bf16[512,512]{1,0:T(8,128)(2,1)} %get-tuple-element.19), channel_id=1, source_target_pairs={{0,24},{1,25},{2,26},{3,27},{4,28},{5,29},{6,30},{7,31},{8,0},{9,1... | collective-permute-start | bytes 1572872 | tf_op jit(solution)/shard_map/ppermute | solution.py:31
  140.9 26.9 %collective-permute-start.13 = (bf16[512,512]{1,0:T(8,128)(2,1)}, bf16[512,512]{1,0:T(8,128)(2,1)}, u32[]{:S(2)}, u32[]{:S(2)}) collective-permute-start(bf16[512,512]{1,0:T(8,128)(2,1)} %get-tuple-element.20), channel_id=1, source_target_pairs={{0,8},{1,9},{2,10},{3,11},{4,12},{5,13},{6,14},{7,15},{8,16},{9,17... | collective-permute-start | bytes 1572872 | tf_op jit(solution)/shard_map/ppermute | solution.py:31
  152.2 19.8 %collective-permute-start.8 = (bf16[256,256]{1,0:T(8,128)(2,1)S(1)}, bf16[256,256]{1,0:T(8,128)(2,1)S(1)}, u32[]{:S(2)}, u32[]{:S(2)}) collective-permute-start(bf16[256,256]{1,0:T(8,128)(2,1)S(1)} %fusion.14), channel_id=1, source_target_pairs={{1,64},{3,66},{5,68},{7,70},{9,72},{11,74},{13,76},{15,78},{17,80}... | collective-permute-start | bytes 393224 | tf_op jit(solution)/shard_map/ppermute | solution.py:31
  165.2 6.8 %collective-permute-start.7 = (bf16[256,256]{1,0:T(8,128)(2,1)S(1)}, bf16[256,256]{1,0:T(8,128)(2,1)S(1)}, u32[]{:S(2)}, u32[]{:S(2)}) collective-permute-start(bf16[256,256]{1,0:T(8,128)(2,1)S(1)} %fusion.14), channel_id=1, source_target_pairs={{0,1},{1,65},{2,3},{3,67},{4,5},{5,69},{6,7},{7,71},{8,9},{9,73},{... | collective-permute-start | bytes 393224 | tf_op jit(solution)/shard_map/ppermute | solution.py:31
  170.1 29.8 %collective-permute-start.15 = (bf16[512,512]{1,0:T(8,128)(2,1)}, bf16[512,512]{1,0:T(8,128)(2,1)S(1)}, u32[]{:S(2)}, u32[]{:S(2)}) collective-permute-start(bf16[512,512]{1,0:T(8,128)(2,1)} %fusion.7), channel_id=1, source_target_pairs={{0,2},{1,67},{2,4},{3,69},{4,6},{5,71},{6,0},{7,65},{8,10},{9,75},... | collective-permute-start | bytes 1572872 | tf_op jit(solution)/shard_map/ppermute | solution.py:31
  175.7 24.5 %collective-permute-start.6 = (bf16[512,512]{1,0:T(8,128)(2,1)S(1)}, bf16[512,512]{1,0:T(8,128)(2,1)S(1)}, u32[]{:S(2)}, u32[]{:S(2)}) collective-permute-start(bf16[512,512]{1,0:T(8,128)(2,1)S(1)} %reduce_sum.50), channel_id=1, source_target_pairs={{0,2},{1,66},{2,4},{3,68},{4,6},{5,70},{6,0},{7,64},{8,10},{9,74},... | collective-permute-start | bytes 1572872 | tf_op jit(solution)/shard_map/ppermute | solution.py:31
  (12 other events, 62.1 us)
